TPU v7x, 128 devices: a whole 4x4x4 slice. The times are simulated.
128 devices in a mesh: row: 16 (over x, z_lo, core), col: 8 (over z_hi, y).
Axes of the slice: x: 4, y: 4, z: 4 (z_hi: 2, z_lo: 2; z = z_hi * 2 + z_lo), core: 2. Of those that a mesh axis runs over, the one named last changes fastest.
Arguments:
- solution: float32 [524288, 64], P(('col', 'row')), may hold values from -6 to 6
- residual: float32 [98304, 64], P(('row', 'col')), may hold values from -6 to 6
- direction: float32 [524288, 64], P(('col', 'row')), may hold values from -6 to 6
- gradient: float32 [524288, 64], P(('col', 'row'))
- blocks: float32 [16, 2048, 128, 128], P('row', 'col'), may hold values from -0.078125 to 0.078125
- block_rows: int32 [16, 2048], P('row', 'col'), may hold values from 0 to 47
- block_cols: int32 [16, 2048], P('row', 'col'), may hold values from 0 to 511
- counts: int32 [16, 8], P('row', 'col'), may hold values from 64 to 256, as said below
Outputs:
- new_solution: float32 [524288, 64], P(('col', 'row'))
- new_residual: float32 [98304, 64], P(('row', 'col'))
- new_direction: float32 [524288, 64], P(('col', 'row'))
Inputs may be any that keep to these rules, and one draw needn't show every extreme that they name: Some tile has all 256 slots live in every draw; the counts differ from tile to tile.
All inputs are finite; a program needn't handle non-finite values.
Results may differ from a plain program's by a relative error of at most 0.0001.
Values sent between devices are 32-bit elements; how exact they have to be, the bound alone decides.
No kernel may reach another device: no remote copies, remote signals or barrier semaphores. Data moves between devices by JAX's collectives and lax.ppermute only.
A program may use at most 192 MiB of HBM per device.

v0:
```python
import jax
import jax.numpy as jnp
from jax import lax
from jax.sharding import PartitionSpec as P

EPS = 1e-06


def block_product(tile_blocks, source_blocks, transposed):
    if transposed:
        return jnp.einsum(
            "bji,bjk->bik", tile_blocks, source_blocks, precision=lax.Precision.HIGHEST
        )
    return jnp.einsum("bij,bjk->bik", tile_blocks, source_blocks, precision=lax.Precision.HIGHEST)


def tile_apply(
    tile_blocks, gather_index, target_index, live_count, source, target_count, transposed
):
    slot_total = tile_blocks.shape[0]
    slot_live = (jnp.arange(slot_total, dtype=jnp.int32) < live_count).astype(jnp.float32)
    picked = jnp.take(source, gather_index, axis=0)
    product = block_product(tile_blocks, picked, transposed) * slot_live[:, None, None]
    return jax.ops.segment_sum(product, target_index, num_segments=target_count)


def per_device(solution, residual, direction, gradient, blocks, block_rows, block_cols, counts):
    tile_blocks = blocks[0]
    block_size = tile_blocks.shape[-1]
    width = direction.shape[1]
    row_index = block_rows[0]
    col_index = block_cols[0]
    live_count = counts[0, 0]
    col_count = lax.axis_size("col")
    gamma = lax.psum(jnp.sum(gradient * gradient, axis=0), ("row", "col"))
    panel = lax.all_gather(direction, "row", axis=0, tiled=True)
    cb_tile = panel.shape[0] // block_size
    ray_rows = residual.shape[0]
    br_tile = ray_rows * col_count // block_size
    image_part = tile_apply(
        tile_blocks,
        col_index,
        row_index,
        live_count,
        panel.reshape(cb_tile, block_size, width),
        br_tile,
        False,
    )
    image_part = image_part.reshape(br_tile * block_size, width)
    image_local = lax.psum_scatter(image_part, "col", scatter_dimension=0, tiled=True)
    image_norms = lax.psum(jnp.sum(image_local * image_local, axis=0), ("row", "col"))
    alpha = gamma / (image_norms + EPS)
    new_residual = residual - alpha[None, :] * image_local
    ray_tile = lax.all_gather(new_residual, "col", axis=0, tiled=True)
    new_solution = solution + alpha[None, :] * direction
    cell_part = tile_apply(
        tile_blocks,
        row_index,
        col_index,
        live_count,
        ray_tile.reshape(br_tile, block_size, width),
        cb_tile,
        True,
    )
    cell_part = cell_part.reshape(cb_tile * block_size, width)
    new_gradient = lax.psum_scatter(cell_part, "row", scatter_dimension=0, tiled=True)
    new_norms = lax.psum(jnp.sum(new_gradient * new_gradient, axis=0), ("row", "col"))
    beta = new_norms / gamma
    new_direction = new_gradient + beta[None, :] * direction
    return (new_solution, new_residual, new_direction)


def solution(mesh):
    placed = (
        P(("col", "row"), None),
        P(("row", "col"), None),
        P(("col", "row"), None),
        P(("col", "row"), None),
        P("row", "col", None, None),
        P("row", "col"),
        P("row", "col"),
        P("row", "col"),
    )
    return jax.shard_map(
        per_device,
        mesh=mesh,
        in_specs=placed,
        out_specs=(P(("col", "row"), None), P(("row", "col"), None), P(("col", "row"), None)),
        check_vma=False,
    )
```

profile of v0, /device:TPU:1, one launch (start us, length us, event | category | flops | bytes accessed | tf_op | source)
XLA Modules:
  0.0 719.8 jit_solution(16760542525794823402)
XLA Ops:
  7.2 0.0 all-gather.3.cloned.1.call-start
  7.2 0.7 all-gather.3.cloned.1.call-update
  7.9 0.0 reduce-scatter.3.cloned.1.call-start
  8.6 0.7 compare_select_fusion.1
  9.3 0.7 compare_convert_fusion
  10.0 95.0 %all-gather.3.cloned.1.call-done = f32[65536,64]{0,1:T(8,128)} async-done(((f32[4096,64]{0,1:T(8,128)}), f32[65536,64]{0,1:T(8,128)}) %all-gather.3.cloned.1.call-update) | async-done | bytes 16777232 | tf_op jit(solution)/shard_map/all_gather | solution.py:36
  105.0 11.8 %copy_bitcast_fusion.1 = f32[512,128,64]{1,2,0:T(8,128)} fusion(f32[65536,64]{0,1:T(8,128)} %all-gather.3.cloned.1.call-done), kind=kLoop, calls=%fused_computation.5 | loop fusion | bytes 33554432 | tf_op jit(solution)/shard_map/reshape | solution.py:45
  116.7 10.1 %gather_fusion = f32[256,128,64]{1,2,0:T(8,128)} fusion(f32[512,128,64]{1,2,0:T(8,128)} %copy_bitcast_fusion.1, s32[1024]{0:T(1024)S(1)} %pad_clamp_fusion.1), kind=kCustom, calls=%fused_computation | custom fusion | bytes 16778240 | tf_op jit(solution)/shard_map/jit(_take)/gather | solution.py:22
  126.8 36.1 %multiply_bitcast_fusion.1 = f32[256,128,64]{1,2,0:T(8,128)} fusion(f32[256]{0:T(256)S(1)} %get-tuple-element.7, f32[1,256,128,128]{3,2,1,0:T(8,128)} %param.12, f32[256,128,64]{1,2,0:T(8,128)} %gather_fusion, pred[256]{0:T(512)(128)(4,1)S(1)} %get-tuple-element.8), kind=kOutput, calls=%fused_computation.12 | convolution fusion | flops 3225419776 | bytes 33555712 | tf_op jit(solution)/shard_map/bij,bjk->bik/dot_general | solution.py:14
  162.9 0.2 broadcast_in_dim.29
  163.1 26.1 %scatter_fusion = f32[48,128,64]{1,2,0:T(8,128)S(1)} fusion(f32[48,128,64]{1,2,0:T(8,128)S(1)} %broadcast_in_dim.29, s32[256]{0:T(256)S(1)} %bitcast.45, f32[256,128,64]{1,2,0:T(8,128)} %multiply_bitcast_fusion.1), kind=kCustom, calls=%fused_computation.2 | custom fusion | flops 2097152 | bytes 25166848 | tf_op jit(solution)/shard_map/scatter-add | solution.py:24
  189.2 1.3 copy_bitcast_fusion.2
  190.5 0.0 reduce-scatter.3.cloned.1.call-update
  190.5 0.0 all-gather.5.cloned.1.call-start
  190.6 0.2 multiply_reduce_fusion.1
  190.8 73.6 %reduce-scatter.3.cloned.1.call-done = f32[768,64]{0,1:T(8,128)} async-done(((f32[6144,64]{0,1:T(8,128)}), f32[768,64]{0,1:T(8,128)}) %reduce-scatter.3.cloned.1.call-update) | async-done | bytes 196624 | tf_op jit(solution)/shard_map/reduce_scatter | solution.py:50
  264.3 1.0 multiply_reduce_fusion.2
  265.4 65.4 %all-reduce = (f32[64]{0:T(128)S(1)}, f32[64]{0:T(128)S(1)}) all-reduce(f32[64]{0:T(128)S(1)} %multiply_reduce_fusion.1, f32[64]{0:T(128)S(1)} %multiply_reduce_fusion.2), channel_id=1, replica_groups=mesh['row'=16,'col'=8] {'row','col'}, use_global_device_ids=true, to_apply=%region_1.0 | all-reduce | flops 128 | bytes 1024 | tf_op jit(solution)/shard_map/psum | solution.py:35
  330.8 1.7 multiply_subtract_fusion
  332.5 0.0 all-gather.5.cloned.1.call-update
  332.5 0.2 reduce-scatter.5.cloned.1.call-start
  332.8 46.0 %all-gather.5.cloned.1.call-done = f32[6144,64]{0,1:T(8,128)} async-done(((f32[768,64]{0,1:T(8,128)}), f32[6144,64]{0,1:T(8,128)}) %all-gather.5.cloned.1.call-update) | async-done | bytes 1572880 | tf_op jit(solution)/shard_map/all_gather | solution.py:54
  378.8 1.6 copy_bitcast_fusion.3
  380.4 4.4 gather_fusion.1
  384.7 19.9 %multiply_bitcast_fusion = f32[256,128,64]{1,2,0:T(8,128)} fusion(f32[256]{0:T(256)S(1)} %get-tuple-element.7, f32[1,256,128,128]{3,2,1,0:T(8,128)} %param.12, f32[256,128,64]{1,2,0:T(8,128)} %gather_fusion.1, pred[256]{0:T(512)(128)(4,1)S(1)} %compare_and_fusion), kind=kOutput, calls=%fused_computation.10 | convolution fusion | flops 3225419776 | bytes 33555712 | tf_op jit(solution)/shard_map/bji,bjk->bik/dot_general | solution.py:11
  404.7 7.9 %broadcast_in_dim.32 = f32[512,128,64]{1,2,0:T(8,128)} broadcast(f32[]{:T(128)} %constant.18.clone.1), dimensions={} | broadcast | bytes 16777220 | tf_op jit(solution)/shard_map/broadcast_in_dim | solution.py:24
  412.5 39.4 %scatter_fusion.1 = f32[512,128,64]{1,2,0:T(8,128)} fusion(f32[512,128,64]{1,2,0:T(8,128)} %broadcast_in_dim.32, s32[256]{0:T(256)S(1)} %bitcast.44, f32[256,128,64]{1,2,0:T(8,128)} %multiply_bitcast_fusion), kind=kCustom, calls=%fused_computation.3 | custom fusion | flops 2097152 | bytes 25166848 | tf_op jit(solution)/shard_map/scatter-add | solution.py:24
  451.9 11.4 %copy_bitcast_fusion = f32[65536,64]{0,1:T(8,128)} fusion(f32[512,128,64]{1,2,0:T(8,128)} %scatter_fusion.1), kind=kLoop, calls=%fused_computation.4 | loop fusion | bytes 33554432 | tf_op jit(solution)/shard_map/reshape | solution.py:65
  463.3 181.1 %reduce-scatter.5.cloned.1.call-done = f32[4096,64]{0,1:T(8,128)} async-done(((f32[65536,64]{0,1:T(8,128)}), f32[4096,64]{0,1:T(8,128)}) %reduce-scatter.5.cloned.1.call-update) | async-done | bytes 1048592 | tf_op jit(solution)/shard_map/reduce_scatter | solution.py:66
  644.5 1.4 multiply_reduce_fusion
  645.9 64.6 %psum.23 = f32[64]{0:T(128)S(1)} all-reduce(f32[64]{0:T(128)S(1)} %multiply_reduce_fusion), channel_id=1, replica_groups=mesh['row'=16,'col'=8] {'row','col'}, use_global_device_ids=true, to_apply=%region_9.10 | all-reduce | flops 64 | bytes 512 | tf_op jit(solution)/shard_map/psum | solution.py:67
  710.5 2.8 multiply_add_fusion
  (19 shorter events, 0.1 us)
Async XLA Ops:
  7.2 97.8 %all-gather.3.cloned.1.call-start = ((), (), s32[]{:S(2)}) async-start(), calls=%async_computation.2 | async-start | bytes 17825792 | tf_op jit(solution)/shard_map/all_gather | solution.py:36
  7.9 256.4 %reduce-scatter.3.cloned.1.call-start = ((), (), s32[]{:S(2)}) async-start(), calls=%async_computation.3 | async-start | bytes 1769472 | tf_op jit(solution)/shard_map/reduce_scatter | solution.py:50
  126.8 36.3 %copy-start.5 = (s32[1,256]{1,0:T(1,128)S(1)}, s32[1,256]{1,0:T(1,128)}, u32[]{:S(2)}) copy-start(s32[1,256]{1,0:T(1,128)} %param.13) | copy-start | bytes 3076
  163.1 27.5 %copy-start.1 = (f32[4096,64]{0,1:T(8,128)S(1)}, f32[4096,64]{0,1:T(8,128)}, u32[]{:S(2)}) copy-start(f32[4096,64]{0,1:T(8,128)} %param.11) | copy-start | bytes 3145732
  163.1 167.7 %copy-start.3 = (f32[768,64]{0,1:T(8,128)S(1)}, f32[768,64]{0,1:T(8,128)}, u32[]{:S(2)}) copy-start(f32[768,64]{0,1:T(8,128)} %param.9) | copy-start | bytes 589828
  190.5 188.3 %all-gather.5.cloned.1.call-start = ((), (), s32[]{:S(2)}) async-start(), calls=%async_computation.4 | async-start | bytes 1769472 | tf_op jit(solution)/shard_map/all_gather | solution.py:54
  332.5 312.0 %reduce-scatter.5.cloned.1.call-start = ((), (), s32[]{:S(2)}) async-start(), calls=%async_computation.5 | async-start | bytes 17825792 | tf_op jit(solution)/shard_map/reduce_scatter | solution.py:66
  404.7 7.9 %copy-start.4 = (s32[1,256]{1,0:T(1,128)S(1)}, s32[1,256]{1,0:T(1,128)}, u32[]{:S(2)}) copy-start(s32[1,256]{1,0:T(1,128)} %param.14) | copy-start | bytes 3076
  463.3 247.2 %copy-start = (f32[4096,64]{0,1:T(8,128)S(1)}, f32[4096,64]{0,1:T(8,128)}, u32[]{:S(2)}) copy-start(f32[4096,64]{0,1:T(8,128)} %param.10) | copy-start | bytes 3145732
  463.3 247.2 %copy-start.2 = (f32[4096,64]{0,1:T(8,128)S(1)}, f32[4096,64]{0,1:T(8,128)}, u32[]{:S(2)}) copy-start(f32[4096,64]{0,1:T(8,128)} %param.8) | copy-start | bytes 3145732
Sparse Core Ops, SparseCore 0:
  9.7 95.2 all-gather.2
  190.6 73.6 reduce-scatter.2
  332.6 46.0 all-gather.4
  463.5 180.9 reduce-scatter.4
where the time goes:
time: 721 us; the launch traced here: 720 us
  waiting for transfers between devices  396 us (55%)
  blocking collectives  130 us (18%)
  other arithmetic  74.1 us (10%)
  matrix products  56 us (8%)
  local copies, waits for them, and re-layouts  48.5 us (7%)
  between operations  14.5 us (2%)
    reduce_scatter x1, waiting for transfers between devices, per_device(): lax.psum_scatter(cell_part, 'row', scatter_dimension=0, tiled=True)  181 us
    all_gather x1, waiting for transfers between devices, per_device(): panel = lax.all_gather(direction, 'row', axis=0, tiled=True)  95 us
    reduce_scatter x1, waiting for transfers between devices, per_device(): lax.psum_scatter(image_part, 'col', scatter_dimension=0, tiled=True)  73.6 us
    scatter-add x2, other arithmetic, tile_apply(): return jax.ops.segment_sum(product, target_index, num_segments=target_count)  65.6 us
    psum x1, blocking collectives, per_device(): gamma = lax.psum(jnp.sum(gradient * gradient, axis=0), ('row', 'col'))  65.4 us
    psum x1, blocking collectives, per_device(): lax.psum(jnp.sum(new_gradient * new_gradient, axis=0), ('row', 'col'))  64.6 us
    all_gather x1, waiting for transfers between devices, per_device(): ray_tile = lax.all_gather(new_residual, 'col', axis=0, tiled=True)  46 us
    dot_general x1, matrix products, block_product(): jnp.einsum('bij,bjk->bik', tile_blocks, source_blocks, precision=lax.Prec...  36.1 us
  transfers between devices with their start and end apart: 4, of which 4 were waited for; matrix products, arithmetic and copies ran while one was open for 0% of the time, Pallas kernels for 0%

commit v1 on v0

v1 whole, which is shorter than its diff:
```python
import functools

import jax
import jax.numpy as jnp
from jax import lax
from jax.experimental import pallas as pl
from jax.experimental.pallas import tpu as pltpu
from jax.sharding import PartitionSpec as P

EPS = 1e-06
BS = 128
GROUP = 8
VMEM_BYTES = 56 * 1024 * 1024

NX, NZ, NCORE = 4, 2, 2
NZH, NY = 2, 4


def row_of(x, z, c):
    return (x % NX) * 4 + (z % NZ) * 2 + c % NCORE


def col_of(z, y):
    return (z % NZH) * 4 + y % NY


def row_shift(value, dx, dz, dc):
    pairs = [
        (row_of(x + dx, z + dz, c + dc), row_of(x, z, c))
        for x in range(NX)
        for z in range(NZ)
        for c in range(NCORE)
    ]
    return lax.ppermute(value, "row", pairs)


def col_shift(value, dz, dy):
    pairs = [(col_of(z + dz, y + dy), col_of(z, y)) for z in range(NZH) for y in range(NY)]
    return lax.ppermute(value, "col", pairs)


def sum_everywhere(row):
    count = NX * NZ * NCORE * NZH * NY
    sent = jnp.broadcast_to(row[None], (count, 1, row.shape[1]))
    got = lax.all_to_all(sent, ("row", "col"), 0, 0, tiled=True)
    return jnp.sum(got, axis=0)


def split(value):
    high = value.astype(jnp.bfloat16)
    low = (value - high.astype(jnp.float32)).astype(jnp.bfloat16)
    return high, low


def doubled(value):
    high, low = split(value)
    return jnp.concatenate(
        [jnp.concatenate([high, high], axis=1), jnp.concatenate([low, low], axis=1)], axis=0
    )


def forward_kernel(
    kc, places, rows_ref, cols_ref, meta_ref, blocks_ref, *refs
):
    pieces = refs[: len(places)]
    outs = refs[len(places) : len(places) + NY]
    panel, acc, sems = refs[len(places) + NY :]
    step = pl.program_id(0)
    count = meta_ref[0]
    x, z, c = meta_ref[1], meta_ref[2], meta_ref[3]
    half = kc // 2

    @pl.when(step == 0)
    def _():
        copies = []
        for number, (dx, dz, dc, stacked, part) in enumerate(places):
            for rel in range(NZ if stacked else 1):
                owner = ((x + dx) % NX) * 4 + ((z + dz + rel) % NZ) * 2 + (c + dc) % NCORE
                source = pieces[number].at[rel] if stacked else pieces[number]
                copies.append(
                    pltpu.make_async_copy(
                        source,
                        panel.at[owner, pl.ds(part * half, half), :],
                        sems.at[len(copies)],
                    )
                )
        for copy in copies:
            copy.start()
        acc[...] = jnp.zeros_like(acc)
        for copy in copies:
            copy.wait()

    base = step * GROUP

    def product(slot):
        cell = cols_ref[base + slot]
        offset = pl.multiple_of((cell % 32) * BS, BS)
        left = doubled(panel[cell // 32, :, pl.ds(offset, BS)])
        high, low = split(blocks_ref[slot])
        right = jnp.concatenate([high, low], axis=1)
        both = lax.dot_general(
            left, right, (((1,), (1,)), ((), ())), preferred_element_type=jnp.float32
        )
        live = jnp.where(base + slot < count, 1.0, 0.0)
        return (both[:kc] + both[kc:]) * live

    @pl.when(base < count)
    def _():
        terms = [product(slot) for slot in range(GROUP)]
        for slot in range(GROUP):
            acc[rows_ref[base + slot]] += terms[slot]

    @pl.when(step == pl.num_programs(0) - 1)
    def _():
        zh, y = meta_ref[4], meta_ref[5]
        per = acc.shape[0] // (NZH * NY)
        for dy in range(NY):
            for dz in range(NZH):
                piece = ((zh + dz) % NZH) * 4 + (y + dy) % NY
                for t in range(per):
                    outs[dy][dz, :, t * BS : (t + 1) * BS] = acc[piece * per + t]


def backward_kernel(
    kc, layout, rows_ref, cols_ref, meta_ref, blocks_ref, alpha_ref, *refs
):
    res = refs[:NY]
    img = refs[NY : 2 * NY]
    outs = refs[2 * NY : 2 * NY + len(layout)]
    source, acc, sems = refs[2 * NY + len(layout) :]
    step = pl.program_id(0)
    count = meta_ref[0]
    x, z, c = meta_ref[1], meta_ref[2], meta_ref[3]
    half = kc // 2

    @pl.when(step == 0)
    def _():
        zh, y = meta_ref[4], meta_ref[5]
        per = source.shape[0] // (NZH * NY)
        alpha = alpha_ref[...]
        for dy in range(NY):
            for dz in range(NZH):
                piece = ((zh + dz) % NZH) * 4 + (y + dy) % NY
                for t in range(per):
                    span = slice(t * BS, (t + 1) * BS)
                    value = res[dy][dz, :, span] - alpha * img[dy][dz, :, span]
                    source[piece * per + t] = doubled(value)

        def clear(i, _):
            acc[i] = jnp.zeros(acc.shape[1:], jnp.float32)
            return 0

        lax.fori_loop(0, acc.shape[0], clear, 0)

    base = step * GROUP

    def product(slot):
        left = source[rows_ref[base + slot]]
        high, low = split(blocks_ref[slot])
        right = jnp.concatenate([high, low], axis=0)
        both = lax.dot_general(
            left, right, (((1,), (0,)), ((), ())), preferred_element_type=jnp.float32
        )
        live = jnp.where(base + slot < count, 1.0, 0.0)
        return (both[:kc] + both[kc:]) * live

    @pl.when(base < count)
    def _():
        terms = [product(slot) for slot in range(GROUP)]
        for slot in range(GROUP):
            cell = cols_ref[base + slot]
            offset = pl.multiple_of((cell % 32) * BS, BS)
            acc[cell // 32, :, pl.ds(offset, BS)] += terms[slot]

    @pl.when(step == pl.num_programs(0) - 1)
    def _():
        copies = []
        for number, (part, dc, owners) in enumerate(layout):
            for rel, (dx, dz) in enumerate(owners):
                owner = ((x + dx) % NX) * 4 + ((z + dz) % NZ) * 2 + (c + dc) % NCORE
                target = outs[number].at[rel] if len(owners) > 1 else outs[number]
                copies.append(
                    pltpu.make_async_copy(
                        acc.at[owner, pl.ds(part * half, half), :],
                        target,
                        sems.at[len(copies)],
                    )
                )
        for copy in copies:
            copy.start()
        for copy in copies:
            copy.wait()


def block_map(step, rows_ref, cols_ref, meta_ref):
    last = jnp.maximum(meta_ref[0] - 1, 0) // GROUP
    return (jnp.minimum(step, last), 0, 0)


def fixed_map(rank):
    def index(step, rows_ref, cols_ref, meta_ref):
        return (0,) * rank

    return index


def cost(kc, slots):
    return pl.CostEstimate(
        flops=6 * slots * BS * BS * kc,
        bytes_accessed=4 * (slots * BS * BS + 2 * 16 * kc * 4096),
        transcendentals=0,
    )


def forward(blocks, rows, cols, meta, places, pieces, kc):
    slots = blocks.shape[0]
    any_spec = pl.BlockSpec(memory_space=pl.ANY)
    shape = (NZH, kc, 6 * BS)
    copies = sum(NZ if place[3] else 1 for place in places)
    return pl.pallas_call(
        functools.partial(forward_kernel, kc, places),
        grid_spec=pltpu.PrefetchScalarGridSpec(
            num_scalar_prefetch=3,
            grid=(slots // GROUP,),
            in_specs=[pl.BlockSpec((GROUP, BS, BS), block_map)] + [any_spec] * len(pieces),
            out_specs=[pl.BlockSpec(shape, fixed_map(3))] * NY,
            scratch_shapes=[
                pltpu.VMEM((16, kc, 4096), jnp.float32),
                pltpu.VMEM((48, kc, BS), jnp.float32),
                pltpu.SemaphoreType.DMA((copies,)),
            ],
        ),
        out_shape=[jax.ShapeDtypeStruct(shape, jnp.float32)] * NY,
        compiler_params=pltpu.CompilerParams(vmem_limit_bytes=VMEM_BYTES),
        cost_estimate=cost(kc, slots),
    )(rows, cols, meta, blocks, *pieces)


def backward(blocks, rows, cols, meta, alpha, res, img, layout, kc):
    slots = blocks.shape[0]
    any_spec = pl.BlockSpec(memory_space=pl.ANY)
    half = kc // 2
    tile = pl.BlockSpec(res[0].shape, fixed_map(3))
    shapes = [
        (half, 4096) if len(owners) == 1 else (len(owners), half, 4096)
        for _, _, owners in layout
    ]
    return pl.pallas_call(
        functools.partial(backward_kernel, kc, layout),
        grid_spec=pltpu.PrefetchScalarGridSpec(
            num_scalar_prefetch=3,
            grid=(slots // GROUP,),
            in_specs=[pl.BlockSpec((GROUP, BS, BS), block_map)]
            + [pl.BlockSpec((kc, 1), fixed_map(2))]
            + [tile] * (2 * NY),
            out_specs=[any_spec] * len(layout),
            scratch_shapes=[
                pltpu.VMEM((48, 2 * kc, 2 * BS), jnp.bfloat16),
                pltpu.VMEM((16, kc, 4096), jnp.float32),
                pltpu.SemaphoreType.DMA((sum(len(o) for _, _, o in layout),)),
            ],
        ),
        out_shape=[jax.ShapeDtypeStruct(shape, jnp.float32) for shape in shapes],
        compiler_params=pltpu.CompilerParams(vmem_limit_bytes=VMEM_BYTES),
        cost_estimate=cost(kc, slots),
    )(rows, cols, meta, blocks, alpha, *res, *img)


def gather_panel(chunk):
    half = chunk.shape[0] // 2
    first, second = chunk[:half], chunk[half:]
    places, pieces = [], []

    def add(value, dx, dz, stacked, part):
        places.append((dx, dz, 0, stacked, part))
        pieces.append(value)
        places.append((dx, dz, 1, stacked, part))
        pieces.append(row_shift(value, 0, 0, 1))

    first_z = row_shift(first, 0, 1, 0)
    second_x = {dx: row_shift(second, dx, 0, 0) for dx in (1, 3, 2)}
    pair = jnp.stack([first, first_z])
    first_x = {dx: row_shift(pair, dx, 0, 0) for dx in (1, 3, 2)}
    add(pair, 0, 0, True, 0)
    add(second, 0, 0, False, 1)
    add(row_shift(second, 0, 1, 0), 0, 1, False, 1)
    for dx in (1, 3, 2):
        add(second_x[dx], dx, 0, False, 1)
        add(row_shift(second_x[dx], 0, 1, 0), dx, 1, False, 1)
    for dx in (1, 3, 2):
        add(first_x[dx], dx, 0, True, 0)
    return tuple(places), pieces


def cell_layout():
    entries = []
    for dc in (1, 0):
        for dx in (2, 1, 3, 0):
            entries.append((1, dc, ((dx, 1),)))
        for dx in (1, 3, 2, 0):
            entries.append((0, dc, ((dx, 0), (dx, 1))))
        entries.append((1, dc, tuple((dx, 0) for dx in (2, 1, 3, 0))))
    return tuple(entries)


def scatter_cells(parts):
    other, own = parts[:9], parts[9:]
    summed = [mine + row_shift(sent, 0, 0, 1) for mine, sent in zip(own, other)]
    second_far = dict(zip((2, 1, 3, 0), summed[:4]))
    first = dict(zip((1, 3, 2, 0), summed[4:8]))
    second_near = dict(zip((2, 1, 3, 0), range(4)))
    second_got, first_got = [], []
    second_own = None
    for dx in (2, 1, 3, 0):
        term = summed[8][second_near[dx]] + row_shift(second_far[dx], 0, 1, 0)
        if dx:
            second_got.append(row_shift(term, -dx, 0, 0))
        else:
            second_own = term
    for dx in (1, 3, 2):
        first_got.append(row_shift(first[dx], -dx, 0, 0))
    pair = first[0] + first_got[0] + first_got[1] + first_got[2]
    first_own = pair[0] + row_shift(pair[1], 0, 1, 0)
    second_own = second_own + second_got[0] + second_got[1] + second_got[2]
    return jnp.concatenate([first_own, second_own], axis=0)


def per_device(solution, residual, direction, gradient, blocks, block_rows, block_cols, counts):
    tile_blocks = blocks[0]
    rows, cols = block_rows[0], block_cols[0]
    width = direction.shape[1]
    sol, res, dirn, grad = solution.T, residual.T, direction.T, gradient.T
    row_index, col_index = lax.axis_index("row"), lax.axis_index("col")
    meta = jnp.stack(
        [
            counts[0, 0],
            row_index // 4,
            (row_index // 2) % 2,
            row_index % 2,
            col_index // 4,
            col_index % 4,
        ]
    ).astype(jnp.int32)

    places, pieces = gather_panel(dirn)
    res_pair = jnp.stack([res, col_shift(res, 1, 0)])
    res_tile = [res_pair] + [col_shift(res_pair, 0, dy) for dy in (1, 2, 3)]

    image_parts = forward(tile_blocks, rows, cols, meta, places, pieces, width)
    got = [col_shift(image_parts[dy], 0, -dy) for dy in (1, 3, 2)]
    mine = image_parts[0] + got[0] + got[1] + got[2]
    image = mine[0] + col_shift(mine[1], 1, 0)
    image_pair = jnp.stack([image, col_shift(image, 1, 0)])
    image_tile = [image_pair] + [col_shift(image_pair, 0, dy) for dy in (1, 2, 3)]
    norms = jnp.concatenate([jnp.sum(grad * grad, axis=1), jnp.sum(image * image, axis=1)])
    norms = sum_everywhere(norms[None])[0]
    gamma, image_norms = norms[:width], norms[width:]
    alpha = (gamma / (image_norms + EPS))[:, None]

    layout = cell_layout()
    cell_parts = backward(
        tile_blocks, rows, cols, meta, alpha, res_tile, image_tile, layout, width
    )
    new_residual = res - alpha * image
    new_solution = sol + alpha * dirn
    new_gradient = scatter_cells(cell_parts)
    new_norms = jnp.sum(new_gradient * new_gradient, axis=1)
    new_norms = sum_everywhere(jnp.concatenate([new_norms, new_norms])[None])[0, :width]
    beta = (new_norms / gamma)[:, None]
    new_direction = new_gradient + beta * dirn
    return new_solution.T, new_residual.T, new_direction.T


def solution(mesh):
    placed = (
        P(("col", "row"), None),
        P(("row", "col"), None),
        P(("col", "row"), None),
        P(("col", "row"), None),
        P("row", "col", None, None),
        P("row", "col"),
        P("row", "col"),
        P("row", "col"),
    )
    return jax.shard_map(
        per_device,
        mesh=mesh,
        in_specs=placed,
        out_specs=(P(("col", "row"), None), P(("row", "col"), None), P(("col", "row"), None)),
        check_vma=False,
    )
```

time: 721 us -> 392 us (0.54)
  waiting for transfers between devices: 396 us -> 175 us
  starting transfers between devices: 0.34 us -> 125 us
  blocking collectives: 130 us -> 30.5 us
  other arithmetic: 74.1 us -> 7.79 us
  matrix products: 56 us -> 0 us
  Pallas kernels: 0 us -> 42.8 us
  local copies, waits for them, and re-layouts: 48.5 us -> 8.02 us
  between operations: 14.5 us -> 1.84 us
    reduce_scatter x2 -> x0, waiting for transfers between devices: 255 us -> none  [the longest x1 181 us: per_device(): lax.psum_scatter(cell_part, 'row', scatter_dimension=0, tiled=True)]
    ppermute x0 -> x55, waiting for transfers between devices: none -> 166 us  [the longest x43 154 us: row_shift(): return lax.ppermute(value, 'row', pairs)]
    all_gather x2 -> x0, waiting for transfers between devices: 141 us -> none  [the longest x1 95 us: per_device(): panel = lax.all_gather(direction, 'row', axis=0, tiled=True)]
    psum x2 -> x0, blocking collectives: 130 us -> none  [the longest x1 65.4 us: per_device(): gamma = lax.psum(jnp.sum(gradient * gradient, axis=0), ('row', 'col'))]
    ppermute x0 -> x55, starting transfers between devices: none -> 120 us  [the longest x43 82.6 us: row_shift(): return lax.ppermute(value, 'row', pairs)]
    scatter-add x2 -> x0, other arithmetic: 65.6 us -> none  [tile_apply(): return jax.ops.segment_sum(product, target_index, num_segments=target_count)]
    dot_general x2 -> x0, matrix products: 56 us -> none  [the longest x1 36.1 us: block_product(): jnp.einsum('bij,bjk->bik', tile_blocks, source_blocks, precision=lax.Prec...]
    pallas_call x0 -> x2, Pallas kernels: none -> 42.8 us  [the longest x1 21.9 us: backward(): pl.pallas_call(functools.partial(backward_kernel, kc, layout), grid_spec=...]
  transfers between devices with their start and end apart: 4 -> 56, of which waited for: 4 -> 23; matrix products, arithmetic and copies ran while one was open for 0% -> 2% of each run, Pallas kernels for 0% -> 0%
where the time goes in v1:
time: 392 us; the launch traced here: 390 us
  waiting for transfers between devices  175 us (45%)
  starting transfers between devices  125 us (32%)
  Pallas kernels  42.8 us (11%)
  blocking collectives  30.5 us (8%)
  local copies, waits for them, and re-layouts  8.02 us (2%)
  other arithmetic  7.79 us (2%)
    ppermute x43, waiting for transfers between devices, row_shift(): return lax.ppermute(value, 'row', pairs)  154 us
    ppermute x43, starting transfers between devices, row_shift(): return lax.ppermute(value, 'row', pairs)  82.6 us
    ppermute x12, starting transfers between devices, col_shift(): return lax.ppermute(value, 'col', pairs)  37.1 us
    all_to_all x1, blocking collectives, sum_everywhere(): got = lax.all_to_all(sent, ('row', 'col'), 0, 0, tiled=True)  30.5 us
    pallas_call x1, Pallas kernels, backward(): pl.pallas_call(functools.partial(backward_kernel, kc, layout), grid_spec=...  21.9 us
    pallas_call x1, Pallas kernels, forward(): pl.pallas_call(functools.partial(forward_kernel, kc, places), grid_spec=p...  20.9 us
    ppermute x12, waiting for transfers between devices, col_shift(): return lax.ppermute(value, 'col', pairs)  11.7 us
    all_to_all x1, waiting for transfers between devices, sum_everywhere(): got = lax.all_to_all(sent, ('row', 'col'), 0, 0, tiled=True)  8.97 us
  transfers between devices with their start and end apart: 56, of which 23 were waited for; matrix products, arithmetic and copies ran while one was open for 2% of the time, Pallas kernels for 0%

profile of v1, /device:TPU:1, one launch (start us, length us, event | category | flops | bytes accessed | tf_op | source)
XLA Modules:
  0.0 390.2 jit_solution(15851999561890021755)
XLA Ops:
  9.4 7.2 %collective-permute-done.9.refs_10_ = f32[32,4096]{1,0:T(8,128)S(1)} collective-permute-done((f32[32,4096]{1,0:T(8,128)S(1)}, f32[32,4096]{1,0:T(8,128)S(1)}, u32[]{:S(2)}, u32[]{:S(2)}) %collective-permute-start.9) | collective-permute-done | bytes 524320 | tf_op jit(solution)/shard_map/ppermute | solution.py:34
  18.2 10.9 %collective-permute-done.13.refs_14_ = f32[32,4096]{1,0:T(8,128)S(1)} collective-permute-done((f32[32,4096]{1,0:T(8,128)S(1)}, f32[32,4096]{1,0:T(8,128)S(1)}, u32[]{:S(2)}, u32[]{:S(2)}) %collective-permute-start.13) | collective-permute-done | bytes 524320 | tf_op jit(solution)/shard_map/ppermute | solution.py:34
  34.7 8.6 %collective-permute-done.11.refs_12_ = f32[32,4096]{1,0:T(8,128)S(1)} collective-permute-done((f32[32,4096]{1,0:T(8,128)S(1)}, f32[32,4096]{1,0:T(8,128)S(1)}, u32[]{:S(2)}, u32[]{:S(2)}) %collective-permute-start.11) | collective-permute-done | bytes 524320 | tf_op jit(solution)/shard_map/ppermute | solution.py:34
  45.8 8.8 %collective-permute-done.15.refs_16_ = f32[32,4096]{1,0:T(8,128)S(1)} collective-permute-done((f32[32,4096]{1,0:T(8,128)S(1)}, f32[32,4096]{1,0:T(8,128)S(1)}, u32[]{:S(2)}, u32[]{:S(2)}) %collective-permute-start.15) | collective-permute-done | bytes 524320 | tf_op jit(solution)/shard_map/ppermute | solution.py:34
  54.5 11.3 %collective-permute-done.7.refs_8_ = f32[32,4096]{1,0:T(8,128)} collective-permute-done((f32[32,4096]{1,0:T(8,128)S(1)}, f32[32,4096]{1,0:T(8,128)}, u32[]{:S(2)}, u32[]{:S(2)}) %collective-permute-start.7) | collective-permute-done | bytes 524320 | tf_op jit(solution)/shard_map/ppermute | solution.py:34
  71.7 5.2 %collective-permute-done.17.refs_18_ = f32[2,32,4096]{2,1,0:T(8,128)S(1)} collective-permute-done((f32[2,32,4096]{2,1,0:T(8,128)S(1)}, f32[2,32,4096]{2,1,0:T(8,128)S(1)}, u32[]{:S(2)}, u32[]{:S(2)}) %collective-permute-start.17) | collective-permute-done | bytes 1048608 | tf_op jit(solution)/shard_map/ppermute | solution.py:34
  76.9 6.1 %collective-permute-start.18 = (f32[2,32,4096]{2,1,0:T(8,128)S(1)}, f32[2,32,4096]{2,1,0:T(8,128)}, u32[]{:S(2)}, u32[]{:S(2)}) collective-permute-start(f32[2,32,4096]{2,1,0:T(8,128)S(1)} %collective-permute-done.17.refs_18_), channel_id=1, source_target_pairs={{8,0},{0,8},{24,16},{16,24},{40,32},{32,40},{56,48},{48,56},{72,64... | collective-permute-start | bytes 3145736 | tf_op jit(solution)/shard_map/ppermute | solution.py:34
  83.0 29.9 %collective-permute-done.19.refs_20_ = f32[2,32,4096]{2,1,0:T(8,128)} collective-permute-done((f32[2,32,4096]{2,1,0:T(8,128)S(1)}, f32[2,32,4096]{2,1,0:T(8,128)}, u32[]{:S(2)}, u32[]{:S(2)}) %collective-permute-start.19) | collective-permute-done | bytes 1048608 | tf_op jit(solution)/shard_map/ppermute | solution.py:34
  120.2 20.9 %shard_map.103 = (f32[2,64,768]{2,1,0:T(8,128)}, f32[2,64,768]{2,1,0:T(8,128)}, f32[2,64,768]{2,1,0:T(8,128)}, f32[2,64,768]{2,1,0:T(8,128)}) custom-call(s32[256]{0:T(256)} %bitcast.82, s32[256]{0:T(256)} %bitcast.84, s32[6]{0:T(128)} %stack.50.meta_ref, f32[256,128,128]{2,1,0:T(8,128)} %bitcast.71, f32[2,32,4096]{2,1,0:T(8,128)} %copy-done.1, ...), custom_call_target="tpu_custom_call" | custom-call | flops 1610612736 | bytes 50331648 | tf_op jit(solution)/shard_map/pallas_call | solution.py:220
  141.1 6.2 %collective-permute-start.23 = (f32[2,64,768]{2,1,0:T(8,128)}, f32[2,64,768]{2,1,0:T(8,128)S(1)}, u32[]{:S(2)}, u32[]{:S(2)}) collective-permute-start(f32[2,64,768]{2,1,0:T(8,128)} %get-tuple-element.26), channel_id=1, source_target_pairs={{3,0},{0,1},{1,2},{2,3},{7,4},{4,5},{5,6},{6,7},{11,8},{8,9},{9,10... | collective-permute-start | bytes 1179656 | tf_op jit(solution)/shard_map/ppermute | solution.py:39
  147.3 5.4 %collective-permute-start.24 = (f32[2,64,768]{2,1,0:T(8,128)}, f32[2,64,768]{2,1,0:T(8,128)S(1)}, u32[]{:S(2)}, u32[]{:S(2)}) collective-permute-start(f32[2,64,768]{2,1,0:T(8,128)} %get-tuple-element.27), channel_id=1, source_target_pairs={{1,0},{2,1},{3,2},{0,3},{5,4},{6,5},{7,6},{4,7},{9,8},{10,9},{11,1... | collective-permute-start | bytes 1179656 | tf_op jit(solution)/shard_map/ppermute | solution.py:39
  153.8 4.0 %collective-permute-start.27 = (f32[64,768]{1,0:T(8,128)S(1)}, f32[64,768]{1,0:T(8,128)S(1)}, u32[]{:S(2)}, u32[]{:S(2)}) collective-permute-start(f32[64,768]{1,0:T(8,128)S(1)} %bitcast.75), channel_id=1, source_target_pairs={{4,0},{5,1},{6,2},{7,3},{0,4},{1,5},{2,6},{3,7},{12,8},{13,9},{14,... | collective-permute-start | bytes 589832 | tf_op jit(solution)/shard_map/ppermute | solution.py:39
  157.8 3.0 collective-permute-done.23
  160.8 8.0 %collective-permute-done.24 = f32[2,64,768]{2,1,0:T(8,128)S(1)} collective-permute-done((f32[2,64,768]{2,1,0:T(8,128)}, f32[2,64,768]{2,1,0:T(8,128)S(1)}, u32[]{:S(2)}, u32[]{:S(2)}) %collective-permute-start.24) | collective-permute-done | bytes 393248 | tf_op jit(solution)/shard_map/ppermute | solution.py:39
  169.9 4.8 %collective-permute-start.26 = (f32[64,768]{1,0:T(8,128)S(1)}, f32[64,768]{1,0:T(8,128)S(1)}, u32[]{:S(2)}, u32[]{:S(2)}) collective-permute-start(f32[64,768]{1,0:T(8,128)S(1)} %slice_bitcast_fusion.6), channel_id=1, source_target_pairs={{4,0},{5,1},{6,2},{7,3},{0,4},{1,5},{2,6},{3,7},{12,8},{13,9},{14,... | collective-permute-start | bytes 589832 | tf_op jit(solution)/shard_map/ppermute | solution.py:39
  174.8 4.3 %collective-permute-start.28 = (f32[2,64,768]{2,1,0:T(8,128)S(1)}, f32[2,64,768]{2,1,0:T(8,128)S(1)}, u32[]{:S(2)}, u32[]{:S(2)}) collective-permute-start(f32[2,64,768]{2,1,0:T(8,128)S(1)} %pad_maximum_fusion.2.refs_0_), channel_id=1, source_target_pairs={{1,0},{2,1},{3,2},{0,3},{5,4},{6,5},{7,6},{4,7},{9,8},{10,9},{11,1... | collective-permute-start | bytes 1179656 | tf_op jit(solution)/shard_map/ppermute | solution.py:39
  182.8 3.6 collective-permute-start.29
  187.3 3.3 collective-permute-start.32
  191.6 30.5 %all_to_all.10 = f32[128,1,128]{2,1,0:T(1,128)S(1)} all-to-all(f32[128,1,128]{2,1,0:T(1,128)S(1)} %broadcast_in_dim.4), channel_id=1, replica_groups=mesh['row'=16,'col'=8] {'row','col'}, dimensions={0} | all-to-all | bytes 131072 | tf_op jit(solution)/shard_map/all_to_all | solution.py:45
  223.8 21.9 %shard_map.104 = (f32[32,4096]{1,0:T(8,128)}, f32[32,4096]{1,0:T(8,128)}, f32[32,4096]{1,0:T(8,128)}, f32[32,4096]{1,0:T(8,128)}, f32[2,32,4096]{2,1,0:T(8,128)}...) custom-call(s32[256]{0:T(256)} %bitcast.83, ...), custom_call_target="tpu_custom_call" | custom-call | flops 1610612736 | bytes 50331648 | tf_op jit(solution)/shard_map/pallas_call | solution.py:248
  245.7 3.1 collective-permute-start.36
  258.9 4.3 %collective-permute-start.41 = (f32[2,32,4096]{2,1,0:T(8,128)S(1)}, f32[2,32,4096]{2,1,0:T(8,128)S(1)}, u32[]{:S(2)}, u32[]{:S(2)}) collective-permute-start(f32[2,32,4096]{2,1,0:T(8,128)S(1)} %add.123), channel_id=1, source_target_pairs={{64,0},{72,8},{80,16},{88,24},{96,32},{104,40},{112,48},{120,56},{... | collective-permute-start | bytes 3145736 | tf_op jit(solution)/shard_map/ppermute | solution.py:34
  266.8 4.0 %collective-permute-start.45 = (f32[32,4096]{1,0:T(8,128)S(1)}, f32[32,4096]{1,0:T(8,128)S(1)}, u32[]{:S(2)}, u32[]{:S(2)}) collective-permute-start(f32[32,4096]{1,0:T(8,128)S(1)} %add.127), channel_id=1, source_target_pairs={{16,0},{24,8},{0,16},{8,24},{48,32},{56,40},{32,48},{40,56},{80,64... | collective-permute-start | bytes 1572872 | tf_op jit(solution)/shard_map/ppermute | solution.py:34
  270.8 11.2 %collective-permute-done.37 = f32[2,32,4096]{2,1,0:T(8,128)S(1)} collective-permute-done((f32[2,32,4096]{2,1,0:T(8,128)S(1)}, f32[2,32,4096]{2,1,0:T(8,128)S(1)}, u32[]{:S(2)}, u32[]{:S(2)}) %collective-permute-start.37) | collective-permute-done | bytes 1048608 | tf_op jit(solution)/shard_map/ppermute | solution.py:34
  282.0 31.0 %collective-permute-start.50 = (f32[32,4096]{1,0:T(8,128)S(1)}, f32[32,4096]{1,0:T(8,128)S(1)}, u32[]{:S(2)}, u32[]{:S(2)}) collective-permute-start(f32[32,4096]{1,0:T(8,128)S(1)} %add.132), channel_id=1, source_target_pairs={{16,0},{24,8},{0,16},{8,24},{48,32},{56,40},{32,48},{40,56},{80,64... | collective-permute-start | bytes 1572872 | tf_op jit(solution)/shard_map/ppermute | solution.py:34
  316.3 7.9 %collective-permute-done.50 = f32[32,4096]{1,0:T(8,128)S(1)} collective-permute-done((f32[32,4096]{1,0:T(8,128)S(1)}, f32[32,4096]{1,0:T(8,128)S(1)}, u32[]{:S(2)}, u32[]{:S(2)}) %collective-permute-start.50) | collective-permute-done | bytes 524320 | tf_op jit(solution)/shard_map/ppermute | solution.py:34
  324.2 11.2 %collective-permute-done.53 = f32[32,4096]{1,0:T(8,128)S(1)} collective-permute-done((f32[32,4096]{1,0:T(8,128)S(1)}, f32[32,4096]{1,0:T(8,128)S(1)}, u32[]{:S(2)}, u32[]{:S(2)}) %collective-permute-start.53) | collective-permute-done | bytes 524320 | tf_op jit(solution)/shard_map/ppermute | solution.py:34
  335.5 11.2 %collective-permute-done.47 = f32[32,4096]{1,0:T(8,128)S(1)} collective-permute-done((f32[32,4096]{1,0:T(8,128)S(1)}, f32[32,4096]{1,0:T(8,128)S(1)}, u32[]{:S(2)}, u32[]{:S(2)}) %collective-permute-start.47) | collective-permute-done | bytes 524320 | tf_op jit(solution)/shard_map/ppermute | solution.py:34
  349.7 8.2 %collective-permute-done.42 = f32[32,4096]{1,0:T(8,128)S(1)} collective-permute-done((f32[32,4096]{1,0:T(8,128)S(1)}, f32[32,4096]{1,0:T(8,128)S(1)}, u32[]{:S(2)}, u32[]{:S(2)}) %collective-permute-start.42) | collective-permute-done | bytes 524320 | tf_op jit(solution)/shard_map/ppermute | solution.py:34
  359.2 14.0 %collective-permute-done.51 = f32[32,4096]{1,0:T(8,128)S(1)} collective-permute-done((f32[32,4096]{1,0:T(8,128)S(1)}, f32[32,4096]{1,0:T(8,128)S(1)}, u32[]{:S(2)}, u32[]{:S(2)}) %collective-permute-start.51) | collective-permute-done | bytes 524320 | tf_op jit(solution)/shard_map/ppermute | solution.py:34
  374.2 5.1 %all-to-all-start.1 = ((f32[128,1,128]{2,1,0:T(1,128)}), f32[128,1,128]{2,1,0:T(1,128)S(1)}, u32[]{:S(2)}, u32[]{:S(2)}) async-start(f32[128,1,128]{2,1,0:T(1,128)} %broadcast_in_dim.5), calls=%async_computation.1 | async-start | bytes 131072 | tf_op jit(solution)/shard_map/all_to_all | solution.py:45
  380.1 9.0 %all-to-all-done.1 = f32[128,1,128]{2,1,0:T(1,128)S(1)} async-done(((f32[128,1,128]{2,1,0:T(1,128)}), f32[128,1,128]{2,1,0:T(1,128)S(1)}, u32[]{:S(2)}, u32[]{:S(2)}) %all-to-all-start.1) | async-done | bytes 65568 | tf_op jit(solution)/shard_map/all_to_all | solution.py:45
  (189 shorter events, 64.4 us)
Async XLA Ops:
  4.1 25.0 %collective-permute-start.13 = (f32[32,4096]{1,0:T(8,128)S(1)}, f32[32,4096]{1,0:T(8,128)S(1)}, u32[]{:S(2)}, u32[]{:S(2)}) collective-permute-start(f32[32,4096]{1,0:T(8,128)S(1)} %get-tuple-element.52.refs_2_), channel_id=1, source_target_pairs={{64,0},{72,8},{80,16},{88,24},{96,32},{104,40},{112,48},{120,56},{... | collective-permute-start | bytes 1572872 | tf_op jit(solution)/shard_map/ppermute | solution.py:34
  6.5 24.2 %collective-permute-start.5 = (f32[32,4096]{1,0:T(8,128)S(1)}, f32[32,4096]{1,0:T(8,128)S(1)}, u32[]{:S(2)}, u32[]{:S(2)}) collective-permute-start(f32[32,4096]{1,0:T(8,128)S(1)} %get-tuple-element.52.refs_2_), channel_id=1, source_target_pairs={{32,0},{40,8},{48,16},{56,24},{64,32},{72,40},{80,48},{88,56},{96,... | collective-permute-start | bytes 1572872 | tf_op jit(solution)/shard_map/ppermute | solution.py:34
  7.7 23.1 %collective-permute-start = (f32[32,4096]{1,0:T(8,128)S(1)}, f32[32,4096]{1,0:T(8,128)S(1)}, u32[]{:S(2)}, u32[]{:S(2)}) collective-permute-start(f32[32,4096]{1,0:T(8,128)S(1)} %get-tuple-element.54), channel_id=1, source_target_pairs={{16,0},{24,8},{0,16},{8,24},{48,32},{56,40},{32,48},{40,56},{80,64... | collective-permute-start | bytes 1572872 | tf_op jit(solution)/shard_map/ppermute | solution.py:34
  9.3 22.9 %collective-permute-start.3 = (f32[32,4096]{1,0:T(8,128)S(1)}, f32[32,4096]{1,0:T(8,128)S(1)}, u32[]{:S(2)}, u32[]{:S(2)}) collective-permute-start(f32[32,4096]{1,0:T(8,128)S(1)} %get-tuple-element.52.refs_2_), channel_id=1, source_target_pairs={{16,0},{24,8},{0,16},{8,24},{48,32},{56,40},{32,48},{40,56},{80,64... | collective-permute-start | bytes 1572872 | tf_op jit(solution)/shard_map/ppermute | solution.py:34
  30.8 23.8 %collective-permute-start.15 = (f32[32,4096]{1,0:T(8,128)S(1)}, f32[32,4096]{1,0:T(8,128)S(1)}, u32[]{:S(2)}, u32[]{:S(2)}) collective-permute-start(f32[32,4096]{1,0:T(8,128)S(1)} %collective-permute-done.13.refs_14_), channel_id=1, source_target_pairs={{16,0},{24,8},{0,16},{8,24},{48,32},{56,40},{32,48},{40,56},{80,64... | collective-permute-start | bytes 1572872 | tf_op jit(solution)/shard_map/ppermute | solution.py:34
  30.8 35.0 %collective-permute-start.7 = (f32[32,4096]{1,0:T(8,128)S(1)}, f32[32,4096]{1,0:T(8,128)}, u32[]{:S(2)}, u32[]{:S(2)}) collective-permute-start(f32[32,4096]{1,0:T(8,128)S(1)} %collective-permute-done.5.refs_6_), channel_id=1, source_target_pairs={{16,0},{24,8},{0,16},{8,24},{48,32},{56,40},{32,48},{40,56},{80,64... | collective-permute-start | bytes 1572872 | tf_op jit(solution)/shard_map/ppermute | solution.py:34
  32.2 33.6 %collective-permute-start.10 = (f32[32,4096]{1,0:T(8,128)S(1)}, f32[32,4096]{1,0:T(8,128)S(1)}, u32[]{:S(2)}, u32[]{:S(2)}) collective-permute-start(f32[32,4096]{1,0:T(8,128)S(1)} %collective-permute-done.9.refs_10_), channel_id=1, source_target_pairs={{8,0},{0,8},{24,16},{16,24},{40,32},{32,40},{56,48},{48,56},{72,64... | collective-permute-start | bytes 1572872 | tf_op jit(solution)/shard_map/ppermute | solution.py:34
  34.6 31.8 %collective-permute-start.14 = (f32[32,4096]{1,0:T(8,128)S(1)}, f32[32,4096]{1,0:T(8,128)S(1)}, u32[]{:S(2)}, u32[]{:S(2)}) collective-permute-start(f32[32,4096]{1,0:T(8,128)S(1)} %collective-permute-done.13.refs_14_), channel_id=1, source_target_pairs={{8,0},{0,8},{24,16},{16,24},{40,32},{32,40},{56,48},{48,56},{72,64... | collective-permute-start | bytes 1572872 | tf_op jit(solution)/shard_map/ppermute | solution.py:34
  43.3 25.7 %collective-permute-start.6 = (f32[32,4096]{1,0:T(8,128)S(1)}, f32[32,4096]{1,0:T(8,128)S(1)}, u32[]{:S(2)}, u32[]{:S(2)}) collective-permute-start(f32[32,4096]{1,0:T(8,128)S(1)} %collective-permute-done.5.refs_6_), channel_id=1, source_target_pairs={{8,0},{0,8},{24,16},{16,24},{40,32},{32,40},{56,48},{48,56},{72,64... | collective-permute-start | bytes 1572872 | tf_op jit(solution)/shard_map/ppermute | solution.py:34
  54.5 22.4 %collective-permute-start.17 = (f32[2,32,4096]{2,1,0:T(8,128)S(1)}, f32[2,32,4096]{2,1,0:T(8,128)S(1)}, u32[]{:S(2)}, u32[]{:S(2)}) collective-permute-start(f32[2,32,4096]{2,1,0:T(8,128)S(1)} %pad_maximum_fusion.refs_0_), channel_id=1, source_target_pairs={{32,0},{40,8},{48,16},{56,24},{64,32},{72,40},{80,48},{88,56},{96,... | collective-permute-start | bytes 3145736 | tf_op jit(solution)/shard_map/ppermute | solution.py:34
  65.9 47.0 %collective-permute-start.19 = (f32[2,32,4096]{2,1,0:T(8,128)S(1)}, f32[2,32,4096]{2,1,0:T(8,128)}, u32[]{:S(2)}, u32[]{:S(2)}) collective-permute-start(f32[2,32,4096]{2,1,0:T(8,128)S(1)} %pad_maximum_fusion.refs_0_), channel_id=1, source_target_pairs={{96,0},{104,8},{112,16},{120,24},{0,32},{8,40},{16,48},{24,56},{32... | collective-permute-start | bytes 3145736 | tf_op jit(solution)/shard_map/ppermute | solution.py:34
  65.9 49.4 %collective-permute-start.21 = (f32[2,32,4096]{2,1,0:T(8,128)S(1)}, f32[2,32,4096]{2,1,0:T(8,128)}, u32[]{:S(2)}, u32[]{:S(2)}) collective-permute-start(f32[2,32,4096]{2,1,0:T(8,128)S(1)} %pad_maximum_fusion.refs_0_), channel_id=1, source_target_pairs={{64,0},{72,8},{80,16},{88,24},{96,32},{104,40},{112,48},{120,56},{... | collective-permute-start | bytes 3145736 | tf_op jit(solution)/shard_map/ppermute | solution.py:34
  70.6 49.6 %collective-permute-start.1 = (f32[2,32,4096]{2,1,0:T(8,128)S(1)}, f32[2,32,4096]{2,1,0:T(8,128)}, u32[]{:S(2)}, u32[]{:S(2)}) collective-permute-start(f32[2,32,4096]{2,1,0:T(8,128)S(1)} %pad_maximum_fusion.refs_0_), channel_id=1, source_target_pairs={{8,0},{0,8},{24,16},{16,24},{40,32},{32,40},{56,48},{48,56},{72,64... | collective-permute-start | bytes 3145736 | tf_op jit(solution)/shard_map/ppermute | solution.py:34
  71.3 44.0 %collective-permute-start.16 = (f32[32,4096]{1,0:T(8,128)S(1)}, f32[32,4096]{1,0:T(8,128)S(1)}, u32[]{:S(2)}, u32[]{:S(2)}) collective-permute-start(f32[32,4096]{1,0:T(8,128)S(1)} %collective-permute-done.15.refs_16_), channel_id=1, source_target_pairs={{8,0},{0,8},{24,16},{16,24},{40,32},{32,40},{56,48},{48,56},{72,64... | collective-permute-start | bytes 1572872 | tf_op jit(solution)/shard_map/ppermute | solution.py:34
  76.9 43.2 %collective-permute-start.18 = (f32[2,32,4096]{2,1,0:T(8,128)S(1)}, f32[2,32,4096]{2,1,0:T(8,128)}, u32[]{:S(2)}, u32[]{:S(2)}) collective-permute-start(f32[2,32,4096]{2,1,0:T(8,128)S(1)} %collective-permute-done.17.refs_18_), channel_id=1, source_target_pairs={{8,0},{0,8},{24,16},{16,24},{40,32},{32,40},{56,48},{48,56},{72,64... | collective-permute-start | bytes 3145736 | tf_op jit(solution)/shard_map/ppermute | solution.py:34
  147.3 21.6 %collective-permute-start.24 = (f32[2,64,768]{2,1,0:T(8,128)}, f32[2,64,768]{2,1,0:T(8,128)S(1)}, u32[]{:S(2)}, u32[]{:S(2)}) collective-permute-start(f32[2,64,768]{2,1,0:T(8,128)} %get-tuple-element.27), channel_id=1, source_target_pairs={{1,0},{2,1},{3,2},{0,3},{5,4},{6,5},{7,6},{4,7},{9,8},{10,9},{11,1... | collective-permute-start | bytes 1179656 | tf_op jit(solution)/shard_map/ppermute | solution.py:39
  182.8 40.1 %collective-permute-start.29 = (f32[2,64,768]{2,1,0:T(8,128)S(1)}, f32[2,64,768]{2,1,0:T(8,128)S(1)}, u32[]{:S(2)}, u32[]{:S(2)}) collective-permute-start(f32[2,64,768]{2,1,0:T(8,128)S(1)} %pad_maximum_fusion.2.refs_0_), channel_id=1, source_target_pairs={{2,0},{3,1},{0,2},{1,3},{6,4},{7,5},{4,6},{5,7},{10,8},{11,9},{8,1... | collective-permute-start | bytes 1179656 | tf_op jit(solution)/shard_map/ppermute | solution.py:39
  186.4 36.5 %collective-permute-start.30 = (f32[2,64,768]{2,1,0:T(8,128)S(1)}, f32[2,64,768]{2,1,0:T(8,128)S(1)}, u32[]{:S(2)}, u32[]{:S(2)}) collective-permute-start(f32[2,64,768]{2,1,0:T(8,128)S(1)} %pad_maximum_fusion.2.refs_0_), channel_id=1, source_target_pairs={{3,0},{0,1},{1,2},{2,3},{7,4},{4,5},{5,6},{6,7},{11,8},{8,9},{9,10... | collective-permute-start | bytes 1179656 | tf_op jit(solution)/shard_map/ppermute | solution.py:39
  187.3 35.6 %collective-permute-start.32 = (f32[2,64,768]{2,1,0:T(8,128)S(1)}, f32[2,64,768]{2,1,0:T(8,128)}, u32[]{:S(2)}, u32[]{:S(2)}) collective-permute-start(f32[2,64,768]{2,1,0:T(8,128)S(1)} %pad_maximum_fusion.3.refs_4_), channel_id=1, source_target_pairs={{1,0},{2,1},{3,2},{0,3},{5,4},{6,5},{7,6},{4,7},{9,8},{10,9},{11,1... | collective-permute-start | bytes 1179656 | tf_op jit(solution)/shard_map/ppermute | solution.py:39
  190.6 32.3 %collective-permute-start.33 = (f32[2,64,768]{2,1,0:T(8,128)S(1)}, f32[2,64,768]{2,1,0:T(8,128)}, u32[]{:S(2)}, u32[]{:S(2)}) collective-permute-start(f32[2,64,768]{2,1,0:T(8,128)S(1)} %pad_maximum_fusion.3.refs_4_), channel_id=1, source_target_pairs={{2,0},{3,1},{0,2},{1,3},{6,4},{7,5},{4,6},{5,7},{10,8},{11,9},{8,1... | collective-permute-start | bytes 1179656 | tf_op jit(solution)/shard_map/ppermute | solution.py:39
  190.7 32.2 %collective-permute-start.34 = (f32[2,64,768]{2,1,0:T(8,128)S(1)}, f32[2,64,768]{2,1,0:T(8,128)}, u32[]{:S(2)}, u32[]{:S(2)}) collective-permute-start(f32[2,64,768]{2,1,0:T(8,128)S(1)} %pad_maximum_fusion.3.refs_4_), channel_id=1, source_target_pairs={{3,0},{0,1},{1,2},{2,3},{7,4},{4,5},{5,6},{6,7},{11,8},{8,9},{9,10... | collective-permute-start | bytes 1179656 | tf_op jit(solution)/shard_map/ppermute | solution.py:39
  256.2 25.9 %collective-permute-start.37 = (f32[2,32,4096]{2,1,0:T(8,128)S(1)}, f32[2,32,4096]{2,1,0:T(8,128)S(1)}, u32[]{:S(2)}, u32[]{:S(2)}) collective-permute-start(f32[2,32,4096]{2,1,0:T(8,128)S(1)} %add.119), channel_id=1, source_target_pairs={{96,0},{104,8},{112,16},{120,24},{0,32},{8,40},{16,48},{24,56},{32... | collective-permute-start | bytes 3145736 | tf_op jit(solution)/shard_map/ppermute | solution.py:34
  256.3 56.7 %collective-permute-start.39 = (f32[2,32,4096]{2,1,0:T(8,128)S(1)}, f32[2,32,4096]{2,1,0:T(8,128)S(1)}, u32[]{:S(2)}, u32[]{:S(2)}) collective-permute-start(f32[2,32,4096]{2,1,0:T(8,128)S(1)} %add.121), channel_id=1, source_target_pairs={{32,0},{40,8},{48,16},{56,24},{64,32},{72,40},{80,48},{88,56},{96,... | collective-permute-start | bytes 3145736 | tf_op jit(solution)/shard_map/ppermute | solution.py:34
  258.9 54.1 %collective-permute-start.41 = (f32[2,32,4096]{2,1,0:T(8,128)S(1)}, f32[2,32,4096]{2,1,0:T(8,128)S(1)}, u32[]{:S(2)}, u32[]{:S(2)}) collective-permute-start(f32[2,32,4096]{2,1,0:T(8,128)S(1)} %add.123), channel_id=1, source_target_pairs={{64,0},{72,8},{80,16},{88,24},{96,32},{104,40},{112,48},{120,56},{... | collective-permute-start | bytes 3145736 | tf_op jit(solution)/shard_map/ppermute | solution.py:34
  263.3 51.5 %collective-permute-start.43 = (f32[4,32,4096]{2,1,0:T(8,128)S(1)}, f32[4,32,4096]{2,1,0:T(8,128)S(1)}, u32[]{:S(2)}, u32[]{:S(2)}) collective-permute-start(f32[4,32,4096]{2,1,0:T(8,128)S(1)} %copy-done.33), channel_id=1, source_target_pairs={{8,0},{0,8},{24,16},{16,24},{40,32},{32,40},{56,48},{48,56},{72,64... | collective-permute-start | bytes 6291464 | tf_op jit(solution)/shard_map/ppermute | solution.py:34
  266.8 91.2 %collective-permute-start.45 = (f32[32,4096]{1,0:T(8,128)S(1)}, f32[32,4096]{1,0:T(8,128)S(1)}, u32[]{:S(2)}, u32[]{:S(2)}) collective-permute-start(f32[32,4096]{1,0:T(8,128)S(1)} %add.127), channel_id=1, source_target_pairs={{16,0},{24,8},{0,16},{8,24},{48,32},{56,40},{32,48},{40,56},{80,64... | collective-permute-start | bytes 1572872 | tf_op jit(solution)/shard_map/ppermute | solution.py:34
  282.0 42.2 %collective-permute-start.50 = (f32[32,4096]{1,0:T(8,128)S(1)}, f32[32,4096]{1,0:T(8,128)S(1)}, u32[]{:S(2)}, u32[]{:S(2)}) collective-permute-start(f32[32,4096]{1,0:T(8,128)S(1)} %add.132), channel_id=1, source_target_pairs={{16,0},{24,8},{0,16},{8,24},{48,32},{56,40},{32,48},{40,56},{80,64... | collective-permute-start | bytes 1572872 | tf_op jit(solution)/shard_map/ppermute | solution.py:34
  313.0 22.5 %collective-permute-start.53 = (f32[32,4096]{1,0:T(8,128)S(1)}, f32[32,4096]{1,0:T(8,128)S(1)}, u32[]{:S(2)}, u32[]{:S(2)}) collective-permute-start(f32[32,4096]{1,0:T(8,128)S(1)} %add.135), channel_id=1, source_target_pairs={{16,0},{24,8},{0,16},{8,24},{48,32},{56,40},{32,48},{40,56},{80,64... | collective-permute-start | bytes 1572872 | tf_op jit(solution)/shard_map/ppermute | solution.py:34
  313.0 33.7 %collective-permute-start.47 = (f32[32,4096]{1,0:T(8,128)S(1)}, f32[32,4096]{1,0:T(8,128)S(1)}, u32[]{:S(2)}, u32[]{:S(2)}) collective-permute-start(f32[32,4096]{1,0:T(8,128)S(1)} %add.129), channel_id=1, source_target_pairs={{16,0},{24,8},{0,16},{8,24},{48,32},{56,40},{32,48},{40,56},{80,64... | collective-permute-start | bytes 1572872 | tf_op jit(solution)/shard_map/ppermute | solution.py:34
  314.8 43.2 %collective-permute-start.42 = (f32[32,4096]{1,0:T(8,128)S(1)}, f32[32,4096]{1,0:T(8,128)S(1)}, u32[]{:S(2)}, u32[]{:S(2)}) collective-permute-start(f32[32,4096]{1,0:T(8,128)S(1)} %slice_bitcast_fusion.4), channel_id=1, source_target_pairs={{16,0},{24,8},{0,16},{8,24},{48,32},{56,40},{32,48},{40,56},{80,64... | collective-permute-start | bytes 1572872 | tf_op jit(solution)/shard_map/ppermute | solution.py:34
  347.0 26.1 %collective-permute-start.51 = (f32[32,4096]{1,0:T(8,128)S(1)}, f32[32,4096]{1,0:T(8,128)S(1)}, u32[]{:S(2)}, u32[]{:S(2)}) collective-permute-start(f32[32,4096]{1,0:T(8,128)S(1)} %get-tuple-element.51), channel_id=1, source_target_pairs={{96,0},{104,8},{112,16},{120,24},{0,32},{8,40},{16,48},{24,56},{32... | collective-permute-start | bytes 1572872 | tf_op jit(solution)/shard_map/ppermute | solution.py:34
  347.1 26.1 %collective-permute-start.54 = (f32[32,4096]{1,0:T(8,128)S(1)}, f32[32,4096]{1,0:T(8,128)S(1)}, u32[]{:S(2)}, u32[]{:S(2)}) collective-permute-start(f32[32,4096]{1,0:T(8,128)S(1)} %get-tuple-element.50), channel_id=1, source_target_pairs={{32,0},{40,8},{48,16},{56,24},{64,32},{72,40},{80,48},{88,56},{96,... | collective-permute-start | bytes 1572872 | tf_op jit(solution)/shard_map/ppermute | solution.py:34
  (59 other events, 1517.4 us)

commit v2 on v0

v2 whole, which is shorter than its diff:
```python
import functools

import jax
import jax.numpy as jnp
from jax import lax
from jax.experimental import pallas as pl
from jax.experimental.pallas import tpu as pltpu
from jax.sharding import PartitionSpec as P

EPS = 1e-06
BS = 128
GROUP = 16
HEAD = 8
CHUNKS = 1
VMEM_BYTES = 56 * 1024 * 1024

NX, NZ, NCORE = 4, 2, 2
NZH, NY = 2, 4


def row_of(x, z, c):
    return (x % NX) * 4 + (z % NZ) * 2 + c % NCORE


def col_of(z, y):
    return (z % NZH) * 4 + y % NY


def row_shift(value, dx, dz, dc):
    pairs = [
        (row_of(x + dx, z + dz, c + dc), row_of(x, z, c))
        for x in range(NX)
        for z in range(NZ)
        for c in range(NCORE)
    ]
    return lax.ppermute(value, "row", pairs)


def col_shift(value, dz, dy):
    pairs = [(col_of(z + dz, y + dy), col_of(z, y)) for z in range(NZH) for y in range(NY)]
    return lax.ppermute(value, "col", pairs)


def sum_over(row, axes):
    count = lax.axis_size(axes)
    sent = jnp.broadcast_to(row[None], (count, 1, row.shape[1]))
    return jnp.sum(lax.all_to_all(sent, axes, 0, 0, tiled=True), axis=0)


def split(value):
    high = value.astype(jnp.bfloat16)
    low = (value - high.astype(jnp.float32)).astype(jnp.bfloat16)
    return high, low


def doubled(value):
    high, low = split(value)
    return jnp.concatenate(
        [jnp.concatenate([high, high], axis=1), jnp.concatenate([low, low], axis=1)], axis=0
    )


def start_blocks(blocks, held, sems, groups):
    def start(group, _):
        span = pl.ds(group * GROUP, GROUP)
        pltpu.make_async_copy(blocks.at[span], held.at[span], sems.at[group]).start()
        return 0

    lax.fori_loop(0, groups, start, 0)


def wait_blocks(blocks, held, sems, group):
    span = pl.ds(group * GROUP, GROUP)
    pltpu.make_async_copy(blocks.at[span], held.at[span], sems.at[group]).wait()


def forward_kernel(kc, places, meta_ref, blocks_ref, *refs):
    pieces = refs[: len(places)]
    outs = refs[len(places) : len(places) + NY]
    panel, acc, held, sems, block_sems = refs[len(places) + NY :]
    count = meta_ref[0]
    x, z, c = meta_ref[1], meta_ref[2], meta_ref[3]
    groups = (count + GROUP - 1) // GROUP
    slots = held.shape[0]

    copies = []
    for number, (dc, entries) in enumerate(places):
        for first, size, (dx, dz), start in entries:
            owner = ((x + dx) % NX) * 4 + ((z + dz) % NZ) * 2 + (c + dc) % NCORE
            copies.append(
                pltpu.make_async_copy(
                    pieces[number].at[pl.ds(first, size)],
                    panel.at[owner, pl.ds(start, size), :],
                    sems.at[len(copies)],
                )
            )
    for copy in copies:
        copy.start()
    start_blocks(blocks_ref, held, block_sems, groups)
    acc[...] = jnp.zeros_like(acc)
    for copy in copies:
        copy.wait()

    def work(group, _):
        wait_blocks(blocks_ref, held, block_sems, group)
        for inner in range(GROUP):
            slot = group * GROUP + inner
            cell = meta_ref[HEAD + slots + slot]
            offset = pl.multiple_of((cell % 32) * BS, BS)
            left = doubled(panel[cell // 32, :, pl.ds(offset, BS)])
            high, low = split(held[slot])
            right = jnp.concatenate([high, low], axis=1)
            both = lax.dot_general(
                right, left, (((1,), (1,)), ((), ())), preferred_element_type=jnp.float32
            )
            live = jnp.where(slot < count, 1.0, 0.0)
            acc[meta_ref[HEAD + slot]] += both * live
        return 0

    lax.fori_loop(0, groups, work, 0)

    zh, y = meta_ref[4], meta_ref[5]
    per = acc.shape[0] // (NZH * NY)
    for dy in range(NY):
        for dz in range(NZH):
            piece = ((zh + dz) % NZH) * 4 + (y + dy) % NY
            for t in range(per):
                both = acc[piece * per + t].T
                outs[dy][dz, :, t * BS : (t + 1) * BS] = both[:kc] + both[kc:]


def backward_kernel(kc, layout, meta_ref, blocks_ref, alpha_ref, *refs):
    res = refs[:NY]
    img = refs[NY : 2 * NY]
    outs = refs[2 * NY : 2 * NY + len(layout)]
    source, acc, held, sems, block_sems = refs[2 * NY + len(layout) :]
    count = meta_ref[0]
    x, z, c = meta_ref[1], meta_ref[2], meta_ref[3]
    groups = (count + GROUP - 1) // GROUP
    slots = held.shape[0]
    start_blocks(blocks_ref, held, block_sems, groups)

    zh, y = meta_ref[4], meta_ref[5]
    per = source.shape[0] // (NZH * NY)
    alpha = alpha_ref[...]
    for dy in range(NY):
        for dz in range(NZH):
            piece = ((zh + dz) % NZH) * 4 + (y + dy) % NY
            for t in range(per):
                span = slice(t * BS, (t + 1) * BS)
                value = res[dy][dz, :, span] - alpha * img[dy][dz, :, span]
                source[piece * per + t] = doubled(value)

    def clear(i, _):
        acc[i] = jnp.zeros(acc.shape[1:], jnp.float32)
        return 0

    lax.fori_loop(0, acc.shape[0], clear, 0)

    def work(group, _):
        wait_blocks(blocks_ref, held, block_sems, group)
        for inner in range(GROUP):
            slot = group * GROUP + inner
            left = source[meta_ref[HEAD + slot]]
            high, low = split(held[slot])
            right = jnp.concatenate([high, low], axis=0)
            both = lax.dot_general(
                left, right, (((1,), (0,)), ((), ())), preferred_element_type=jnp.float32
            )
            live = jnp.where(slot < count, 1.0, 0.0)
            cell = meta_ref[HEAD + slots + slot]
            offset = pl.multiple_of((cell % 32) * BS, BS)
            acc[cell // 32, :, pl.ds(offset, BS)] += (both[:kc] + both[kc:]) * live
        return 0

    lax.fori_loop(0, groups, work, 0)

    copies = []
    for number, (dc, entries) in enumerate(layout):
        for first, size, (dx, dz), start in entries:
            owner = ((x + dx) % NX) * 4 + ((z + dz) % NZ) * 2 + (c + dc) % NCORE
            copies.append(
                pltpu.make_async_copy(
                    acc.at[owner, pl.ds(start, size), :],
                    outs[number].at[pl.ds(first, size)],
                    sems.at[len(copies)],
                )
            )
    for copy in copies:
        copy.start()
    for copy in copies:
        copy.wait()


def cost(kc, slots):
    return pl.CostEstimate(
        flops=6 * slots * BS * BS * kc,
        bytes_accessed=4 * (slots * BS * BS + 2 * 16 * kc * 4096),
        transcendentals=0,
    )


def forward(blocks, meta, places, pieces, kc):
    slots = blocks.shape[0]
    smem, vmem = pl.BlockSpec(memory_space=pltpu.SMEM), pl.BlockSpec(memory_space=pltpu.VMEM)
    any_spec = pl.BlockSpec(memory_space=pl.ANY)
    copies = sum(len(entries) for _, entries in places)
    return pl.pallas_call(
        functools.partial(forward_kernel, kc, places),
        in_specs=[smem] + [any_spec] * (1 + len(pieces)),
        out_specs=[vmem] * NY,
        scratch_shapes=[
            pltpu.VMEM((16, kc, 4096), jnp.float32),
            pltpu.VMEM((48, BS, 2 * kc), jnp.float32),
            pltpu.VMEM(blocks.shape, jnp.float32),
            pltpu.SemaphoreType.DMA((copies,)),
            pltpu.SemaphoreType.DMA((slots // GROUP,)),
        ],
        out_shape=[jax.ShapeDtypeStruct((NZH, kc, 6 * BS), jnp.float32)] * NY,
        compiler_params=pltpu.CompilerParams(vmem_limit_bytes=VMEM_BYTES),
        cost_estimate=cost(kc, slots),
    )(meta, blocks, *pieces)


def backward(blocks, meta, alpha, res, img, layout, kc):
    slots = blocks.shape[0]
    smem, vmem = pl.BlockSpec(memory_space=pltpu.SMEM), pl.BlockSpec(memory_space=pltpu.VMEM)
    any_spec = pl.BlockSpec(memory_space=pl.ANY)
    shapes = [(sum(entry[1] for entry in entries), 4096) for _, entries in layout]
    return pl.pallas_call(
        functools.partial(backward_kernel, kc, layout),
        in_specs=[smem] + [any_spec] + [vmem] * (1 + 2 * NY),
        out_specs=[any_spec] * len(layout),
        scratch_shapes=[
            pltpu.VMEM((48, 2 * kc, 2 * BS), jnp.bfloat16),
            pltpu.VMEM((16, kc, 4096), jnp.float32),
            pltpu.VMEM(blocks.shape, jnp.float32),
            pltpu.SemaphoreType.DMA((sum(len(entries) for _, entries in layout),)),
            pltpu.SemaphoreType.DMA((slots // GROUP,)),
        ],
        out_shape=[jax.ShapeDtypeStruct(shape, jnp.float32) for shape in shapes],
        compiler_params=pltpu.CompilerParams(vmem_limit_bytes=VMEM_BYTES),
        cost_estimate=cost(kc, slots),
    )(meta, blocks, alpha, *res, *img)


def after(*values):
    return lax.optimization_barrier(values)


def swap_core(value):
    return row_shift(value, 0, 0, 1)


def swap_z(value):
    return row_shift(value, 0, 1, 0)


def send_x(value, step):
    return row_shift(value, -step, 0, 0)


def shard_pieces(kc):
    h, q = kc // 2, kc // 4
    return (
        ((0, kc, (0, 0), 0),),
        ((0, kc, (0, 1), 0),),
        ((0, kc, (3, 0), 0),),
        ((0, kc, (1, 0), 0),),
        ((0, h, (3, 1), h), (h, h, (1, 1), h)),
        ((0, h, (2, 0), 0), (h, h, (3, 1), 0)),
        ((0, h, (2, 0), h), (h, h, (1, 1), 0)),
        ((0, h, (2, 1), h),),
        ((0, q, (2, 1), 0),),
        ((0, q, (2, 1), q),),
    )


def both_cores(kc):
    return tuple((dc, entries) for dc in range(NCORE) for entries in shard_pieces(kc))


def gather_panel(own):
    kc = own.shape[0]
    h, q = kc // 2, kc // 4
    z1, up1, down1 = swap_z(own), send_x(own, 1), send_x(own, -1)
    z1, up1, down1 = after(z1, up1, down1)
    z2 = swap_z(jnp.concatenate([up1[h:], down1[h:]]))
    up2 = send_x(jnp.concatenate([up1[:h], z1[:h]]), 1)
    down2 = send_x(jnp.concatenate([down1[h:], z1[:h]]), -1)
    z2, up2, down2 = after(z2, up2, down2)
    z3 = swap_z(down2[:h])
    up3, down3 = send_x(up2[h : h + q], 1), send_x(down2[h + q :], -1)
    pieces = [own, z1, up1, down1, z2, up2, down2, z3, up3, down3]
    return pieces + [swap_core(piece) for piece in pieces]


def scatter_cells(parts, kc):
    h, q = kc // 2, kc // 4
    count = len(parts) // 2
    terms = [mine + swap_core(sent) for mine, sent in zip(parts[:count], parts[count:])]
    own, z1, up1, down1, z2, up2, down2, z3, up3, down3 = terms
    z3, up3, down3 = swap_z(z3), send_x(up3, -1), send_x(down3, 1)
    z2, z3 = after(z2, z3)
    z2 = swap_z(z2)
    up2 = send_x(jnp.concatenate([up2[:h], up2[h : h + q] + up3, up2[h + q :]]), -1)
    down2 = send_x(jnp.concatenate([down2[:h] + z3, down2[h : h + q], down2[h + q :] + down3]), 1)
    z1 = swap_z(jnp.concatenate([z1[:h] + up2[h:] + down2[h:], z1[h:]]))
    up1 = send_x(up1 + jnp.concatenate([up2[:h], z2[:h]]), -1)
    down1 = send_x(down1 + jnp.concatenate([jnp.zeros_like(z2[:h]), down2[:h] + z2[h:]]), 1)
    return own + z1 + up1 + down1


def gather_rays(pair):
    return [pair] + [col_shift(pair, 0, dy) for dy in (1, 2, 3)]


def sum_rays(parts):
    got = [col_shift(parts[dy], 0, -dy) for dy in (1, 3, 2)]
    mine = parts[0] + got[0] + got[1] + got[2]
    return mine + col_shift(mine, 1, 0)[::-1]


def per_device(solution, residual, direction, gradient, blocks, block_rows, block_cols, counts):
    tile_blocks = blocks[0]
    width = direction.shape[1]
    kc = width // CHUNKS
    sol, res, dirn, grad = solution.T, residual.T, direction.T, gradient.T
    row_index, col_index = lax.axis_index("row"), lax.axis_index("col")
    head = [
        counts[0, 0],
        row_index // 4,
        (row_index // 2) % 2,
        row_index % 2,
        col_index // 4,
        col_index % 4,
    ]
    head = jnp.stack(head + [jnp.int32(0)] * (HEAD - len(head))).astype(jnp.int32)
    meta = jnp.concatenate([head, block_rows[0], block_cols[0]])
    layout = both_cores(kc)

    old_norms = jnp.sum(grad * grad, axis=1, keepdims=True)
    ride = jnp.concatenate([res, jnp.broadcast_to(old_norms, (width, BS))], axis=1)
    res_tile = gather_rays(jnp.stack([ride, col_shift(ride, 1, 0)]))
    old_norms = sum(jnp.sum(pair[:, :, -1], axis=0) for pair in res_tile)
    outputs = []
    for chunk in range(CHUNKS):
        span = slice(chunk * kc, (chunk + 1) * kc)
        s, r, d = sol[span], res[span], dirn[span]
        pieces = gather_panel(d)
        image_pair = sum_rays(forward(tile_blocks, meta, layout, pieces, kc))
        image = image_pair[0]
        image_tile = gather_rays(image_pair)
        norms = sum(jnp.sum(pair * pair, axis=(0, 2)) for pair in image_tile)
        norms = jnp.concatenate([old_norms[span], norms])
        norms = sum_over(jnp.pad(norms, (0, 128 - 2 * kc))[None], ("row",))[0]
        gamma, image_norms = norms[:kc], norms[kc : 2 * kc]
        alpha = (gamma / (image_norms + EPS))[:, None]
        cell_parts = backward(
            tile_blocks,
            meta,
            alpha,
            [pair[:, span] for pair in res_tile],
            image_tile,
            layout,
            kc,
        )
        new_gradient = scatter_cells(cell_parts, kc)
        new_norms = jnp.sum(new_gradient * new_gradient, axis=1)
        new_norms = jnp.pad(new_norms, (0, 128 - kc))[None]
        new_norms = sum_over(new_norms, ("row", "col"))[0, :kc]
        beta = (new_norms / gamma)[:, None]
        outputs.append((s + alpha * d, r - alpha * image, new_gradient + beta * d))
    return tuple(jnp.concatenate(parts, axis=0).T for parts in zip(*outputs))


def solution(mesh):
    placed = (
        P(("col", "row"), None),
        P(("row", "col"), None),
        P(("col", "row"), None),
        P(("col", "row"), None),
        P("row", "col", None, None),
        P("row", "col"),
        P("row", "col"),
        P("row", "col"),
    )
    return jax.shard_map(
        per_device,
        mesh=mesh,
        in_specs=placed,
        out_specs=(P(("col", "row"), None), P(("row", "col"), None), P(("col", "row"), None)),
        check_vma=False,
    )
```

time: 721 us -> 287 us (0.40)
  waiting for transfers between devices: 396 us -> 157 us
  blocking collectives: 130 us -> 9.32 us
  starting transfers between devices: 0.34 us -> 64.3 us
  other arithmetic: 74.1 us -> 16.2 us
  matrix products: 56 us -> 0 us
  local copies, waits for them, and re-layouts: 48.5 us -> 5.06 us
  Pallas kernels: 0 us -> 32.6 us
  between operations: 14.5 us -> 1.85 us
    reduce_scatter x2 -> x0, waiting for transfers between devices: 255 us -> none  [the longest x1 181 us: per_device(): lax.psum_scatter(cell_part, 'row', scatter_dimension=0, tiled=True)]
    ppermute x0 -> x49, waiting for transfers between devices: none -> 148 us  [the longest x38 106 us: row_shift(): return lax.ppermute(value, 'row', pairs)]
    all_gather x2 -> x0, waiting for transfers between devices: 141 us -> none  [the longest x1 95 us: per_device(): panel = lax.all_gather(direction, 'row', axis=0, tiled=True)]
    psum x2 -> x0, blocking collectives: 130 us -> none  [the longest x1 65.4 us: per_device(): gamma = lax.psum(jnp.sum(gradient * gradient, axis=0), ('row', 'col'))]
    scatter-add x2 -> x0, other arithmetic: 65.6 us -> none  [tile_apply(): return jax.ops.segment_sum(product, target_index, num_segments=target_count)]
    ppermute x0 -> x49, starting transfers between devices: none -> 56.2 us  [the longest x38 36.2 us: row_shift(): return lax.ppermute(value, 'row', pairs)]
    dot_general x2 -> x0, matrix products: 56 us -> none  [the longest x1 36.1 us: block_product(): jnp.einsum('bij,bjk->bik', tile_blocks, source_blocks, precision=lax.Prec...]
    pallas_call x0 -> x2, Pallas kernels: none -> 32.6 us  [the longest x1 16.4 us: backward(): pl.pallas_call(functools.partial(backward_kernel, kc, layout), in_specs=[...]
  transfers between devices with their start and end apart: 4 -> 50, of which waited for: 4 -> 23; matrix products, arithmetic and copies ran while one was open for 0% -> 6% of each run, Pallas kernels for 0% -> 0%
where the time goes in v2:
time: 287 us
  waiting for transfers between devices  157 us (55%)
  starting transfers between devices  64.3 us (22%)
  Pallas kernels  32.6 us (11%)
  other arithmetic  16.2 us (6%)
  blocking collectives  9.32 us (3%)
  local copies, waits for them, and re-layouts  5.06 us (2%)
    ppermute x38, waiting for transfers between devices, row_shift(): return lax.ppermute(value, 'row', pairs)  106 us
    ppermute x11, waiting for transfers between devices, col_shift(): return lax.ppermute(value, 'col', pairs)  42.6 us
    ppermute x38, starting transfers between devices, row_shift(): return lax.ppermute(value, 'row', pairs)  36.2 us
    ppermute x11, starting transfers between devices, col_shift(): return lax.ppermute(value, 'col', pairs)  20 us
    pallas_call x1, Pallas kernels, backward(): pl.pallas_call(functools.partial(backward_kernel, kc, layout), in_specs=[...  16.4 us
    pallas_call x1, Pallas kernels, forward(): pl.pallas_call(functools.partial(forward_kernel, kc, places), in_specs=[s...  16.2 us
    all_to_all x1, blocking collectives, sum_over(): return jnp.sum(lax.all_to_all(sent, axes, 0, 0, tiled=True), axis=0)  9.32 us
    all_to_all x1, waiting for transfers between devices, sum_over(): return jnp.sum(lax.all_to_all(sent, axes, 0, 0, tiled=True), axis=0)  8.96 us
  transfers between devices with their start and end apart: 50, of which 23 were waited for; matrix products, arithmetic and copies ran while one was open for 6% of the time, Pallas kernels for 0%

profile of v2, /device:TPU:1, one launch (start us, length us, event | category | flops | bytes accessed | tf_op | source)
XLA Modules:
  0.0 286.7 jit_solution(3999512208391218401)
XLA Ops:
  0.6 2.5 collective-permute-start.4
  5.9 20.4 %collective-permute-done.4.refs_1_ = f32[64,4096]{1,0:T(8,128)S(1)} collective-permute-done((f32[64,4096]{1,0:T(8,128)}, f32[64,4096]{1,0:T(8,128)S(1)}, u32[]{:S(2)}, u32[]{:S(2)}) %collective-permute-start.4) | collective-permute-done | bytes 1048608 | tf_op jit(solution)/shard_map/ppermute | solution.py:36
  32.0 2.4 collective-permute-start.13
  34.4 17.4 %collective-permute-done.7.refs_4_ = f32[64,4096]{1,0:T(8,128)} collective-permute-done((f32[64,4096]{1,0:T(8,128)S(1)}, f32[64,4096]{1,0:T(8,128)}, u32[]{:S(2)}, u32[]{:S(2)}) %collective-permute-start.7) | collective-permute-done | bytes 1048608 | tf_op jit(solution)/shard_map/ppermute | solution.py:36
  51.8 2.8 collective-permute-start.15
  57.5 2.5 collective-permute-start.12
  62.0 3.3 %collective-permute-done.12.refs_9_ = f32[16,4096]{1,0:T(8,128)S(1)} collective-permute-done((f32[16,4096]{1,0:T(8,128)S(1)}, f32[16,4096]{1,0:T(8,128)S(1)}, u32[]{:S(2)}, u32[]{:S(2)}) %collective-permute-start.12) | collective-permute-done | bytes 262176 | tf_op jit(solution)/shard_map/ppermute | solution.py:36
  65.6 8.6 %collective-permute-done.11.refs_8_ = f32[16,4096]{1,0:T(8,128)S(1)} collective-permute-done((f32[16,4096]{1,0:T(8,128)S(1)}, f32[16,4096]{1,0:T(8,128)S(1)}, u32[]{:S(2)}, u32[]{:S(2)}) %collective-permute-start.11) | collective-permute-done | bytes 262176 | tf_op jit(solution)/shard_map/ppermute | solution.py:36
  81.8 16.2 %shard_map.103 = (f32[2,64,768]{2,1,0:T(8,128)}, f32[2,64,768]{2,1,0:T(8,128)}, f32[2,64,768]{2,1,0:T(8,128)}, f32[2,64,768]{2,1,0:T(8,128)}) custom-call(s32[520]{0:T(1024)} %concatenate.34.meta_ref, f32[256,128,128]{2,1,0:T(8,128)} %bitcast.39, f32[64,4096]{1,0:T(8,128)} %bitcast.45, f32[64,4096]{1,0:T(8,128)} %copy-done.5, f32[64,4096]{1,0:T(8,128)} %copy-done.1, ...), custom_call_target="tpu_custom_call" | custom-call | flops 1610612736 | bytes 50331648 | tf_op jit(solution)/shard_map/pallas_call | solution.py:208
  98.0 2.7 collective-permute-start.24
  101.6 4.8 %collective-permute-start = (f32[64,896]{1,0:T(8,128)S(1)}, f32[64,896]{1,0:T(8,128)S(1)}, u32[]{:S(2)}, u32[]{:S(2)}) collective-permute-start(f32[64,896]{1,0:T(8,128)S(1)} %get-tuple-element.86), channel_id=1, source_target_pairs={{4,0},{5,1},{6,2},{7,3},{0,4},{1,5},{2,6},{3,7},{12,8},{13,9},{14,... | collective-permute-start | bytes 688136 | tf_op jit(solution)/shard_map/ppermute | solution.py:41
  106.4 5.8 %collective-permute-done = f32[64,896]{1,0:T(8,128)S(1)} collective-permute-done((f32[64,896]{1,0:T(8,128)S(1)}, f32[64,896]{1,0:T(8,128)S(1)}, u32[]{:S(2)}, u32[]{:S(2)}) %collective-permute-start) | collective-permute-done | bytes 229408 | tf_op jit(solution)/shard_map/ppermute | solution.py:41
  112.3 7.1 %collective-permute-done.25 = f32[2,64,768]{2,1,0:T(8,128)S(1)} collective-permute-done((f32[2,64,768]{2,1,0:T(8,128)}, f32[2,64,768]{2,1,0:T(8,128)S(1)}, u32[]{:S(2)}, u32[]{:S(2)}) %collective-permute-start.25) | collective-permute-done | bytes 393248 | tf_op jit(solution)/shard_map/ppermute | solution.py:41
  120.6 3.3 %collective-permute-start.26 = (f32[2,64,768]{2,1,0:T(8,128)S(1)}, f32[2,64,768]{2,1,0:T(8,128)S(1)}, u32[]{:S(2)}, u32[]{:S(2)}) collective-permute-start(f32[2,64,768]{2,1,0:T(8,128)S(1)} %add_add_fusion.1), channel_id=1, source_target_pairs={{4,0},{5,1},{6,2},{7,3},{0,4},{1,5},{2,6},{3,7},{12,8},{13,9},{14,... | collective-permute-start | bytes 1179656 | tf_op jit(solution)/shard_map/ppermute | solution.py:41
  126.4 3.1 %collective-permute-done.3.refs_3_ = f32[2,64,896]{2,1,0:T(8,128)S(1)} collective-permute-done((f32[2,64,896]{2,1,0:T(8,128)S(1)}, f32[2,64,896]{2,1,0:T(8,128)S(1)}, u32[]{:S(2)}, u32[]{:S(2)}) %collective-permute-start.3) | collective-permute-done | bytes 458784 | tf_op jit(solution)/shard_map/ppermute | solution.py:41
  129.7 2.5 collective-permute-done.26
  133.5 4.5 %collective-permute-done.2.refs_2_ = f32[2,64,896]{2,1,0:T(8,128)S(1)} collective-permute-done((f32[2,64,896]{2,1,0:T(8,128)S(1)}, f32[2,64,896]{2,1,0:T(8,128)S(1)}, u32[]{:S(2)}, u32[]{:S(2)}) %collective-permute-start.2) | collective-permute-done | bytes 458784 | tf_op jit(solution)/shard_map/ppermute | solution.py:41
  139.8 6.3 %collective-permute-done.1.refs_1_ = f32[2,64,896]{2,1,0:T(8,128)S(1)} collective-permute-done((f32[2,64,896]{2,1,0:T(8,128)S(1)}, f32[2,64,896]{2,1,0:T(8,128)S(1)}, u32[]{:S(2)}, u32[]{:S(2)}) %collective-permute-start.1) | collective-permute-done | bytes 458784 | tf_op jit(solution)/shard_map/ppermute | solution.py:41
  146.3 3.2 %collective-permute-start.27 = (f32[2,64,768]{2,1,0:T(8,128)S(1)}, f32[2,64,768]{2,1,0:T(8,128)S(1)}, u32[]{:S(2)}, u32[]{:S(2)}) collective-permute-start(f32[2,64,768]{2,1,0:T(8,128)S(1)} %get-tuple-element.70.refs_4_), channel_id=1, source_target_pairs={{1,0},{2,1},{3,2},{0,3},{5,4},{6,5},{7,6},{4,7},{9,8},{10,9},{11,1... | collective-permute-start | bytes 1179656 | tf_op jit(solution)/shard_map/ppermute | solution.py:41
  149.7 5.5 %collective-permute-done.28.refs_6_ = f32[2,64,768]{2,1,0:T(8,128)S(1)} collective-permute-done((f32[2,64,768]{2,1,0:T(8,128)S(1)}, f32[2,64,768]{2,1,0:T(8,128)S(1)}, u32[]{:S(2)}, u32[]{:S(2)}) %collective-permute-start.28) | collective-permute-done | bytes 393248 | tf_op jit(solution)/shard_map/ppermute | solution.py:41
  155.3 7.8 %collective-permute-done.27.refs_5_ = f32[2,64,768]{2,1,0:T(8,128)S(1)} collective-permute-done((f32[2,64,768]{2,1,0:T(8,128)S(1)}, f32[2,64,768]{2,1,0:T(8,128)S(1)}, u32[]{:S(2)}, u32[]{:S(2)}) %collective-permute-start.27) | collective-permute-done | bytes 393248 | tf_op jit(solution)/shard_map/ppermute | solution.py:41
  163.3 9.3 %all_to_all.10 = f32[16,1,128]{2,1,0:T(1,128)S(1)} all-to-all(f32[16,1,128]{2,1,0:T(1,128)S(1)} %broadcast_in_dim.7), channel_id=1, replica_groups=mesh['row'=16,'col'=8] {'row'}, dimensions={0} | all-to-all | bytes 16384 | tf_op jit(solution)/shard_map/all_to_all | solution.py:47
  173.4 16.4 %shard_map.104 = (f32[64,4096]{1,0:T(8,128)}, f32[64,4096]{1,0:T(8,128)}, f32[64,4096]{1,0:T(8,128)}, f32[64,4096]{1,0:T(8,128)}, f32[64,4096]{1,0:T(8,128)}, /*...) custom-call(s32[520]{0:T(1024)} %concatenate.34.meta_ref, ...), custom_call_target="tpu_custom_call" | custom-call | flops 1610612736 | bytes 50331648 | tf_op jit(solution)/shard_map/pallas_call | solution.py:230
  191.0 3.0 %collective-permute-done.33 = f32[16,4096]{1,0:T(8,128)S(1)} collective-permute-done((f32[16,4096]{1,0:T(8,128)}, f32[16,4096]{1,0:T(8,128)S(1)}, u32[]{:S(2)}, u32[]{:S(2)}) %collective-permute-start.33) | collective-permute-done | bytes 262176 | tf_op jit(solution)/shard_map/ppermute | solution.py:36
  203.0 2.6 collective-permute-start.35
  207.1 8.2 %collective-permute-done.39 = f32[32,4096]{1,0:T(8,128)S(1)} collective-permute-done((f32[32,4096]{1,0:T(8,128)S(1)}, f32[32,4096]{1,0:T(8,128)S(1)}, u32[]{:S(2)}, u32[]{:S(2)}) %collective-permute-start.39) | collective-permute-done | bytes 524320 | tf_op jit(solution)/shard_map/ppermute | solution.py:36
  220.4 6.8 %collective-permute-done.35 = f32[64,4096]{1,0:T(8,128)S(1)} collective-permute-done((f32[64,4096]{1,0:T(8,128)S(1)}, f32[64,4096]{1,0:T(8,128)S(1)}, u32[]{:S(2)}, u32[]{:S(2)}) %collective-permute-start.35) | collective-permute-done | bytes 1048608 | tf_op jit(solution)/shard_map/ppermute | solution.py:36
  229.0 11.9 %collective-permute-done.42 = f32[64,4096]{1,0:T(8,128)S(1)} collective-permute-done((f32[64,4096]{1,0:T(8,128)S(1)}, f32[64,4096]{1,0:T(8,128)S(1)}, u32[]{:S(2)}, u32[]{:S(2)}) %collective-permute-start.42) | collective-permute-done | bytes 1048608 | tf_op jit(solution)/shard_map/ppermute | solution.py:36
  245.3 18.0 %collective-permute-done.43 = f32[64,4096]{1,0:T(8,128)S(1)} collective-permute-done((f32[64,4096]{1,0:T(8,128)S(1)}, f32[64,4096]{1,0:T(8,128)S(1)}, u32[]{:S(2)}, u32[]{:S(2)}) %collective-permute-start.43) | collective-permute-done | bytes 1048608 | tf_op jit(solution)/shard_map/ppermute | solution.py:36
  264.2 2.4 collective-permute-done.48
  267.7 8.1 %all-to-all-start.1 = ((f32[128,1,128]{2,1,0:T(1,128)}), f32[128,1,128]{2,1,0:T(1,128)S(1)}, u32[]{:S(2)}, u32[]{:S(2)}) async-start(f32[128,1,128]{2,1,0:T(1,128)} %broadcast_in_dim.8), calls=%async_computation.1 | async-start | bytes 131072 | tf_op jit(solution)/shard_map/all_to_all | solution.py:47
  276.5 9.0 %all-to-all-done.1 = f32[128,1,128]{2,1,0:T(1,128)S(1)} async-done(((f32[128,1,128]{2,1,0:T(1,128)}), f32[128,1,128]{2,1,0:T(1,128)S(1)}, u32[]{:S(2)}, u32[]{:S(2)}) %all-to-all-start.1) | async-done | bytes 65568 | tf_op jit(solution)/shard_map/all_to_all | solution.py:47
  (186 shorter events, 56.4 us)
Async XLA Ops:
  0.6 25.6 %collective-permute-start.4 = (f32[64,4096]{1,0:T(8,128)}, f32[64,4096]{1,0:T(8,128)S(1)}, u32[]{:S(2)}, u32[]{:S(2)}) collective-permute-start(f32[64,4096]{1,0:T(8,128)} %bitcast.41), channel_id=1, source_target_pairs={{16,0},{24,8},{0,16},{8,24},{48,32},{56,40},{32,48},{40,56},{80,64... | collective-permute-start | bytes 3145736 | tf_op jit(solution)/shard_map/ppermute | solution.py:36
  3.2 25.1 %collective-permute-start.5 = (f32[64,4096]{1,0:T(8,128)}, f32[64,4096]{1,0:T(8,128)S(1)}, u32[]{:S(2)}, u32[]{:S(2)}) collective-permute-start(f32[64,4096]{1,0:T(8,128)} %bitcast.42), channel_id=1, source_target_pairs={{96,0},{104,8},{112,16},{120,24},{0,32},{8,40},{16,48},{24,56},{32... | collective-permute-start | bytes 3145736 | tf_op jit(solution)/shard_map/ppermute | solution.py:36
  4.4 23.9 %collective-permute-start.6 = (f32[64,4096]{1,0:T(8,128)}, f32[64,4096]{1,0:T(8,128)S(1)}, u32[]{:S(2)}, u32[]{:S(2)}) collective-permute-start(f32[64,4096]{1,0:T(8,128)} %bitcast.43), channel_id=1, source_target_pairs={{32,0},{40,8},{48,16},{56,24},{64,32},{72,40},{80,48},{88,56},{96,... | collective-permute-start | bytes 3145736 | tf_op jit(solution)/shard_map/ppermute | solution.py:36
  28.8 23.0 %collective-permute-start.7 = (f32[64,4096]{1,0:T(8,128)S(1)}, f32[64,4096]{1,0:T(8,128)}, u32[]{:S(2)}, u32[]{:S(2)}) collective-permute-start(f32[64,4096]{1,0:T(8,128)S(1)} %get-tuple-element.83), channel_id=1, source_target_pairs={{16,0},{24,8},{0,16},{8,24},{48,32},{56,40},{32,48},{40,56},{80,64... | collective-permute-start | bytes 3145736 | tf_op jit(solution)/shard_map/ppermute | solution.py:36
  29.3 25.3 %collective-permute-start.8 = (f32[64,4096]{1,0:T(8,128)S(1)}, f32[64,4096]{1,0:T(8,128)}, u32[]{:S(2)}, u32[]{:S(2)}) collective-permute-start(f32[64,4096]{1,0:T(8,128)S(1)} %get-tuple-element.84), channel_id=1, source_target_pairs={{96,0},{104,8},{112,16},{120,24},{0,32},{8,40},{16,48},{24,56},{32... | collective-permute-start | bytes 3145736 | tf_op jit(solution)/shard_map/ppermute | solution.py:36
  30.2 26.0 %collective-permute-start.9 = (f32[64,4096]{1,0:T(8,128)S(1)}, f32[64,4096]{1,0:T(8,128)S(1)}, u32[]{:S(2)}, u32[]{:S(2)}) collective-permute-start(f32[64,4096]{1,0:T(8,128)S(1)} %get-tuple-element.82), channel_id=1, source_target_pairs={{32,0},{40,8},{48,16},{56,24},{64,32},{72,40},{80,48},{88,56},{96,... | collective-permute-start | bytes 3145736 | tf_op jit(solution)/shard_map/ppermute | solution.py:36
  32.0 24.4 %collective-permute-start.13 = (f32[64,4096]{1,0:T(8,128)}, f32[64,4096]{1,0:T(8,128)S(1)}, u32[]{:S(2)}, u32[]{:S(2)}) collective-permute-start(f32[64,4096]{1,0:T(8,128)} %bitcast.44), channel_id=1, source_target_pairs={{8,0},{0,8},{24,16},{16,24},{40,32},{32,40},{56,48},{48,56},{72,64... | collective-permute-start | bytes 3145736 | tf_op jit(solution)/shard_map/ppermute | solution.py:36
  34.4 23.2 %collective-permute-start.14 = (f32[64,4096]{1,0:T(8,128)S(1)}, f32[64,4096]{1,0:T(8,128)S(1)}, u32[]{:S(2)}, u32[]{:S(2)}) collective-permute-start(f32[64,4096]{1,0:T(8,128)S(1)} %collective-permute-done.4.refs_1_), channel_id=1, source_target_pairs={{8,0},{0,8},{24,16},{16,24},{40,32},{32,40},{56,48},{48,56},{72,64... | collective-permute-start | bytes 3145736 | tf_op jit(solution)/shard_map/ppermute | solution.py:36
  56.3 25.4 %collective-permute-start.19 = (f32[64,4096]{1,0:T(8,128)S(1)}, f32[64,4096]{1,0:T(8,128)}, u32[]{:S(2)}, u32[]{:S(2)}) collective-permute-start(f32[64,4096]{1,0:T(8,128)S(1)} %collective-permute-done.9.refs_6_), channel_id=1, source_target_pairs={{8,0},{0,8},{24,16},{16,24},{40,32},{32,40},{56,48},{48,56},{72,64... | collective-permute-start | bytes 3145736 | tf_op jit(solution)/shard_map/ppermute | solution.py:36
  56.4 19.6 %collective-permute-start.10 = (f32[32,4096]{1,0:T(8,128)S(1)}, f32[32,4096]{1,0:T(8,128)}, u32[]{:S(2)}, u32[]{:S(2)}) collective-permute-start(f32[32,4096]{1,0:T(8,128)S(1)} %slice.99), channel_id=1, source_target_pairs={{16,0},{24,8},{0,16},{8,24},{48,32},{56,40},{32,48},{40,56},{80,64... | collective-permute-start | bytes 1572872 | tf_op jit(solution)/shard_map/ppermute | solution.py:36
  60.0 21.7 %collective-permute-start.18 = (f32[64,4096]{1,0:T(8,128)}, f32[64,4096]{1,0:T(8,128)}, u32[]{:S(2)}, u32[]{:S(2)}) collective-permute-start(f32[64,4096]{1,0:T(8,128)} %collective-permute-done.8.refs_5_), channel_id=1, source_target_pairs={{8,0},{0,8},{24,16},{16,24},{40,32},{32,40},{56,48},{48,56},{72,64... | collective-permute-start | bytes 3145736 | tf_op jit(solution)/shard_map/ppermute | solution.py:36
  60.7 21.0 %collective-permute-start.17 = (f32[64,4096]{1,0:T(8,128)}, f32[64,4096]{1,0:T(8,128)}, u32[]{:S(2)}, u32[]{:S(2)}) collective-permute-start(f32[64,4096]{1,0:T(8,128)} %collective-permute-done.7.refs_4_), channel_id=1, source_target_pairs={{8,0},{0,8},{24,16},{16,24},{40,32},{32,40},{56,48},{48,56},{72,64... | collective-permute-start | bytes 3145736 | tf_op jit(solution)/shard_map/ppermute | solution.py:36
  98.0 14.4 %collective-permute-start.23 = (f32[2,64,768]{2,1,0:T(8,128)}, f32[2,64,768]{2,1,0:T(8,128)S(1)}, u32[]{:S(2)}, u32[]{:S(2)}) collective-permute-start(f32[2,64,768]{2,1,0:T(8,128)} %get-tuple-element.42), channel_id=1, source_target_pairs={{3,0},{0,1},{1,2},{2,3},{7,4},{4,5},{5,6},{6,7},{11,8},{8,9},{9,10... | collective-permute-start | bytes 1179656 | tf_op jit(solution)/shard_map/ppermute | solution.py:41
  100.7 18.8 %collective-permute-start.25 = (f32[2,64,768]{2,1,0:T(8,128)}, f32[2,64,768]{2,1,0:T(8,128)S(1)}, u32[]{:S(2)}, u32[]{:S(2)}) collective-permute-start(f32[2,64,768]{2,1,0:T(8,128)} %get-tuple-element.44), channel_id=1, source_target_pairs={{2,0},{3,1},{0,2},{1,3},{6,4},{7,5},{4,6},{5,7},{10,8},{11,9},{8,1... | collective-permute-start | bytes 1179656 | tf_op jit(solution)/shard_map/ppermute | solution.py:41
  112.2 17.2 %collective-permute-start.3 = (f32[2,64,896]{2,1,0:T(8,128)S(1)}, f32[2,64,896]{2,1,0:T(8,128)S(1)}, u32[]{:S(2)}, u32[]{:S(2)}) collective-permute-start(f32[2,64,896]{2,1,0:T(8,128)S(1)} %pad_maximum_fusion.6.refs_0_), channel_id=1, source_target_pairs={{3,0},{0,1},{1,2},{2,3},{7,4},{4,5},{5,6},{6,7},{11,8},{8,9},{9,10... | collective-permute-start | bytes 1376264 | tf_op jit(solution)/shard_map/ppermute | solution.py:41
  125.3 20.8 %collective-permute-start.1 = (f32[2,64,896]{2,1,0:T(8,128)S(1)}, f32[2,64,896]{2,1,0:T(8,128)S(1)}, u32[]{:S(2)}, u32[]{:S(2)}) collective-permute-start(f32[2,64,896]{2,1,0:T(8,128)S(1)} %pad_maximum_fusion.6.refs_0_), channel_id=1, source_target_pairs={{1,0},{2,1},{3,2},{0,3},{5,4},{6,5},{7,6},{4,7},{9,8},{10,9},{11,1... | collective-permute-start | bytes 1376264 | tf_op jit(solution)/shard_map/ppermute | solution.py:41
  132.3 17.2 %collective-permute-start.29 = (f32[2,64,768]{2,1,0:T(8,128)S(1)}, f32[2,64,768]{2,1,0:T(8,128)S(1)}, u32[]{:S(2)}, u32[]{:S(2)}) collective-permute-start(f32[2,64,768]{2,1,0:T(8,128)S(1)} %get-tuple-element.70.refs_4_), channel_id=1, source_target_pairs={{3,0},{0,1},{1,2},{2,3},{7,4},{4,5},{5,6},{6,7},{11,8},{8,9},{9,10... | collective-permute-start | bytes 1179656 | tf_op jit(solution)/shard_map/ppermute | solution.py:41
  138.2 16.9 %collective-permute-start.28 = (f32[2,64,768]{2,1,0:T(8,128)S(1)}, f32[2,64,768]{2,1,0:T(8,128)S(1)}, u32[]{:S(2)}, u32[]{:S(2)}) collective-permute-start(f32[2,64,768]{2,1,0:T(8,128)S(1)} %get-tuple-element.70.refs_4_), channel_id=1, source_target_pairs={{2,0},{3,1},{0,2},{1,3},{6,4},{7,5},{4,6},{5,7},{10,8},{11,9},{8,1... | collective-permute-start | bytes 1179656 | tf_op jit(solution)/shard_map/ppermute | solution.py:41
  146.3 16.7 %collective-permute-start.27 = (f32[2,64,768]{2,1,0:T(8,128)S(1)}, f32[2,64,768]{2,1,0:T(8,128)S(1)}, u32[]{:S(2)}, u32[]{:S(2)}) collective-permute-start(f32[2,64,768]{2,1,0:T(8,128)S(1)} %get-tuple-element.70.refs_4_), channel_id=1, source_target_pairs={{1,0},{2,1},{3,2},{0,3},{5,4},{6,5},{7,6},{4,7},{9,8},{10,9},{11,1... | collective-permute-start | bytes 1179656 | tf_op jit(solution)/shard_map/ppermute | solution.py:41
  196.4 23.8 %collective-permute-start.31 = (f32[64,4096]{1,0:T(8,128)}, f32[64,4096]{1,0:T(8,128)S(1)}, u32[]{:S(2)}, u32[]{:S(2)}) collective-permute-start(f32[64,4096]{1,0:T(8,128)} %get-tuple-element.48), channel_id=1, source_target_pairs={{8,0},{0,8},{24,16},{16,24},{40,32},{32,40},{56,48},{48,56},{72,64... | collective-permute-start | bytes 3145736 | tf_op jit(solution)/shard_map/ppermute | solution.py:36
  197.9 17.4 %collective-permute-start.36 = (f32[64,4096]{1,0:T(8,128)}, f32[64,4096]{1,0:T(8,128)S(1)}, u32[]{:S(2)}, u32[]{:S(2)}) collective-permute-start(f32[64,4096]{1,0:T(8,128)} %get-tuple-element.54), channel_id=1, source_target_pairs={{8,0},{0,8},{24,16},{16,24},{40,32},{32,40},{56,48},{48,56},{72,64... | collective-permute-start | bytes 3145736 | tf_op jit(solution)/shard_map/ppermute | solution.py:36
  199.5 17.2 %collective-permute-start.41 = (f32[16,4096]{1,0:T(8,128)S(1)}, f32[16,4096]{1,0:T(8,128)S(1)}, u32[]{:S(2)}, u32[]{:S(2)}) collective-permute-start(f32[16,4096]{1,0:T(8,128)S(1)} %add.159), channel_id=1, source_target_pairs={{96,0},{104,8},{112,16},{120,24},{0,32},{8,40},{16,48},{24,56},{32... | collective-permute-start | bytes 786440 | tf_op jit(solution)/shard_map/ppermute | solution.py:36
  203.0 24.1 %collective-permute-start.35 = (f32[64,4096]{1,0:T(8,128)S(1)}, f32[64,4096]{1,0:T(8,128)S(1)}, u32[]{:S(2)}, u32[]{:S(2)}) collective-permute-start(f32[64,4096]{1,0:T(8,128)S(1)} %pad_maximum_fusion.3), channel_id=1, source_target_pairs={{32,0},{40,8},{48,16},{56,24},{64,32},{72,40},{80,48},{88,56},{96,... | collective-permute-start | bytes 3145736 | tf_op jit(solution)/shard_map/ppermute | solution.py:36
  216.9 24.1 %collective-permute-start.42 = (f32[64,4096]{1,0:T(8,128)S(1)}, f32[64,4096]{1,0:T(8,128)S(1)}, u32[]{:S(2)}, u32[]{:S(2)}) collective-permute-start(f32[64,4096]{1,0:T(8,128)S(1)} %pad_maximum_fusion.4), channel_id=1, source_target_pairs={{96,0},{104,8},{112,16},{120,24},{0,32},{8,40},{16,48},{24,56},{32... | collective-permute-start | bytes 3145736 | tf_op jit(solution)/shard_map/ppermute | solution.py:36
  217.8 23.2 %collective-permute-start.45 = (f32[64,4096]{1,0:T(8,128)S(1)}, f32[64,4096]{1,0:T(8,128)S(1)}, u32[]{:S(2)}, u32[]{:S(2)}) collective-permute-start(f32[64,4096]{1,0:T(8,128)S(1)} %add.156), channel_id=1, source_target_pairs={{16,0},{24,8},{0,16},{8,24},{48,32},{56,40},{32,48},{40,56},{80,64... | collective-permute-start | bytes 3145736 | tf_op jit(solution)/shard_map/ppermute | solution.py:36
  218.1 24.0 %collective-permute-start.44 = (f32[64,4096]{1,0:T(8,128)S(1)}, f32[64,4096]{1,0:T(8,128)S(1)}, u32[]{:S(2)}, u32[]{:S(2)}) collective-permute-start(f32[64,4096]{1,0:T(8,128)S(1)} %copy-done.29), channel_id=1, source_target_pairs={{8,0},{0,8},{24,16},{16,24},{40,32},{32,40},{56,48},{48,56},{72,64... | collective-permute-start | bytes 3145736 | tf_op jit(solution)/shard_map/ppermute | solution.py:36
  220.2 23.5 %collective-permute-start.47 = (f32[64,4096]{1,0:T(8,128)S(1)}, f32[64,4096]{1,0:T(8,128)S(1)}, u32[]{:S(2)}, u32[]{:S(2)}) collective-permute-start(f32[64,4096]{1,0:T(8,128)S(1)} %copy-done.28), channel_id=1, source_target_pairs={{8,0},{0,8},{24,16},{16,24},{40,32},{32,40},{56,48},{48,56},{72,64... | collective-permute-start | bytes 3145736 | tf_op jit(solution)/shard_map/ppermute | solution.py:36
  227.2 18.1 %collective-permute-start.30 = (f32[64,4096]{1,0:T(8,128)S(1)}, f32[64,4096]{1,0:T(8,128)S(1)}, u32[]{:S(2)}, u32[]{:S(2)}) collective-permute-start(f32[64,4096]{1,0:T(8,128)S(1)} %copy-done.27), channel_id=1, source_target_pairs={{8,0},{0,8},{24,16},{16,24},{40,32},{32,40},{56,48},{48,56},{72,64... | collective-permute-start | bytes 3145736 | tf_op jit(solution)/shard_map/ppermute | solution.py:36
  241.4 21.9 %collective-permute-start.43 = (f32[64,4096]{1,0:T(8,128)S(1)}, f32[64,4096]{1,0:T(8,128)S(1)}, u32[]{:S(2)}, u32[]{:S(2)}) collective-permute-start(f32[64,4096]{1,0:T(8,128)S(1)} %pad_maximum_fusion.5), channel_id=1, source_target_pairs={{16,0},{24,8},{0,16},{8,24},{48,32},{56,40},{32,48},{40,56},{80,64... | collective-permute-start | bytes 3145736 | tf_op jit(solution)/shard_map/ppermute | solution.py:36
  242.2 22.0 %collective-permute-start.46 = (f32[64,4096]{1,0:T(8,128)S(1)}, f32[64,4096]{1,0:T(8,128)S(1)}, u32[]{:S(2)}, u32[]{:S(2)}) collective-permute-start(f32[64,4096]{1,0:T(8,128)S(1)} %maximum_add_fusion), channel_id=1, source_target_pairs={{32,0},{40,8},{48,16},{56,24},{64,32},{72,40},{80,48},{88,56},{96,... | collective-permute-start | bytes 3145736 | tf_op jit(solution)/shard_map/ppermute | solution.py:36
  243.8 22.8 %collective-permute-start.48 = (f32[64,4096]{1,0:T(8,128)S(1)}, f32[64,4096]{1,0:T(8,128)S(1)}, u32[]{:S(2)}, u32[]{:S(2)}) collective-permute-start(f32[64,4096]{1,0:T(8,128)S(1)} %pad_add_fusion), channel_id=1, source_target_pairs={{96,0},{104,8},{112,16},{120,24},{0,32},{8,40},{16,48},{24,56},{32... | collective-permute-start | bytes 3145736 | tf_op jit(solution)/shard_map/ppermute | solution.py:36
  267.7 17.8 %all-to-all-start.1 = ((f32[128,1,128]{2,1,0:T(1,128)}), f32[128,1,128]{2,1,0:T(1,128)S(1)}, u32[]{:S(2)}, u32[]{:S(2)}) async-start(f32[128,1,128]{2,1,0:T(1,128)} %broadcast_in_dim.8), calls=%async_computation.1 | async-start | bytes 131072 | tf_op jit(solution)/shard_map/all_to_all | solution.py:47
  (48 other events, 1036.4 us)

commit v3 on v2

--- a/solution.py
+++ b/solution.py
@@ -11,7 +11,7 @@
 BS = 128
 GROUP = 16
 HEAD = 8
-CHUNKS = 1
+YROWS = 40
 VMEM_BYTES = 56 * 1024 * 1024
 
 NX, NZ, NCORE = 4, 2, 2
@@ -76,8 +76,8 @@
 
 def forward_kernel(kc, places, meta_ref, blocks_ref, *refs):
     pieces = refs[: len(places)]
-    outs = refs[len(places) : len(places) + NY]
-    panel, acc, held, sems, block_sems = refs[len(places) + NY :]
+    outs = refs[len(places) : len(places) + NY + NZH]
+    panel, acc, held, sems, block_sems = refs[len(places) + NY + NZH :]
     count = meta_ref[0]
     x, z, c = meta_ref[1], meta_ref[2], meta_ref[3]
     groups = (count + GROUP - 1) // GROUP
@@ -126,7 +126,9 @@
             piece = ((zh + dz) % NZH) * 4 + (y + dy) % NY
             for t in range(per):
                 both = acc[piece * per + t].T
-                outs[dy][dz, :, t * BS : (t + 1) * BS] = both[:kc] + both[kc:]
+                both = both[:kc] + both[kc:]
+                outs[dy][dz, :, t * BS : (t + 1) * BS] = both[:YROWS]
+                outs[NY + dz][dy, :, t * BS : (t + 1) * BS] = both[YROWS:]
 
 
 def backward_kernel(kc, layout, meta_ref, blocks_ref, alpha_ref, *refs):
@@ -208,7 +210,7 @@
     return pl.pallas_call(
         functools.partial(forward_kernel, kc, places),
         in_specs=[smem] + [any_spec] * (1 + len(pieces)),
-        out_specs=[vmem] * NY,
+        out_specs=[vmem] * (NY + NZH),
         scratch_shapes=[
             pltpu.VMEM((16, kc, 4096), jnp.float32),
             pltpu.VMEM((48, BS, 2 * kc), jnp.float32),
@@ -216,7 +218,8 @@
             pltpu.SemaphoreType.DMA((copies,)),
             pltpu.SemaphoreType.DMA((slots // GROUP,)),
         ],
-        out_shape=[jax.ShapeDtypeStruct((NZH, kc, 6 * BS), jnp.float32)] * NY,
+        out_shape=[jax.ShapeDtypeStruct((NZH, YROWS, 6 * BS), jnp.float32)] * NY
+        + [jax.ShapeDtypeStruct((NY, kc - YROWS, 6 * BS), jnp.float32)] * NZH,
         compiler_params=pltpu.CompilerParams(vmem_limit_bytes=VMEM_BYTES),
         cost_estimate=cost(kc, slots),
     )(meta, blocks, *pieces)
@@ -280,51 +283,101 @@
     return tuple((dc, entries) for dc in range(NCORE) for entries in shard_pieces(kc))
 
 
-def gather_panel(own):
-    kc = own.shape[0]
-    h, q = kc // 2, kc // 4
-    z1, up1, down1 = swap_z(own), send_x(own, 1), send_x(own, -1)
-    z1, up1, down1 = after(z1, up1, down1)
+def by_step(kc):
+    pieces = shard_pieces(kc)
+    layout = []
+    for dc in range(NCORE):
+        for step in (pieces[7:], pieces[4:7], pieces[:4]):
+            entries, base = [], 0
+            for piece in step:
+                entries += [(base + first, size, owner, start) for first, size, owner, start in piece]
+                base += sum(entry[1] for entry in piece)
+            layout.append((dc, tuple(entries)))
+    return tuple(layout)
+
+
+def first_step(own):
+    return swap_z(own), send_x(own, 1), send_x(own, -1)
+
+
+def second_step(z1, up1, down1):
+    h = z1.shape[0] // 2
     z2 = swap_z(jnp.concatenate([up1[h:], down1[h:]]))
     up2 = send_x(jnp.concatenate([up1[:h], z1[:h]]), 1)
     down2 = send_x(jnp.concatenate([down1[h:], z1[:h]]), -1)
-    z2, up2, down2 = after(z2, up2, down2)
-    z3 = swap_z(down2[:h])
-    up3, down3 = send_x(up2[h : h + q], 1), send_x(down2[h + q :], -1)
-    pieces = [own, z1, up1, down1, z2, up2, down2, z3, up3, down3]
-    return pieces + [swap_core(piece) for piece in pieces]
-
-
-def scatter_cells(parts, kc):
-    h, q = kc // 2, kc // 4
+    return z2, up2, down2
+
+
+def third_step(z2, up2, down2):
+    h = z2.shape[0] // 2
+    q = h // 2
+    return swap_z(down2[:h]), send_x(up2[h : h + q], 1), send_x(down2[h + q :], -1)
+
+
+def with_core(pieces):
+    return list(pieces) + [swap_core(piece) for piece in pieces]
+
+
+def sum_cores(parts, kc):
     count = len(parts) // 2
-    terms = [mine + swap_core(sent) for mine, sent in zip(parts[:count], parts[count:])]
-    own, z1, up1, down1, z2, up2, down2, z3, up3, down3 = terms
-    z3, up3, down3 = swap_z(z3), send_x(up3, -1), send_x(down3, 1)
-    z2, z3 = after(z2, z3)
+    sent, got = list(parts[count:]), []
+    for number in range(count):
+        got.append(swap_core(sent[number]))
+        if number + 1 < count:
+            got[number], sent[number + 1] = after(got[number], sent[number + 1])
+    steps = [mine + other for mine, other in zip(parts[:count], got)]
+    pieces, sizes = [], [sum(entry[1] for entry in piece) for piece in shard_pieces(kc)]
+    for step, numbers in zip(steps, ((7, 8, 9), (4, 5, 6), (0, 1, 2, 3))):
+        base, cut = 0, []
+        for number in numbers:
+            cut.append(step[base : base + sizes[number]])
+            base += sizes[number]
+        pieces = cut + pieces
+    return pieces
+
+
+def third_back(z3, up3, down3):
+    return swap_z(z3), send_x(up3, -1), send_x(down3, 1)
+
+
+def second_back(z2, up2, down2, z3, up3, down3):
+    h = z2.shape[0] // 2
+    q = h // 2
     z2 = swap_z(z2)
     up2 = send_x(jnp.concatenate([up2[:h], up2[h : h + q] + up3, up2[h + q :]]), -1)
     down2 = send_x(jnp.concatenate([down2[:h] + z3, down2[h : h + q], down2[h + q :] + down3]), 1)
+    return z2, up2, down2
+
+
+def first_back(z1, up1, down1, z2, up2, down2):
+    h = z2.shape[0] // 2
     z1 = swap_z(jnp.concatenate([z1[:h] + up2[h:] + down2[h:], z1[h:]]))
     up1 = send_x(up1 + jnp.concatenate([up2[:h], z2[:h]]), -1)
-    down1 = send_x(down1 + jnp.concatenate([jnp.zeros_like(z2[:h]), down2[:h] + z2[h:]]), 1)
-    return own + z1 + up1 + down1
-
-
-def gather_rays(pair):
+    down1 = send_x(jnp.concatenate([down1[:h], down1[h:] + down2[:h] + z2[h:]]), 1)
+    return z1, up1, down1
+
+
+def sum_rays(parts, far):
+    first, near = parts[:NY], parts[NY] + far
+    got = [col_shift(first[dy], 0, -dy) for dy in (1, 3, 2)]
+    mine = first[0] + got[0] + got[1] + got[2]
+    got = [col_shift(near[dy], 0, -dy) for dy in (1, 3, 2)]
+    rest = near[0] + got[0] + got[1] + got[2]
+    return mine[0] + col_shift(mine[1], 1, 0), rest
+
+
+def spread_y(pair):
     return [pair] + [col_shift(pair, 0, dy) for dy in (1, 2, 3)]
 
 
-def sum_rays(parts):
-    got = [col_shift(parts[dy], 0, -dy) for dy in (1, 3, 2)]
-    mine = parts[0] + got[0] + got[1] + got[2]
-    return mine + col_shift(mine, 1, 0)[::-1]
+def pad_row(row):
+    return jnp.pad(row, (0, BS - row.shape[0]))[None]
 
 
 def per_device(solution, residual, direction, gradient, blocks, block_rows, block_cols, counts):
     tile_blocks = blocks[0]
     width = direction.shape[1]
-    kc = width // CHUNKS
+    kc = width
     sol, res, dirn, grad = solution.T, residual.T, direction.T, gradient.T
     row_index, col_index = lax.axis_index("row"), lax.axis_index("col")
     head = [
@@ -337,41 +390,48 @@
     ]
     head = jnp.stack(head + [jnp.int32(0)] * (HEAD - len(head))).astype(jnp.int32)
     meta = jnp.concatenate([head, block_rows[0], block_cols[0]])
-    layout = both_cores(kc)
-
-    old_norms = jnp.sum(grad * grad, axis=1, keepdims=True)
-    ride = jnp.concatenate([res, jnp.broadcast_to(old_norms, (width, BS))], axis=1)
-    res_tile = gather_rays(jnp.stack([ride, col_shift(ride, 1, 0)]))
-    old_norms = sum(jnp.sum(pair[:, :, -1], axis=0) for pair in res_tile)
-    outputs = []
-    for chunk in range(CHUNKS):
-        span = slice(chunk * kc, (chunk + 1) * kc)
-        s, r, d = sol[span], res[span], dirn[span]
-        pieces = gather_panel(d)
-        image_pair = sum_rays(forward(tile_blocks, meta, layout, pieces, kc))
-        image = image_pair[0]
-        image_tile = gather_rays(image_pair)
-        norms = sum(jnp.sum(pair * pair, axis=(0, 2)) for pair in image_tile)
-        norms = jnp.concatenate([old_norms[span], norms])
-        norms = sum_over(jnp.pad(norms, (0, 128 - 2 * kc))[None], ("row",))[0]
-        gamma, image_norms = norms[:kc], norms[kc : 2 * kc]
-        alpha = (gamma / (image_norms + EPS))[:, None]
-        cell_parts = backward(
-            tile_blocks,
-            meta,
-            alpha,
-            [pair[:, span] for pair in res_tile],
-            image_tile,
-            layout,
-            kc,
-        )
-        new_gradient = scatter_cells(cell_parts, kc)
-        new_norms = jnp.sum(new_gradient * new_gradient, axis=1)
-        new_norms = jnp.pad(new_norms, (0, 128 - kc))[None]
-        new_norms = sum_over(new_norms, ("row", "col"))[0, :kc]
-        beta = (new_norms / gamma)[:, None]
-        outputs.append((s + alpha * d, r - alpha * image, new_gradient + beta * d))
-    return tuple(jnp.concatenate(parts, axis=0).T for parts in zip(*outputs))
+
+    own = dirn
+    first = first_step(own)
+    first, meta = after(first, meta)
+    own_other, z1_other = swap_core(own), swap_core(first[0])
+    second = second_step(*first)
+    ride, z1_other = after(res, z1_other)
+    ride1, ride3 = col_shift(ride, 0, 1), col_shift(ride, 0, 3)
+    second, ride1, ride3 = after(second, ride1, ride3)
+    third = third_step(*second)
+    others = [swap_core(piece) for piece in (*first[1:], *second)]
+    ride, others = after(ride, others)
+    ride2 = col_shift(ride, 0, 2)
+    rides = jnp.stack([res, ride1, ride2, ride3])
+    third, rides = after(third, rides)
+    rides_z = col_shift(rides, 1, 0)
+    others += [swap_core(piece) for piece in third]
+    pieces = [own, *first, *second, *third, own_other, z1_other, *others]
+    parts = forward(tile_blocks, meta, both_cores(kc), pieces, kc)
+
+    far = col_shift(parts[NY + 1], 1, 0)
+    far, rides_z = after(far, rides_z)
+    rides = [jnp.stack([rides[dy], rides_z[dy]]) for dy in range(NY)]
+    image = jnp.concatenate(sum_rays(parts, far))
+    norms = jnp.concatenate([jnp.sum(grad * grad, axis=1), jnp.sum(image * image, axis=1)])
+    pair = jnp.stack([image, col_shift(image, 1, 0)])
+    norms, pair = after(norms, pair)
+    image_tile = spread_y(pair)
+    norms = sum_over(norms[None], ("row", "col"))[0]
+    gamma = norms[:width]
+    alpha = (gamma / (norms[width:] + EPS))[:, None]
+    back = backward(tile_blocks, meta, alpha, rides, image_tile, by_step(kc), kc)
+    own_back, z1, up1, down1, z2, up2, down2, z3, up3, down3 = sum_cores(back, kc)
+    third = third_back(z3, up3, down3)
+    z2, third = after(z2, third)
+    second = second_back(z2, up2, down2, *third)
+    z1, up1, down1 = first_back(z1, up1, down1, *second)
+    new_gradient = own_back + z1 + up1 + down1
+    new_norms = jnp.sum(new_gradient * new_gradient, axis=1)
+    new_norms = sum_over(pad_row(new_norms), ("row", "col"))[0, :width]
+    beta = (new_norms / gamma)[:, None]
+    return (sol + alpha * dirn).T, (res - alpha * image).T, (new_gradient + beta * dirn).T
 
 
 def solution(mesh):

time: 287 us -> 265 us (0.923)
  waiting for transfers between devices: 157 us -> 137 us
  starting transfers between devices: 64.3 us -> 82.1 us
  blocking collectives: 9.32 us -> 0 us
  Pallas kernels: 32.6 us -> 24.3 us
  other arithmetic: 16.2 us -> 11.6 us
    ppermute x11 -> x16, waiting for transfers between devices: 42.6 us -> 15.3 us  [col_shift(): return lax.ppermute(value, 'col', pairs)]
    all_to_all x1 -> x2, starting transfers between devices: 8.1 us -> 22.4 us  [sum_over(): return jnp.sum(lax.all_to_all(sent, axes, 0, 0, tiled=True), axis=0)]
    all_to_all x1 -> x0, blocking collectives: 9.32 us -> none  [sum_over(): return jnp.sum(lax.all_to_all(sent, axes, 0, 0, tiled=True), axis=0)]
    all_to_all x1 -> x2, waiting for transfers between devices: 8.96 us -> 17.7 us  [sum_over(): return jnp.sum(lax.all_to_all(sent, axes, 0, 0, tiled=True), axis=0)]
    ppermute x11 -> x16, starting transfers between devices: 20 us -> 28.1 us  [col_shift(): return lax.ppermute(value, 'col', pairs)]
    ppermute x38 -> x31, starting transfers between devices: 36.2 us -> 31.6 us  [row_shift(): return lax.ppermute(value, 'row', pairs)]
    add x16 -> x11, other arithmetic: 10.3 us -> 5.99 us  [the longest x3 2.31 us: sum_cores(): steps = [mine + other for mine, other in zip(parts[:count], got)]]
    pallas_call x1, Pallas kernels: 16.2 us -> 11.9 us  [forward(): pl.pallas_call(functools.partial(forward_kernel, kc, places), in_specs=[s...]
  transfers between devices with their start and end apart: 50 -> 49, of which waited for: 23 -> 28; matrix products, arithmetic and copies ran while one was open for 6% -> 5% of each run, Pallas kernels for 0% -> 4%
where the time goes in v3:
time: 265 us; the launch traced here: 264 us
  waiting for transfers between devices  137 us (52%)
  starting transfers between devices  82.1 us (31%)
  Pallas kernels  24.3 us (9%)
  other arithmetic  11.6 us (4%)
  local copies, waits for them, and re-layouts  7.55 us (3%)
    ppermute x31, waiting for transfers between devices, row_shift(): return lax.ppermute(value, 'row', pairs)  104 us
    ppermute x31, starting transfers between devices, row_shift(): return lax.ppermute(value, 'row', pairs)  31.6 us
    ppermute x16, starting transfers between devices, col_shift(): return lax.ppermute(value, 'col', pairs)  28.1 us
    all_to_all x2, starting transfers between devices, sum_over(): return jnp.sum(lax.all_to_all(sent, axes, 0, 0, tiled=True), axis=0)  22.4 us
    all_to_all x2, waiting for transfers between devices, sum_over(): return jnp.sum(lax.all_to_all(sent, axes, 0, 0, tiled=True), axis=0)  17.7 us
    ppermute x16, waiting for transfers between devices, col_shift(): return lax.ppermute(value, 'col', pairs)  15.3 us
    pallas_call x1, Pallas kernels, backward(): pl.pallas_call(functools.partial(backward_kernel, kc, layout), in_specs=[...  12.4 us
    pallas_call x1, Pallas kernels, forward(): pl.pallas_call(functools.partial(forward_kernel, kc, places), in_specs=[s...  11.9 us
  transfers between devices with their start and end apart: 49, of which 28 were waited for; matrix products, arithmetic and copies ran while one was open for 5% of the time, Pallas kernels for 4%

profile of v3, /device:TPU:1, one launch (start us, length us, event | category | flops | bytes accessed | tf_op | source)
XLA Modules:
  0.0 264.1 jit_solution(15857238957279344504)
XLA Ops:
  0.6 2.5 collective-permute-start
  7.9 18.4 %collective-permute-done.refs_1_ = f32[64,4096]{1,0:T(8,128)S(1)} collective-permute-done((f32[64,4096]{1,0:T(8,128)}, f32[64,4096]{1,0:T(8,128)S(1)}, u32[]{:S(2)}, u32[]{:S(2)}) %collective-permute-start) | collective-permute-done | bytes 1048608 | tf_op jit(solution)/shard_map/ppermute | solution.py:36
  26.3 2.1 collective-permute-done.1.refs_2_
  28.4 1.9 collective-permute-start.6
  33.7 2.8 %collective-permute-start.7 = (f32[64,768]{1,0:T(8,128)S(1)}, f32[64,768]{1,0:T(8,128)S(1)}, u32[]{:S(2)}, u32[]{:S(2)}) collective-permute-start(f32[64,768]{1,0:T(8,128)S(1)} %bitcast.63), channel_id=1, source_target_pairs={{1,0},{2,1},{3,2},{0,3},{5,4},{6,5},{7,6},{4,7},{9,8},{10,9},{11,1... | collective-permute-start | bytes 589832 | tf_op jit(solution)/shard_map/ppermute | solution.py:41
  36.5 19.1 %collective-permute-done.3.refs_4_ = f32[64,4096]{1,0:T(8,128)S(1)} collective-permute-done((f32[64,4096]{1,0:T(8,128)S(1)}, f32[64,4096]{1,0:T(8,128)S(1)}, u32[]{:S(2)}, u32[]{:S(2)}) %collective-permute-start.3) | collective-permute-done | bytes 1048608 | tf_op jit(solution)/shard_map/ppermute | solution.py:36
  64.8 2.9 %collective-permute-start.17 = (f32[64,768]{1,0:T(8,128)S(1)}, f32[64,768]{1,0:T(8,128)S(1)}, u32[]{:S(2)}, u32[]{:S(2)}) collective-permute-start(f32[64,768]{1,0:T(8,128)S(1)} %bitcast.65), channel_id=1, source_target_pairs={{2,0},{3,1},{0,2},{1,3},{6,4},{7,5},{4,6},{5,7},{10,8},{11,9},{8,1... | collective-permute-start | bytes 589832 | tf_op jit(solution)/shard_map/ppermute | solution.py:41
  70.5 1.8 collective-permute-done.17
  72.4 3.8 %collective-permute-done.10.refs_8_ = f32[16,4096]{1,0:T(8,128)S(1)} collective-permute-done((f32[16,4096]{1,0:T(8,128)S(1)}, f32[16,4096]{1,0:T(8,128)S(1)}, u32[]{:S(2)}, u32[]{:S(2)}) %collective-permute-start.10) | collective-permute-done | bytes 262176 | tf_op jit(solution)/shard_map/ppermute | solution.py:36
  78.5 3.4 %collective-permute-start.27 = (f32[4,64,768]{2,1,0:T(8,128)S(1)}, f32[4,64,768]{2,1,0:T(8,128)}, u32[]{:S(2)}, u32[]{:S(2)}) collective-permute-start(f32[4,64,768]{2,1,0:T(8,128)S(1)} %pad_maximum_fusion.7), channel_id=1, source_target_pairs={{4,0},{5,1},{6,2},{7,3},{0,4},{1,5},{2,6},{3,7},{12,8},{13,9},{14,... | collective-permute-start | bytes 2359304 | tf_op jit(solution)/shard_map/ppermute | solution.py:41
  83.6 11.9 %shard_map.103 = (f32[2,40,768]{2,1,0:T(8,128)}, f32[2,40,768]{2,1,0:T(8,128)}, f32[2,40,768]{2,1,0:T(8,128)}, f32[2,40,768]{2,1,0:T(8,128)}, f32[4,24,768]{2,1,0:T(8,128)}, /*index=5*/f32[4,24,768]{2,1,0:T(8,128)}) custom-call(s32[520]{0:T(1024)} %concatenate.33.meta_ref, f32[256,128,128]{2,1,0:T(8,128)} %bitcast.56, f32[64,4096]{1,0:T(8,128)} %bitcast.61, ...), custom_call_target="tpu_custom_call" | custom-call | flops 1610612736 | bytes 50331648 | tf_op jit(solution)/shard_map/pallas_call | solution.py:210
  100.0 3.7 %collective-permute-start.26 = (f32[4,24,768]{2,1,0:T(8,128)}, f32[4,24,768]{2,1,0:T(8,128)S(1)}, u32[]{:S(2)}, u32[]{:S(2)}) collective-permute-start(f32[4,24,768]{2,1,0:T(8,128)} %get-tuple-element.73), channel_id=1, source_target_pairs={{4,0},{5,1},{6,2},{7,3},{0,4},{1,5},{2,6},{3,7},{12,8},{13,9},{14,... | collective-permute-start | bytes 884744 | tf_op jit(solution)/shard_map/ppermute | solution.py:41
  105.0 3.1 %collective-permute-done.24 = f32[2,40,768]{2,1,0:T(8,128)S(1)} collective-permute-done((f32[2,40,768]{2,1,0:T(8,128)}, f32[2,40,768]{2,1,0:T(8,128)S(1)}, u32[]{:S(2)}, u32[]{:S(2)}) %collective-permute-start.24) | collective-permute-done | bytes 245792 | tf_op jit(solution)/shard_map/ppermute | solution.py:41
  109.1 4.8 %collective-permute-start.25 = (f32[40,768]{1,0:T(8,128)S(1)}, f32[40,768]{1,0:T(8,128)S(1)}, u32[]{:S(2)}, u32[]{:S(2)}) collective-permute-start(f32[40,768]{1,0:T(8,128)S(1)} %slice_bitcast_fusion), channel_id=1, source_target_pairs={{4,0},{5,1},{6,2},{7,3},{0,4},{1,5},{2,6},{3,7},{12,8},{13,9},{14,... | collective-permute-start | bytes 368648 | tf_op jit(solution)/shard_map/ppermute | solution.py:41
  115.0 1.9 collective-permute-start.28
  120.0 3.2 %collective-permute-done.30 = f32[24,768]{1,0:T(8,128)S(1)} collective-permute-done((f32[24,768]{1,0:T(8,128)S(1)}, f32[24,768]{1,0:T(8,128)S(1)}, u32[]{:S(2)}, u32[]{:S(2)}) %collective-permute-start.30) | collective-permute-done | bytes 73760 | tf_op jit(solution)/shard_map/ppermute | solution.py:41
  124.9 4.6 %collective-permute-done.31 = f32[64,768]{1,0:T(8,128)S(1)} collective-permute-done((f32[64,768]{1,0:T(8,128)S(1)}, f32[64,768]{1,0:T(8,128)S(1)}, u32[]{:S(2)}, u32[]{:S(2)}) %collective-permute-start.31) | collective-permute-done | bytes 196640 | tf_op jit(solution)/shard_map/ppermute | solution.py:41
  133.2 13.1 %all-to-all-start = ((f32[128,1,128]{2,1,0:T(1,128)}), f32[128,1,128]{2,1,0:T(1,128)S(1)}, u32[]{:S(2)}, u32[]{:S(2)}) async-start(f32[128,1,128]{2,1,0:T(1,128)} %broadcast_in_dim.4), calls=%async_computation | async-start | bytes 131072 | tf_op jit(solution)/shard_map/all_to_all | solution.py:47
  147.3 8.8 %all-to-all-done = f32[128,1,128]{2,1,0:T(1,128)S(1)} async-done(((f32[128,1,128]{2,1,0:T(1,128)}), f32[128,1,128]{2,1,0:T(1,128)S(1)}, u32[]{:S(2)}, u32[]{:S(2)}) %all-to-all-start) | async-done | bytes 65568 | tf_op jit(solution)/shard_map/all_to_all | solution.py:47
  157.7 12.4 %shard_map.104 = (f32[64,4096]{1,0:T(8,128)}, f32[192,4096]{1,0:T(8,128)}, f32[256,4096]{1,0:T(8,128)}, f32[64,4096]{1,0:T(8,128)}, f32[192,4096]{1,0:T(8,128)}, /*index=5*/f32[256,4096]{1,0:T(8,128)}) custom-call(s32[520]{0:T(1024)} %concatenate.33.meta_ref, f32[256,128,128]{2,1,0:T(8,128)} %bitcast.57, f32[64,1]{1,0:T(8,128)} %copy.14.alpha_ref, ...), custom_call_target="tpu_custom_call" | custom-call | flops 1610612736 | bytes 50331648 | tf_op jit(solution)/shard_map/pallas_call | solution.py:233
  170.9 2.5 collective-permute-done.35
  175.2 1.9 collective-permute-start.38
  177.1 2.2 collective-permute-done.36
  179.7 3.7 %collective-permute-start.39 = (f32[16,4096]{1,0:T(8,128)S(1)}, f32[16,4096]{1,0:T(8,128)S(1)}, u32[]{:S(2)}, u32[]{:S(2)}) collective-permute-start(f32[16,4096]{1,0:T(8,128)S(1)} %get-tuple-element.108), channel_id=1, source_target_pairs={{32,0},{40,8},{48,16},{56,24},{64,32},{72,40},{80,48},{88,56},{96,... | collective-permute-start | bytes 786440 | tf_op jit(solution)/shard_map/ppermute | solution.py:36
  183.8 5.5 %collective-permute-done.39 = f32[16,4096]{1,0:T(8,128)S(1)} collective-permute-done((f32[16,4096]{1,0:T(8,128)S(1)}, f32[16,4096]{1,0:T(8,128)S(1)}, u32[]{:S(2)}, u32[]{:S(2)}) %collective-permute-start.39) | collective-permute-done | bytes 262176 | tf_op jit(solution)/shard_map/ppermute | solution.py:36
  189.3 2.7 %collective-permute-done.40 = f32[16,4096]{1,0:T(8,128)S(1)} collective-permute-done((f32[16,4096]{1,0:T(8,128)S(1)}, f32[16,4096]{1,0:T(8,128)S(1)}, u32[]{:S(2)}, u32[]{:S(2)}) %collective-permute-start.40) | collective-permute-done | bytes 262176 | tf_op jit(solution)/shard_map/ppermute | solution.py:36
  195.7 20.1 %collective-permute-done.41 = f32[64,4096]{1,0:T(8,128)S(1)} collective-permute-done((f32[64,4096]{1,0:T(8,128)S(1)}, f32[64,4096]{1,0:T(8,128)S(1)}, u32[]{:S(2)}, u32[]{:S(2)}) %collective-permute-start.41) | collective-permute-done | bytes 1048608 | tf_op jit(solution)/shard_map/ppermute | solution.py:36
  215.8 1.7 collective-permute-done.42
  221.8 18.7 %collective-permute-done.43 = f32[64,4096]{1,0:T(8,128)S(1)} collective-permute-done((f32[64,4096]{1,0:T(8,128)S(1)}, f32[64,4096]{1,0:T(8,128)S(1)}, u32[]{:S(2)}, u32[]{:S(2)}) %collective-permute-start.43) | collective-permute-done | bytes 1048608 | tf_op jit(solution)/shard_map/ppermute | solution.py:36
  240.9 2.0 collective-permute-done.46
  243.9 9.3 %all-to-all-start.1 = ((f32[128,1,128]{2,1,0:T(1,128)}), f32[128,1,128]{2,1,0:T(1,128)S(1)}, u32[]{:S(2)}, u32[]{:S(2)}) async-start(f32[128,1,128]{2,1,0:T(1,128)} %broadcast_in_dim.5), calls=%async_computation.1 | async-start | bytes 131072 | tf_op jit(solution)/shard_map/all_to_all | solution.py:47
  254.0 9.0 %all-to-all-done.1 = f32[128,1,128]{2,1,0:T(1,128)S(1)} async-done(((f32[128,1,128]{2,1,0:T(1,128)}), f32[128,1,128]{2,1,0:T(1,128)S(1)}, u32[]{:S(2)}, u32[]{:S(2)}) %all-to-all-start.1) | async-done | bytes 65568 | tf_op jit(solution)/shard_map/all_to_all | solution.py:47
  (175 shorter events, 56.9 us)
Async XLA Ops:
  0.6 25.6 %collective-permute-start = (f32[64,4096]{1,0:T(8,128)}, f32[64,4096]{1,0:T(8,128)S(1)}, u32[]{:S(2)}, u32[]{:S(2)}) collective-permute-start(f32[64,4096]{1,0:T(8,128)} %bitcast.58), channel_id=1, source_target_pairs={{16,0},{24,8},{0,16},{8,24},{48,32},{56,40},{32,48},{40,56},{80,64... | collective-permute-start | bytes 3145736 | tf_op jit(solution)/shard_map/ppermute | solution.py:36
  3.2 25.1 %collective-permute-start.1 = (f32[64,4096]{1,0:T(8,128)}, f32[64,4096]{1,0:T(8,128)S(1)}, u32[]{:S(2)}, u32[]{:S(2)}) collective-permute-start(f32[64,4096]{1,0:T(8,128)} %bitcast.59), channel_id=1, source_target_pairs={{96,0},{104,8},{112,16},{120,24},{0,32},{8,40},{16,48},{24,56},{32... | collective-permute-start | bytes 3145736 | tf_op jit(solution)/shard_map/ppermute | solution.py:36
  4.4 23.9 %collective-permute-start.2 = (f32[64,4096]{1,0:T(8,128)}, f32[64,4096]{1,0:T(8,128)S(1)}, u32[]{:S(2)}, u32[]{:S(2)}) collective-permute-start(f32[64,4096]{1,0:T(8,128)} %bitcast.60), channel_id=1, source_target_pairs={{32,0},{40,8},{48,16},{56,24},{64,32},{72,40},{80,48},{88,56},{96,... | collective-permute-start | bytes 3145736 | tf_op jit(solution)/shard_map/ppermute | solution.py:36
  30.8 24.9 %collective-permute-start.3 = (f32[64,4096]{1,0:T(8,128)S(1)}, f32[64,4096]{1,0:T(8,128)S(1)}, u32[]{:S(2)}, u32[]{:S(2)}) collective-permute-start(f32[64,4096]{1,0:T(8,128)S(1)} %get-tuple-element.120), channel_id=1, source_target_pairs={{16,0},{24,8},{0,16},{8,24},{48,32},{56,40},{32,48},{40,56},{80,64... | collective-permute-start | bytes 3145736 | tf_op jit(solution)/shard_map/ppermute | solution.py:36
  31.0 25.7 %collective-permute-start.4 = (f32[64,4096]{1,0:T(8,128)S(1)}, f32[64,4096]{1,0:T(8,128)S(1)}, u32[]{:S(2)}, u32[]{:S(2)}) collective-permute-start(f32[64,4096]{1,0:T(8,128)S(1)} %get-tuple-element.121), channel_id=1, source_target_pairs={{96,0},{104,8},{112,16},{120,24},{0,32},{8,40},{16,48},{24,56},{32... | collective-permute-start | bytes 3145736 | tf_op jit(solution)/shard_map/ppermute | solution.py:36
  32.2 25.6 %collective-permute-start.5 = (f32[64,4096]{1,0:T(8,128)S(1)}, f32[64,4096]{1,0:T(8,128)S(1)}, u32[]{:S(2)}, u32[]{:S(2)}) collective-permute-start(f32[64,4096]{1,0:T(8,128)S(1)} %get-tuple-element.119), channel_id=1, source_target_pairs={{32,0},{40,8},{48,16},{56,24},{64,32},{72,40},{80,48},{88,56},{96,... | collective-permute-start | bytes 3145736 | tf_op jit(solution)/shard_map/ppermute | solution.py:36
  33.7 24.0 %collective-permute-start.7 = (f32[64,768]{1,0:T(8,128)S(1)}, f32[64,768]{1,0:T(8,128)S(1)}, u32[]{:S(2)}, u32[]{:S(2)}) collective-permute-start(f32[64,768]{1,0:T(8,128)S(1)} %bitcast.63), channel_id=1, source_target_pairs={{1,0},{2,1},{3,2},{0,3},{5,4},{6,5},{7,6},{4,7},{9,8},{10,9},{11,1... | collective-permute-start | bytes 589832 | tf_op jit(solution)/shard_map/ppermute | solution.py:41
  36.5 21.2 %collective-permute-start.8 = (f32[64,768]{1,0:T(8,128)S(1)}, f32[64,768]{1,0:T(8,128)S(1)}, u32[]{:S(2)}, u32[]{:S(2)}) collective-permute-start(f32[64,768]{1,0:T(8,128)S(1)} %bitcast.64), channel_id=1, source_target_pairs={{3,0},{0,1},{1,2},{2,3},{7,4},{4,5},{5,6},{6,7},{11,8},{8,9},{9,10... | collective-permute-start | bytes 589832 | tf_op jit(solution)/shard_map/ppermute | solution.py:41
  58.8 17.5 %collective-permute-start.9 = (f32[32,4096]{1,0:T(8,128)S(1)}, f32[32,4096]{1,0:T(8,128)S(1)}, u32[]{:S(2)}, u32[]{:S(2)}) collective-permute-start(f32[32,4096]{1,0:T(8,128)S(1)} %slice.160), channel_id=1, source_target_pairs={{16,0},{24,8},{0,16},{8,24},{48,32},{56,40},{32,48},{40,56},{80,64... | collective-permute-start | bytes 1572872 | tf_op jit(solution)/shard_map/ppermute | solution.py:36
  60.3 21.7 %collective-permute-start.18 = (f32[64,4096]{1,0:T(8,128)S(1)}, f32[64,4096]{1,0:T(8,128)S(1)}, u32[]{:S(2)}, u32[]{:S(2)}) collective-permute-start(f32[64,4096]{1,0:T(8,128)S(1)} %bitcast.62), channel_id=1, source_target_pairs={{8,0},{0,8},{24,16},{16,24},{40,32},{32,40},{56,48},{48,56},{72,64... | collective-permute-start | bytes 3145736 | tf_op jit(solution)/shard_map/ppermute | solution.py:36
  67.7 8.5 %collective-permute-start.10 = (f32[16,4096]{1,0:T(8,128)S(1)}, f32[16,4096]{1,0:T(8,128)S(1)}, u32[]{:S(2)}, u32[]{:S(2)}) collective-permute-start(f32[16,4096]{1,0:T(8,128)S(1)} %slice.161), channel_id=1, source_target_pairs={{96,0},{104,8},{112,16},{120,24},{0,32},{8,40},{16,48},{24,56},{32... | collective-permute-start | bytes 786440 | tf_op jit(solution)/shard_map/ppermute | solution.py:36
  78.5 35.4 %collective-permute-start.27 = (f32[4,64,768]{2,1,0:T(8,128)S(1)}, f32[4,64,768]{2,1,0:T(8,128)}, u32[]{:S(2)}, u32[]{:S(2)}) collective-permute-start(f32[4,64,768]{2,1,0:T(8,128)S(1)} %pad_maximum_fusion.7), channel_id=1, source_target_pairs={{4,0},{5,1},{6,2},{7,3},{0,4},{1,5},{2,6},{3,7},{12,8},{13,9},{14,... | collective-permute-start | bytes 2359304 | tf_op jit(solution)/shard_map/ppermute | solution.py:41
  95.5 9.5 %collective-permute-start.22 = (f32[2,40,768]{2,1,0:T(8,128)}, f32[2,40,768]{2,1,0:T(8,128)S(1)}, u32[]{:S(2)}, u32[]{:S(2)}) collective-permute-start(f32[2,40,768]{2,1,0:T(8,128)} %get-tuple-element.69), channel_id=1, source_target_pairs={{3,0},{0,1},{1,2},{2,3},{7,4},{4,5},{5,6},{6,7},{11,8},{8,9},{9,10... | collective-permute-start | bytes 737288 | tf_op jit(solution)/shard_map/ppermute | solution.py:41
  96.9 8.1 %collective-permute-start.23 = (f32[2,40,768]{2,1,0:T(8,128)}, f32[2,40,768]{2,1,0:T(8,128)S(1)}, u32[]{:S(2)}, u32[]{:S(2)}) collective-permute-start(f32[2,40,768]{2,1,0:T(8,128)} %get-tuple-element.70), channel_id=1, source_target_pairs={{1,0},{2,1},{3,2},{0,3},{5,4},{6,5},{7,6},{4,7},{9,8},{10,9},{11,1... | collective-permute-start | bytes 737288 | tf_op jit(solution)/shard_map/ppermute | solution.py:41
  98.2 9.9 %collective-permute-start.24 = (f32[2,40,768]{2,1,0:T(8,128)}, f32[2,40,768]{2,1,0:T(8,128)S(1)}, u32[]{:S(2)}, u32[]{:S(2)}) collective-permute-start(f32[2,40,768]{2,1,0:T(8,128)} %get-tuple-element.71), channel_id=1, source_target_pairs={{2,0},{3,1},{0,2},{1,3},{6,4},{7,5},{4,6},{5,7},{10,8},{11,9},{8,1... | collective-permute-start | bytes 737288 | tf_op jit(solution)/shard_map/ppermute | solution.py:41
  100.0 14.0 %collective-permute-start.26 = (f32[4,24,768]{2,1,0:T(8,128)}, f32[4,24,768]{2,1,0:T(8,128)S(1)}, u32[]{:S(2)}, u32[]{:S(2)}) collective-permute-start(f32[4,24,768]{2,1,0:T(8,128)} %get-tuple-element.73), channel_id=1, source_target_pairs={{4,0},{5,1},{6,2},{7,3},{0,4},{1,5},{2,6},{3,7},{12,8},{13,9},{14,... | collective-permute-start | bytes 884744 | tf_op jit(solution)/shard_map/ppermute | solution.py:41
  109.1 9.8 %collective-permute-start.25 = (f32[40,768]{1,0:T(8,128)S(1)}, f32[40,768]{1,0:T(8,128)S(1)}, u32[]{:S(2)}, u32[]{:S(2)}) collective-permute-start(f32[40,768]{1,0:T(8,128)S(1)} %slice_bitcast_fusion), channel_id=1, source_target_pairs={{4,0},{5,1},{6,2},{7,3},{0,4},{1,5},{2,6},{3,7},{12,8},{13,9},{14,... | collective-permute-start | bytes 368648 | tf_op jit(solution)/shard_map/ppermute | solution.py:41
  129.6 27.4 %collective-permute-start.32 = (f32[2,64,768]{2,1,0:T(8,128)S(1)}, f32[2,64,768]{2,1,0:T(8,128)S(1)}, u32[]{:S(2)}, u32[]{:S(2)}) collective-permute-start(f32[2,64,768]{2,1,0:T(8,128)S(1)} %pad_maximum_fusion.8.refs_4_), channel_id=1, source_target_pairs={{1,0},{2,1},{3,2},{0,3},{5,4},{6,5},{7,6},{4,7},{9,8},{10,9},{11,1... | collective-permute-start | bytes 1179656 | tf_op jit(solution)/shard_map/ppermute | solution.py:41
  130.9 26.0 %collective-permute-start.33 = (f32[2,64,768]{2,1,0:T(8,128)S(1)}, f32[2,64,768]{2,1,0:T(8,128)}, u32[]{:S(2)}, u32[]{:S(2)}) collective-permute-start(f32[2,64,768]{2,1,0:T(8,128)S(1)} %pad_maximum_fusion.8.refs_4_), channel_id=1, source_target_pairs={{2,0},{3,1},{0,2},{1,3},{6,4},{7,5},{4,6},{5,7},{10,8},{11,9},{8,1... | collective-permute-start | bytes 1179656 | tf_op jit(solution)/shard_map/ppermute | solution.py:41
  131.3 25.7 %collective-permute-start.34 = (f32[2,64,768]{2,1,0:T(8,128)S(1)}, f32[2,64,768]{2,1,0:T(8,128)}, u32[]{:S(2)}, u32[]{:S(2)}) collective-permute-start(f32[2,64,768]{2,1,0:T(8,128)S(1)} %pad_maximum_fusion.8.refs_4_), channel_id=1, source_target_pairs={{3,0},{0,1},{1,2},{2,3},{7,4},{4,5},{5,6},{6,7},{11,8},{8,9},{9,10... | collective-permute-start | bytes 1179656 | tf_op jit(solution)/shard_map/ppermute | solution.py:41
  133.2 22.9 %all-to-all-start = ((f32[128,1,128]{2,1,0:T(1,128)}), f32[128,1,128]{2,1,0:T(1,128)S(1)}, u32[]{:S(2)}, u32[]{:S(2)}) async-start(f32[128,1,128]{2,1,0:T(1,128)} %broadcast_in_dim.4), calls=%async_computation | async-start | bytes 131072 | tf_op jit(solution)/shard_map/all_to_all | solution.py:47
  175.2 16.8 %collective-permute-start.38 = (f32[32,4096]{1,0:T(8,128)S(1)}, f32[32,4096]{1,0:T(8,128)S(1)}, u32[]{:S(2)}, u32[]{:S(2)}) collective-permute-start(f32[32,4096]{1,0:T(8,128)S(1)} %slice.213), channel_id=1, source_target_pairs={{16,0},{24,8},{0,16},{8,24},{48,32},{56,40},{32,48},{40,56},{80,64... | collective-permute-start | bytes 1572872 | tf_op jit(solution)/shard_map/ppermute | solution.py:36
  179.3 15.7 %collective-permute-start.37 = (f32[256,4096]{1,0:T(8,128)}, f32[256,4096]{1,0:T(8,128)S(1)}, u32[]{:S(2)}, u32[]{:S(2)}) collective-permute-start(f32[256,4096]{1,0:T(8,128)} %get-tuple-element.84), channel_id=1, source_target_pairs={{8,0},{0,8},{24,16},{16,24},{40,32},{32,40},{56,48},{48,56},{72,64... | collective-permute-start | bytes 12582920 | tf_op jit(solution)/shard_map/ppermute | solution.py:36
  179.7 9.6 %collective-permute-start.39 = (f32[16,4096]{1,0:T(8,128)S(1)}, f32[16,4096]{1,0:T(8,128)S(1)}, u32[]{:S(2)}, u32[]{:S(2)}) collective-permute-start(f32[16,4096]{1,0:T(8,128)S(1)} %get-tuple-element.108), channel_id=1, source_target_pairs={{32,0},{40,8},{48,16},{56,24},{64,32},{72,40},{80,48},{88,56},{96,... | collective-permute-start | bytes 786440 | tf_op jit(solution)/shard_map/ppermute | solution.py:36
  183.4 8.7 %collective-permute-start.40 = (f32[16,4096]{1,0:T(8,128)S(1)}, f32[16,4096]{1,0:T(8,128)S(1)}, u32[]{:S(2)}, u32[]{:S(2)}) collective-permute-start(f32[16,4096]{1,0:T(8,128)S(1)} %get-tuple-element.107), channel_id=1, source_target_pairs={{96,0},{104,8},{112,16},{120,24},{0,32},{8,40},{16,48},{24,56},{32... | collective-permute-start | bytes 786440 | tf_op jit(solution)/shard_map/ppermute | solution.py:36
  192.3 23.4 %collective-permute-start.41 = (f32[64,4096]{1,0:T(8,128)S(1)}, f32[64,4096]{1,0:T(8,128)S(1)}, u32[]{:S(2)}, u32[]{:S(2)}) collective-permute-start(f32[64,4096]{1,0:T(8,128)S(1)} %pad_maximum_fusion.3), channel_id=1, source_target_pairs={{32,0},{40,8},{48,16},{56,24},{64,32},{72,40},{80,48},{88,56},{96,... | collective-permute-start | bytes 3145736 | tf_op jit(solution)/shard_map/ppermute | solution.py:36
  192.8 24.7 %collective-permute-start.42 = (f32[64,4096]{1,0:T(8,128)S(1)}, f32[64,4096]{1,0:T(8,128)S(1)}, u32[]{:S(2)}, u32[]{:S(2)}) collective-permute-start(f32[64,4096]{1,0:T(8,128)S(1)} %pad_maximum_fusion.4), channel_id=1, source_target_pairs={{96,0},{104,8},{112,16},{120,24},{0,32},{8,40},{16,48},{24,56},{32... | collective-permute-start | bytes 3145736 | tf_op jit(solution)/shard_map/ppermute | solution.py:36
  194.0 23.5 %collective-permute-start.44 = (f32[64,4096]{1,0:T(8,128)S(1)}, f32[64,4096]{1,0:T(8,128)S(1)}, u32[]{:S(2)}, u32[]{:S(2)}) collective-permute-start(f32[64,4096]{1,0:T(8,128)S(1)} %slice.212), channel_id=1, source_target_pairs={{16,0},{24,8},{0,16},{8,24},{48,32},{56,40},{32,48},{40,56},{80,64... | collective-permute-start | bytes 3145736 | tf_op jit(solution)/shard_map/ppermute | solution.py:36
  217.9 22.6 %collective-permute-start.43 = (f32[64,4096]{1,0:T(8,128)S(1)}, f32[64,4096]{1,0:T(8,128)S(1)}, u32[]{:S(2)}, u32[]{:S(2)}) collective-permute-start(f32[64,4096]{1,0:T(8,128)S(1)} %pad_maximum_fusion.5), channel_id=1, source_target_pairs={{16,0},{24,8},{0,16},{8,24},{48,32},{56,40},{32,48},{40,56},{80,64... | collective-permute-start | bytes 3145736 | tf_op jit(solution)/shard_map/ppermute | solution.py:36
  218.9 22.0 %collective-permute-start.45 = (f32[64,4096]{1,0:T(8,128)S(1)}, f32[64,4096]{1,0:T(8,128)S(1)}, u32[]{:S(2)}, u32[]{:S(2)}) collective-permute-start(f32[64,4096]{1,0:T(8,128)S(1)} %slice_add_fusion), channel_id=1, source_target_pairs={{32,0},{40,8},{48,16},{56,24},{64,32},{72,40},{80,48},{88,56},{96,... | collective-permute-start | bytes 3145736 | tf_op jit(solution)/shard_map/ppermute | solution.py:36
  220.2 22.7 %collective-permute-start.46 = (f32[64,4096]{1,0:T(8,128)S(1)}, f32[64,4096]{1,0:T(8,128)S(1)}, u32[]{:S(2)}, u32[]{:S(2)}) collective-permute-start(f32[64,4096]{1,0:T(8,128)S(1)} %pad_maximum_fusion.6), channel_id=1, source_target_pairs={{96,0},{104,8},{112,16},{120,24},{0,32},{8,40},{16,48},{24,56},{32... | collective-permute-start | bytes 3145736 | tf_op jit(solution)/shard_map/ppermute | solution.py:36
  243.9 19.0 %all-to-all-start.1 = ((f32[128,1,128]{2,1,0:T(1,128)}), f32[128,1,128]{2,1,0:T(1,128)S(1)}, u32[]{:S(2)}, u32[]{:S(2)}) async-start(f32[128,1,128]{2,1,0:T(1,128)} %broadcast_in_dim.5), calls=%async_computation.1 | async-start | bytes 131072 | tf_op jit(solution)/shard_map/all_to_all | solution.py:47
  (45 other events, 550.5 us)

commit v4 on v3

--- a/solution.py
+++ b/solution.py
@@ -11,8 +11,11 @@
 BS = 128
 GROUP = 16
 HEAD = 8
+NEAR = ((0, 0), (0, 1), (3, 0), (1, 0), (2, 0), (3, 1), (1, 1))
+SEQUENCE = tuple((dx, dz, dc) for dc in (0, 1) for dx, dz in NEAR) + ((2, 1, 0), (2, 1, 1))
 YROWS = 40
-VMEM_BYTES = 56 * 1024 * 1024
+BUFFERS = 6
+VMEM_BYTES = 32 * 1024 * 1024
 
 NX, NZ, NCORE = 4, 2, 2
 NZH, NY = 2, 4
@@ -60,64 +63,91 @@
     )
 
 
-def start_blocks(blocks, held, sems, groups):
-    def start(group, _):
-        span = pl.ds(group * GROUP, GROUP)
-        pltpu.make_async_copy(blocks.at[span], held.at[span], sems.at[group]).start()
+def fetch(blocks, held, sems, meta_ref, group):
+    buffer = group % BUFFERS
+    for inner in range(GROUP):
+        slot = meta_ref[HEAD + group * GROUP + inner]
+        pltpu.make_async_copy(blocks.at[slot], held.at[buffer, inner], sems.at[buffer]).start()
+
+
+def run_groups(blocks, held, sems, meta_ref, start, stop, total, work):
+    def one(group, _):
+        buffer = group % BUFFERS
+        pltpu.make_async_copy(blocks.at[pl.ds(0, GROUP)], held.at[buffer], sems.at[buffer]).wait()
+        work(group, buffer)
+
+        @pl.when(group + BUFFERS < total)
+        def _():
+            fetch(blocks, held, sems, meta_ref, group + BUFFERS)
+
         return 0
 
-    lax.fori_loop(0, groups, start, 0)
-
-
-def wait_blocks(blocks, held, sems, group):
-    span = pl.ds(group * GROUP, GROUP)
-    pltpu.make_async_copy(blocks.at[span], held.at[span], sems.at[group]).wait()
-
-
-def forward_kernel(kc, places, meta_ref, blocks_ref, *refs):
+    lax.fori_loop(start, stop, one, 0)
+
+
+def fetch_first(blocks, held, sems, meta_ref, total):
+    def one(group, _):
+        fetch(blocks, held, sems, meta_ref, group)
+        return 0
+
+    lax.fori_loop(0, jnp.minimum(total, BUFFERS), one, 0)
+
+
+def ends_of(meta_ref, slots, position):
+    return meta_ref[HEAD + 3 * (slots + GROUP) + position]
+
+
+def owner_of(meta_ref, place):
+    dx, dz, dc = place
+    x, z, c = meta_ref[1], meta_ref[2], meta_ref[3]
+    return ((x + dx) % NX) * 4 + ((z + dz) % NZ) * 2 + (c + dc) % NCORE
+
+
+def forward_kernel(kc, slots, stages, places, meta_ref, blocks_ref, *refs):
     pieces = refs[: len(places)]
     outs = refs[len(places) : len(places) + NY + NZH]
-    panel, acc, held, sems, block_sems = refs[len(places) + NY + NZH :]
-    count = meta_ref[0]
-    x, z, c = meta_ref[1], meta_ref[2], meta_ref[3]
-    groups = (count + GROUP - 1) // GROUP
-    slots = held.shape[0]
+    acc, panel, held, sems, block_sems = refs[len(places) + NY + NZH :]
+    last = ends_of(meta_ref, slots, len(SEQUENCE) - 1)
+    total = (last + GROUP - 1) // GROUP
 
     copies = []
     for number, (dc, entries) in enumerate(places):
-        for first, size, (dx, dz), start in entries:
-            owner = ((x + dx) % NX) * 4 + ((z + dz) % NZ) * 2 + (c + dc) % NCORE
-            copies.append(
-                pltpu.make_async_copy(
-                    pieces[number].at[pl.ds(first, size)],
-                    panel.at[owner, pl.ds(start, size), :],
-                    sems.at[len(copies)],
-                )
+        for source, size, (dx, dz), start in entries:
+            position = SEQUENCE.index((dx, dz, dc))
+            copy = pltpu.make_async_copy(
+                pieces[number].at[pl.ds(source, size)],
+                panel.at[position, pl.ds(start, size), :],
+                sems.at[len(copies)],
             )
-    for copy in copies:
+            copies.append((position, copy))
+    for _, copy in copies:
         copy.start()
-    start_blocks(blocks_ref, held, block_sems, groups)
+    fetch_first(blocks_ref, held, block_sems, meta_ref, total)
     acc[...] = jnp.zeros_like(acc)
-    for copy in copies:
-        copy.wait()
-
-    def work(group, _):
-        wait_blocks(blocks_ref, held, block_sems, group)
+
+    def work(group, buffer):
         for inner in range(GROUP):
             slot = group * GROUP + inner
-            cell = meta_ref[HEAD + slots + slot]
-            offset = pl.multiple_of((cell % 32) * BS, BS)
-            left = doubled(panel[cell // 32, :, pl.ds(offset, BS)])
-            high, low = split(held[slot])
+            place = meta_ref[HEAD + 2 * (slots + GROUP) + slot]
+            offset = pl.multiple_of((place % 32) * BS, BS)
+            left = doubled(panel[place // 32, :, pl.ds(offset, BS)])
+            high, low = split(held[buffer, inner])
             right = jnp.concatenate([high, low], axis=1)
             both = lax.dot_general(
                 right, left, (((1,), (1,)), ((), ())), preferred_element_type=jnp.float32
             )
-            live = jnp.where(slot < count, 1.0, 0.0)
-            acc[meta_ref[HEAD + slot]] += both * live
-        return 0
-
-    lax.fori_loop(0, groups, work, 0)
+            live = jnp.where(slot < last, 1.0, 0.0)
+            acc[meta_ref[HEAD + slots + GROUP + slot]] += both * live
+
+    done, waited = 0, 0
+    for stage in stages:
+        for position, copy in copies:
+            if waited <= position < stage:
+                copy.wait()
+        waited = stage
+        stop = total if stage == stages[-1] else ends_of(meta_ref, slots, stage - 1) // GROUP
+        run_groups(blocks_ref, held, block_sems, meta_ref, done, stop, total, work)
+        done = stop
 
     zh, y = meta_ref[4], meta_ref[5]
     per = acc.shape[0] // (NZH * NY)
@@ -131,16 +161,14 @@
                 outs[NY + dz][dy, :, t * BS : (t + 1) * BS] = both[YROWS:]
 
 
-def backward_kernel(kc, layout, meta_ref, blocks_ref, alpha_ref, *refs):
+def backward_kernel(kc, slots, stages, layout, meta_ref, blocks_ref, alpha_ref, *refs):
     res = refs[:NY]
     img = refs[NY : 2 * NY]
     outs = refs[2 * NY : 2 * NY + len(layout)]
     source, acc, held, sems, block_sems = refs[2 * NY + len(layout) :]
-    count = meta_ref[0]
-    x, z, c = meta_ref[1], meta_ref[2], meta_ref[3]
-    groups = (count + GROUP - 1) // GROUP
-    slots = held.shape[0]
-    start_blocks(blocks_ref, held, block_sems, groups)
+    last = ends_of(meta_ref, slots, len(SEQUENCE) - 1)
+    total = (last + GROUP - 1) // GROUP
+    fetch_first(blocks_ref, held, block_sems, meta_ref, total)
 
     zh, y = meta_ref[4], meta_ref[5]
     per = source.shape[0] // (NZH * NY)
@@ -159,92 +187,113 @@
 
     lax.fori_loop(0, acc.shape[0], clear, 0)
 
-    def work(group, _):
-        wait_blocks(blocks_ref, held, block_sems, group)
+    def work(group, buffer):
         for inner in range(GROUP):
             slot = group * GROUP + inner
-            left = source[meta_ref[HEAD + slot]]
-            high, low = split(held[slot])
+            left = source[meta_ref[HEAD + slots + GROUP + slot]]
+            high, low = split(held[buffer, inner])
             right = jnp.concatenate([high, low], axis=0)
             both = lax.dot_general(
                 left, right, (((1,), (0,)), ((), ())), preferred_element_type=jnp.float32
             )
-            live = jnp.where(slot < count, 1.0, 0.0)
-            cell = meta_ref[HEAD + slots + slot]
-            offset = pl.multiple_of((cell % 32) * BS, BS)
-            acc[cell // 32, :, pl.ds(offset, BS)] += (both[:kc] + both[kc:]) * live
-        return 0
-
-    lax.fori_loop(0, groups, work, 0)
+            live = jnp.where(slot < last, 1.0, 0.0)
+            place = meta_ref[HEAD + 2 * (slots + GROUP) + slot]
+            offset = pl.multiple_of((place % 32) * BS, BS)
+            acc[place // 32, :, pl.ds(offset, BS)] += (both[:kc] + both[kc:]) * live
 
     copies = []
     for number, (dc, entries) in enumerate(layout):
-        for first, size, (dx, dz), start in entries:
-            owner = ((x + dx) % NX) * 4 + ((z + dz) % NZ) * 2 + (c + dc) % NCORE
-            copies.append(
-                pltpu.make_async_copy(
-                    acc.at[owner, pl.ds(start, size), :],
-                    outs[number].at[pl.ds(first, size)],
-                    sems.at[len(copies)],
-                )
+        for target, size, (dx, dz), start in entries:
+            position = SEQUENCE.index((dx, dz, dc))
+            copy = pltpu.make_async_copy(
+                acc.at[position, pl.ds(start, size), :],
+                outs[number].at[pl.ds(target, size)],
+                sems.at[len(copies)],
             )
-    for copy in copies:
-        copy.start()
-    for copy in copies:
+            copies.append((position, copy))
+    done, sent = 0, 0
+    for stage in stages:
+        stop = (ends_of(meta_ref, slots, stage - 1) + GROUP - 1) // GROUP
+        run_groups(blocks_ref, held, block_sems, meta_ref, done, stop, total, work)
+        done = stop
+        for position, copy in copies:
+            if sent <= position < stage:
+                copy.start()
+        sent = stage
+    for _, copy in copies:
         copy.wait()
 
 
-def cost(kc, slots):
+def cost(kc, slots, shards):
     return pl.CostEstimate(
         flops=6 * slots * BS * BS * kc,
-        bytes_accessed=4 * (slots * BS * BS + 2 * 16 * kc * 4096),
+        bytes_accessed=4 * (slots * BS * BS + 2 * shards * kc * 4096),
         transcendentals=0,
     )
 
 
-def forward(blocks, meta, places, pieces, kc):
+def forward(blocks, meta, places, pieces, kc, stages):
     slots = blocks.shape[0]
     smem, vmem = pl.BlockSpec(memory_space=pltpu.SMEM), pl.BlockSpec(memory_space=pltpu.VMEM)
     any_spec = pl.BlockSpec(memory_space=pl.ANY)
-    copies = sum(len(entries) for _, entries in places)
+    out_shape = [jax.ShapeDtypeStruct((NZH, YROWS, 6 * BS), jnp.float32)] * NY
+    out_shape += [jax.ShapeDtypeStruct((NY, kc - YROWS, 6 * BS), jnp.float32)] * NZH
     return pl.pallas_call(
-        functools.partial(forward_kernel, kc, places),
+        functools.partial(forward_kernel, kc, slots, stages, places),
         in_specs=[smem] + [any_spec] * (1 + len(pieces)),
-        out_specs=[vmem] * (NY + NZH),
+        out_specs=[vmem] * len(out_shape),
         scratch_shapes=[
+            pltpu.VMEM((48, BS, 2 * kc), jnp.float32),
             pltpu.VMEM((16, kc, 4096), jnp.float32),
-            pltpu.VMEM((48, BS, 2 * kc), jnp.float32),
-            pltpu.VMEM(blocks.shape, jnp.float32),
-            pltpu.SemaphoreType.DMA((copies,)),
-            pltpu.SemaphoreType.DMA((slots // GROUP,)),
+            pltpu.VMEM((BUFFERS, GROUP, BS, BS), jnp.float32),
+            pltpu.SemaphoreType.DMA((sum(len(entries) for _, entries in places),)),
+            pltpu.SemaphoreType.DMA((BUFFERS,)),
         ],
-        out_shape=[jax.ShapeDtypeStruct((NZH, YROWS, 6 * BS), jnp.float32)] * NY
-        + [jax.ShapeDtypeStruct((NY, kc - YROWS, 6 * BS), jnp.float32)] * NZH,
+        out_shape=out_shape,
         compiler_params=pltpu.CompilerParams(vmem_limit_bytes=VMEM_BYTES),
-        cost_estimate=cost(kc, slots),
+        cost_estimate=cost(kc, slots, len(SEQUENCE)),
     )(meta, blocks, *pieces)
 
 
-def backward(blocks, meta, alpha, res, img, layout, kc):
+def backward(blocks, meta, alpha, res, img, layout, kc, stages):
     slots = blocks.shape[0]
     smem, vmem = pl.BlockSpec(memory_space=pltpu.SMEM), pl.BlockSpec(memory_space=pltpu.VMEM)
     any_spec = pl.BlockSpec(memory_space=pl.ANY)
     shapes = [(sum(entry[1] for entry in entries), 4096) for _, entries in layout]
     return pl.pallas_call(
-        functools.partial(backward_kernel, kc, layout),
+        functools.partial(backward_kernel, kc, slots, stages, layout),
         in_specs=[smem] + [any_spec] + [vmem] * (1 + 2 * NY),
         out_specs=[any_spec] * len(layout),
         scratch_shapes=[
             pltpu.VMEM((48, 2 * kc, 2 * BS), jnp.bfloat16),
             pltpu.VMEM((16, kc, 4096), jnp.float32),
-            pltpu.VMEM(blocks.shape, jnp.float32),
+            pltpu.VMEM((BUFFERS, GROUP, BS, BS), jnp.float32),
             pltpu.SemaphoreType.DMA((sum(len(entries) for _, entries in layout),)),
-            pltpu.SemaphoreType.DMA((slots // GROUP,)),
+            pltpu.SemaphoreType.DMA((BUFFERS,)),
         ],
         out_shape=[jax.ShapeDtypeStruct(shape, jnp.float32) for shape in shapes],
         compiler_params=pltpu.CompilerParams(vmem_limit_bytes=VMEM_BYTES),
-        cost_estimate=cost(kc, slots),
+        cost_estimate=cost(kc, slots, len(SEQUENCE)),
     )(meta, blocks, alpha, *res, *img)
+
+
+def sorted_slots(rows, cols, count, x, z, c):
+    slots = rows.shape[0]
+    number = jnp.arange(slots, dtype=jnp.int32)
+    owner = cols // 32
+    code = ((owner // 4 - x) % NX) * 4 + ((owner // 2 - z) % NZ) * 2 + (owner - c) % NCORE
+    codes = jnp.array([dx * 4 + dz * 2 + dc for dx, dz, dc in SEQUENCE], jnp.int32)
+    steps = jnp.arange(len(SEQUENCE), dtype=jnp.int32)
+    position = jnp.sum(jnp.where(code[:, None] == codes, steps, 0), axis=1)
+    live = number < count
+    key = jnp.where(live, position, len(SEQUENCE)) * slots + number
+    rank = jnp.sum((key[None] < key[:, None]).astype(jnp.int32), axis=1)
+    where = rank[None] == number[:, None]
+    place = position * 32 + cols % 32
+    lists = [jnp.sum(jnp.where(where, value[None], 0), axis=1) for value in (number, rows, place)]
+    ends = jnp.sum((live[None] & (position[None] <= steps[:, None])).astype(jnp.int32), axis=1)
+    pad = jnp.zeros((GROUP,), jnp.int32)
+    return jnp.concatenate([part for value in lists for part in (value, pad)] + [ends])
 
 
 def after(*values):
@@ -389,7 +438,8 @@
         col_index % 4,
     ]
     head = jnp.stack(head + [jnp.int32(0)] * (HEAD - len(head))).astype(jnp.int32)
-    meta = jnp.concatenate([head, block_rows[0], block_cols[0]])
+    lists = sorted_slots(block_rows[0], block_cols[0], head[0], head[1], head[2], head[3])
+    meta = jnp.concatenate([head, lists])
 
     own = dirn
     first = first_step(own)
@@ -408,7 +458,7 @@
     rides_z = col_shift(rides, 1, 0)
     others += [swap_core(piece) for piece in third]
     pieces = [own, *first, *second, *third, own_other, z1_other, *others]
-    parts = forward(tile_blocks, meta, both_cores(kc), pieces, kc)
+    parts = forward(tile_blocks, meta, both_cores(kc), pieces, kc, (7, 14, 16))
 
     far = col_shift(parts[NY + 1], 1, 0)
     far, rides_z = after(far, rides_z)
@@ -421,7 +471,7 @@
     norms = sum_over(norms[None], ("row", "col"))[0]
     gamma = norms[:width]
     alpha = (gamma / (norms[width:] + EPS))[:, None]
-    back = backward(tile_blocks, meta, alpha, rides, image_tile, by_step(kc), kc)
+    back = backward(tile_blocks, meta, alpha, rides, image_tile, by_step(kc), kc, (4, 8, 12, 16))
     own_back, z1, up1, down1, z2, up2, down2, z3, up3, down3 = sum_cores(back, kc)
     third = third_back(z3, up3, down3)
     z2, third = after(z2, third)

time: 265 us -> 251 us (0.947)
  Pallas kernels: 24.3 us -> 13.4 us
  local copies, waits for them, and re-layouts: 7.55 us -> 4.74 us
    pallas_call x2, Pallas kernels: 24.3 us -> 13.4 us  [the longest x1 6.72 us: backward(): pl.pallas_call(functools.partial(backward_kernel, kc, slots, stages, layo...]
    ppermute x16, waiting for transfers between devices: 15.3 us -> 18.1 us  [col_shift(): return lax.ppermute(value, 'col', pairs)]
  transfers between devices with their start and end apart: 49 -> 49, of which waited for: 28 -> 25; matrix products, arithmetic and copies ran while one was open for 5% -> 6% of each run, Pallas kernels for 4% -> 3%
where the time goes in v4:
time: 251 us
  waiting for transfers between devices  139 us (55%)
  starting transfers between devices  79.9 us (32%)
  Pallas kernels  13.4 us (5%)
  other arithmetic  12.2 us (5%)
  local copies, waits for them, and re-layouts  4.74 us (2%)
    ppermute x31, waiting for transfers between devices, row_shift(): return lax.ppermute(value, 'row', pairs)  104 us
    ppermute x31, starting transfers between devices, row_shift(): return lax.ppermute(value, 'row', pairs)  31.8 us
    ppermute x16, starting transfers between devices, col_shift(): return lax.ppermute(value, 'col', pairs)  27 us
    all_to_all x2, starting transfers between devices, sum_over(): return jnp.sum(lax.all_to_all(sent, axes, 0, 0, tiled=True), axis=0)  21.1 us
    ppermute x16, waiting for transfers between devices, col_shift(): return lax.ppermute(value, 'col', pairs)  18.1 us
    all_to_all x2, waiting for transfers between devices, sum_over(): return jnp.sum(lax.all_to_all(sent, axes, 0, 0, tiled=True), axis=0)  17.3 us
    pallas_call x1, Pallas kernels, backward(): pl.pallas_call(functools.partial(backward_kernel, kc, slots, stages, layo...  6.72 us
    pallas_call x1, Pallas kernels, forward(): pl.pallas_call(functools.partial(forward_kernel, kc, slots, stages, place...  6.63 us
  transfers between devices with their start and end apart: 49, of which 25 were waited for; matrix products, arithmetic and copies ran while one was open for 6% of the time, Pallas kernels for 3%

profile of v4, /device:TPU:1, one launch (start us, length us, event | category | flops | bytes accessed | tf_op | source)
XLA Modules:
  0.0 251.1 jit_solution(14260980183070611607)
XLA Ops:
  0.6 2.5 %collective-permute-start = (f32[64,4096]{1,0:T(8,128)}, f32[64,4096]{1,0:T(8,128)S(1)}, u32[]{:S(2)}, u32[]{:S(2)}) collective-permute-start(f32[64,4096]{1,0:T(8,128)} %bitcast.61), channel_id=1, source_target_pairs={{16,0},{24,8},{0,16},{8,24},{48,32},{56,40},{32,48},{40,56},{80,64... | collective-permute-start | bytes 3145736 | tf_op jit(solution)/shard_map/ppermute | solution.py:39
  10.0 16.3 %collective-permute-done.refs_1_ = f32[64,4096]{1,0:T(8,128)S(1)} collective-permute-done((f32[64,4096]{1,0:T(8,128)}, f32[64,4096]{1,0:T(8,128)S(1)}, u32[]{:S(2)}, u32[]{:S(2)}) %collective-permute-start) | collective-permute-done | bytes 1048608 | tf_op jit(solution)/shard_map/ppermute | solution.py:39
  26.3 2.1 collective-permute-done.1.refs_2_
  28.4 1.9 collective-permute-start.6
  34.9 2.7 %collective-permute-start.7 = (f32[64,768]{1,0:T(8,128)S(1)}, f32[64,768]{1,0:T(8,128)S(1)}, u32[]{:S(2)}, u32[]{:S(2)}) collective-permute-start(f32[64,768]{1,0:T(8,128)S(1)} %bitcast.68), channel_id=1, source_target_pairs={{1,0},{2,1},{3,2},{0,3},{5,4},{6,5},{7,6},{4,7},{9,8},{10,9},{11,1... | collective-permute-start | bytes 589832 | tf_op jit(solution)/shard_map/ppermute | solution.py:44
  37.7 18.3 %collective-permute-done.3.refs_4_ = f32[64,4096]{1,0:T(8,128)S(1)} collective-permute-done((f32[64,4096]{1,0:T(8,128)S(1)}, f32[64,4096]{1,0:T(8,128)S(1)}, u32[]{:S(2)}, u32[]{:S(2)}) %collective-permute-start.3) | collective-permute-done | bytes 1048608 | tf_op jit(solution)/shard_map/ppermute | solution.py:39
  65.9 2.9 %collective-permute-start.17 = (f32[64,768]{1,0:T(8,128)S(1)}, f32[64,768]{1,0:T(8,128)S(1)}, u32[]{:S(2)}, u32[]{:S(2)}) collective-permute-start(f32[64,768]{1,0:T(8,128)S(1)} %bitcast.70), channel_id=1, source_target_pairs={{2,0},{3,1},{0,2},{1,3},{6,4},{7,5},{4,6},{5,7},{10,8},{11,9},{8,1... | collective-permute-start | bytes 589832 | tf_op jit(solution)/shard_map/ppermute | solution.py:44
  71.7 1.8 collective-permute-done.17
  73.6 3.8 %collective-permute-done.10.refs_8_ = f32[16,4096]{1,0:T(8,128)S(1)} collective-permute-done((f32[16,4096]{1,0:T(8,128)S(1)}, f32[16,4096]{1,0:T(8,128)S(1)}, u32[]{:S(2)}, u32[]{:S(2)}) %collective-permute-start.10) | collective-permute-done | bytes 262176 | tf_op jit(solution)/shard_map/ppermute | solution.py:39
  79.6 3.4 %collective-permute-start.27 = (f32[4,64,768]{2,1,0:T(8,128)S(1)}, f32[4,64,768]{2,1,0:T(8,128)S(1)}, u32[]{:S(2)}, u32[]{:S(2)}) collective-permute-start(f32[4,64,768]{2,1,0:T(8,128)S(1)} %pad_maximum_fusion.7), channel_id=1, source_target_pairs={{4,0},{5,1},{6,2},{7,3},{0,4},{1,5},{2,6},{3,7},{12,8},{13,9},{14,... | collective-permute-start | bytes 2359304 | tf_op jit(solution)/shard_map/ppermute | solution.py:44
  83.0 6.6 %shard_map.112 = (f32[2,40,768]{2,1,0:T(8,128)S(1)}, f32[2,40,768]{2,1,0:T(8,128)S(1)}, f32[2,40,768]{2,1,0:T(8,128)S(1)}, f32[2,40,768]{2,1,0:T(8,128)S(1)}, f3...) custom-call(s32[840]{0:T(1024)S(1)} %concatenate.33.meta_ref, f32[256,128,128]{2,1,0:T(8,128)} %bitcast.66, ...), custom_call_target="tpu_custom_call" | custom-call | flops 1610612736 | bytes 50331648 | tf_op jit(solution)/shard_map/pallas_call | solution.py:241
  89.7 2.0 collective-permute-start.22
  91.7 3.2 %collective-permute-start.23 = (f32[2,40,768]{2,1,0:T(8,128)S(1)}, f32[2,40,768]{2,1,0:T(8,128)S(1)}, u32[]{:S(2)}, u32[]{:S(2)}) collective-permute-start(f32[2,40,768]{2,1,0:T(8,128)S(1)} %get-tuple-element.70), channel_id=1, source_target_pairs={{1,0},{2,1},{3,2},{0,3},{5,4},{6,5},{7,6},{4,7},{9,8},{10,9},{11,1... | collective-permute-start | bytes 737288 | tf_op jit(solution)/shard_map/ppermute | solution.py:44
  94.9 2.1 collective-permute-start.24
  97.7 1.9 collective-permute-start.26
  99.6 6.5 %collective-permute-done.24 = f32[2,40,768]{2,1,0:T(8,128)S(1)} collective-permute-done((f32[2,40,768]{2,1,0:T(8,128)S(1)}, f32[2,40,768]{2,1,0:T(8,128)S(1)}, u32[]{:S(2)}, u32[]{:S(2)}) %collective-permute-start.24) | collective-permute-done | bytes 245792 | tf_op jit(solution)/shard_map/ppermute | solution.py:44
  106.2 4.3 %collective-permute-start.25 = (f32[40,768]{1,0:T(8,128)S(1)}, f32[40,768]{1,0:T(8,128)S(1)}, u32[]{:S(2)}, u32[]{:S(2)}) collective-permute-start(f32[40,768]{1,0:T(8,128)S(1)} %slice_bitcast_fusion), channel_id=1, source_target_pairs={{4,0},{5,1},{6,2},{7,3},{0,4},{1,5},{2,6},{3,7},{12,8},{13,9},{14,... | collective-permute-start | bytes 368648 | tf_op jit(solution)/shard_map/ppermute | solution.py:44
  111.2 2.1 collective-permute-start.29
  115.4 2.6 %collective-permute-done.30 = f32[24,768]{1,0:T(8,128)S(1)} collective-permute-done((f32[24,768]{1,0:T(8,128)S(1)}, f32[24,768]{1,0:T(8,128)S(1)}, u32[]{:S(2)}, u32[]{:S(2)}) %collective-permute-start.30) | collective-permute-done | bytes 73760 | tf_op jit(solution)/shard_map/ppermute | solution.py:44
  119.2 5.0 %collective-permute-done.31 = f32[64,768]{1,0:T(8,128)S(1)} collective-permute-done((f32[64,768]{1,0:T(8,128)S(1)}, f32[64,768]{1,0:T(8,128)S(1)}, u32[]{:S(2)}, u32[]{:S(2)}) %collective-permute-start.31) | collective-permute-done | bytes 196640 | tf_op jit(solution)/shard_map/ppermute | solution.py:44
  126.6 12.2 %all-to-all-start = ((f32[128,1,128]{2,1,0:T(1,128)}), f32[128,1,128]{2,1,0:T(1,128)}, u32[]{:S(2)}, u32[]{:S(2)}) async-start(f32[128,1,128]{2,1,0:T(1,128)} %broadcast_in_dim.72), calls=%async_computation | async-start | bytes 131072 | tf_op jit(solution)/shard_map/all_to_all | solution.py:50
  140.0 8.4 %all-to-all-done = f32[128,1,128]{2,1,0:T(1,128)} async-done(((f32[128,1,128]{2,1,0:T(1,128)}), f32[128,1,128]{2,1,0:T(1,128)}, u32[]{:S(2)}, u32[]{:S(2)}) %all-to-all-start) | async-done | bytes 65568 | tf_op jit(solution)/shard_map/all_to_all | solution.py:50
  149.5 6.7 %shard_map.113 = (f32[64,4096]{1,0:T(8,128)S(1)}, f32[192,4096]{1,0:T(8,128)S(1)}, f32[256,4096]{1,0:T(8,128)S(1)}, f32[64,4096]{1,0:T(8,128)S(1)}, f32[192,4096]{1,0:T(8,128)S(1)}, /*index=5*/f32[256,4096]{1,0:T(8,128)S(1)}) custom-call(s32[840]{0:T(1024)S(1)} %concatenate.33.meta_ref, f32[256,128,128]{2,1,0:T(8,128)} %bitcast.67, ...), custom_call_target="tpu_custom_call" | custom-call | flops 1610612736 | bytes 50331648 | tf_op jit(solution)/shard_map/pallas_call | solution.py:263
  156.2 5.8 %collective-permute-start.35 = (f32[64,4096]{1,0:T(8,128)S(1)}, f32[64,4096]{1,0:T(8,128)S(1)}, u32[]{:S(2)}, u32[]{:S(2)}) collective-permute-start(f32[64,4096]{1,0:T(8,128)S(1)} %get-tuple-element.80), channel_id=1, source_target_pairs={{8,0},{0,8},{24,16},{16,24},{40,32},{32,40},{56,48},{48,56},{72,64... | collective-permute-start | bytes 3145736 | tf_op jit(solution)/shard_map/ppermute | solution.py:39
  162.0 2.3 collective-permute-done.35
  165.0 5.0 %collective-permute-done.36 = f32[192,4096]{1,0:T(8,128)S(1)} collective-permute-done((f32[192,4096]{1,0:T(8,128)S(1)}, f32[192,4096]{1,0:T(8,128)S(1)}, u32[]{:S(2)}, u32[]{:S(2)}) %collective-permute-start.36) | collective-permute-done | bytes 3145760 | tf_op jit(solution)/shard_map/ppermute | solution.py:39
  172.4 5.8 %collective-permute-done.39 = f32[16,4096]{1,0:T(8,128)S(1)} collective-permute-done((f32[16,4096]{1,0:T(8,128)S(1)}, f32[16,4096]{1,0:T(8,128)S(1)}, u32[]{:S(2)}, u32[]{:S(2)}) %collective-permute-start.39) | collective-permute-done | bytes 262176 | tf_op jit(solution)/shard_map/ppermute | solution.py:39
  182.1 21.4 %collective-permute-done.41 = f32[64,4096]{1,0:T(8,128)S(1)} collective-permute-done((f32[64,4096]{1,0:T(8,128)S(1)}, f32[64,4096]{1,0:T(8,128)S(1)}, u32[]{:S(2)}, u32[]{:S(2)}) %collective-permute-start.41) | collective-permute-done | bytes 1048608 | tf_op jit(solution)/shard_map/ppermute | solution.py:39
  208.7 19.6 %collective-permute-done.43 = f32[64,4096]{1,0:T(8,128)S(1)} collective-permute-done((f32[64,4096]{1,0:T(8,128)S(1)}, f32[64,4096]{1,0:T(8,128)S(1)}, u32[]{:S(2)}, u32[]{:S(2)}) %collective-permute-start.43) | collective-permute-done | bytes 1048608 | tf_op jit(solution)/shard_map/ppermute | solution.py:39
  228.3 1.9 collective-permute-done.46
  231.2 9.0 %all-to-all-start.1 = ((f32[128,1,128]{2,1,0:T(1,128)}), f32[128,1,128]{2,1,0:T(1,128)S(1)}, u32[]{:S(2)}, u32[]{:S(2)}) async-start(f32[128,1,128]{2,1,0:T(1,128)} %broadcast_in_dim.73), calls=%async_computation.1 | async-start | bytes 131072 | tf_op jit(solution)/shard_map/all_to_all | solution.py:50
  241.0 8.9 %all-to-all-done.1 = f32[128,1,128]{2,1,0:T(1,128)S(1)} async-done(((f32[128,1,128]{2,1,0:T(1,128)}), f32[128,1,128]{2,1,0:T(1,128)S(1)}, u32[]{:S(2)}, u32[]{:S(2)}) %all-to-all-start.1) | async-done | bytes 65568 | tf_op jit(solution)/shard_map/all_to_all | solution.py:50
  (146 shorter events, 50.3 us)
Async XLA Ops:
  0.6 25.6 %collective-permute-start = (f32[64,4096]{1,0:T(8,128)}, f32[64,4096]{1,0:T(8,128)S(1)}, u32[]{:S(2)}, u32[]{:S(2)}) collective-permute-start(f32[64,4096]{1,0:T(8,128)} %bitcast.61), channel_id=1, source_target_pairs={{16,0},{24,8},{0,16},{8,24},{48,32},{56,40},{32,48},{40,56},{80,64... | collective-permute-start | bytes 3145736 | tf_op jit(solution)/shard_map/ppermute | solution.py:39
  3.2 25.1 %collective-permute-start.1 = (f32[64,4096]{1,0:T(8,128)}, f32[64,4096]{1,0:T(8,128)S(1)}, u32[]{:S(2)}, u32[]{:S(2)}) collective-permute-start(f32[64,4096]{1,0:T(8,128)} %bitcast.62), channel_id=1, source_target_pairs={{96,0},{104,8},{112,16},{120,24},{0,32},{8,40},{16,48},{24,56},{32... | collective-permute-start | bytes 3145736 | tf_op jit(solution)/shard_map/ppermute | solution.py:39
  4.4 23.9 %collective-permute-start.2 = (f32[64,4096]{1,0:T(8,128)}, f32[64,4096]{1,0:T(8,128)S(1)}, u32[]{:S(2)}, u32[]{:S(2)}) collective-permute-start(f32[64,4096]{1,0:T(8,128)} %bitcast.63), channel_id=1, source_target_pairs={{32,0},{40,8},{48,16},{56,24},{64,32},{72,40},{80,48},{88,56},{96,... | collective-permute-start | bytes 3145736 | tf_op jit(solution)/shard_map/ppermute | solution.py:39
  32.0 23.9 %collective-permute-start.3 = (f32[64,4096]{1,0:T(8,128)S(1)}, f32[64,4096]{1,0:T(8,128)S(1)}, u32[]{:S(2)}, u32[]{:S(2)}) collective-permute-start(f32[64,4096]{1,0:T(8,128)S(1)} %get-tuple-element.123), channel_id=1, source_target_pairs={{16,0},{24,8},{0,16},{8,24},{48,32},{56,40},{32,48},{40,56},{80,64... | collective-permute-start | bytes 3145736 | tf_op jit(solution)/shard_map/ppermute | solution.py:39
  32.2 25.5 %collective-permute-start.4 = (f32[64,4096]{1,0:T(8,128)S(1)}, f32[64,4096]{1,0:T(8,128)S(1)}, u32[]{:S(2)}, u32[]{:S(2)}) collective-permute-start(f32[64,4096]{1,0:T(8,128)S(1)} %get-tuple-element.124), channel_id=1, source_target_pairs={{96,0},{104,8},{112,16},{120,24},{0,32},{8,40},{16,48},{24,56},{32... | collective-permute-start | bytes 3145736 | tf_op jit(solution)/shard_map/ppermute | solution.py:39
  33.4 25.6 %collective-permute-start.5 = (f32[64,4096]{1,0:T(8,128)S(1)}, f32[64,4096]{1,0:T(8,128)S(1)}, u32[]{:S(2)}, u32[]{:S(2)}) collective-permute-start(f32[64,4096]{1,0:T(8,128)S(1)} %get-tuple-element.122), channel_id=1, source_target_pairs={{32,0},{40,8},{48,16},{56,24},{64,32},{72,40},{80,48},{88,56},{96,... | collective-permute-start | bytes 3145736 | tf_op jit(solution)/shard_map/ppermute | solution.py:39
  34.9 24.0 %collective-permute-start.7 = (f32[64,768]{1,0:T(8,128)S(1)}, f32[64,768]{1,0:T(8,128)S(1)}, u32[]{:S(2)}, u32[]{:S(2)}) collective-permute-start(f32[64,768]{1,0:T(8,128)S(1)} %bitcast.68), channel_id=1, source_target_pairs={{1,0},{2,1},{3,2},{0,3},{5,4},{6,5},{7,6},{4,7},{9,8},{10,9},{11,1... | collective-permute-start | bytes 589832 | tf_op jit(solution)/shard_map/ppermute | solution.py:44
  37.7 21.3 %collective-permute-start.8 = (f32[64,768]{1,0:T(8,128)S(1)}, f32[64,768]{1,0:T(8,128)S(1)}, u32[]{:S(2)}, u32[]{:S(2)}) collective-permute-start(f32[64,768]{1,0:T(8,128)S(1)} %bitcast.69), channel_id=1, source_target_pairs={{3,0},{0,1},{1,2},{2,3},{7,4},{4,5},{5,6},{6,7},{11,8},{8,9},{9,10... | collective-permute-start | bytes 589832 | tf_op jit(solution)/shard_map/ppermute | solution.py:44
  59.9 17.5 %collective-permute-start.9 = (f32[32,4096]{1,0:T(8,128)S(1)}, f32[32,4096]{1,0:T(8,128)S(1)}, u32[]{:S(2)}, u32[]{:S(2)}) collective-permute-start(f32[32,4096]{1,0:T(8,128)S(1)} %slice.160), channel_id=1, source_target_pairs={{16,0},{24,8},{0,16},{8,24},{48,32},{56,40},{32,48},{40,56},{80,64... | collective-permute-start | bytes 1572872 | tf_op jit(solution)/shard_map/ppermute | solution.py:39
  61.4 21.6 %collective-permute-start.18 = (f32[64,4096]{1,0:T(8,128)S(1)}, f32[64,4096]{1,0:T(8,128)S(1)}, u32[]{:S(2)}, u32[]{:S(2)}) collective-permute-start(f32[64,4096]{1,0:T(8,128)S(1)} %bitcast.64), channel_id=1, source_target_pairs={{8,0},{0,8},{24,16},{16,24},{40,32},{32,40},{56,48},{48,56},{72,64... | collective-permute-start | bytes 3145736 | tf_op jit(solution)/shard_map/ppermute | solution.py:39
  68.9 8.5 %collective-permute-start.10 = (f32[16,4096]{1,0:T(8,128)S(1)}, f32[16,4096]{1,0:T(8,128)S(1)}, u32[]{:S(2)}, u32[]{:S(2)}) collective-permute-start(f32[16,4096]{1,0:T(8,128)S(1)} %slice.161), channel_id=1, source_target_pairs={{96,0},{104,8},{112,16},{120,24},{0,32},{8,40},{16,48},{24,56},{32... | collective-permute-start | bytes 786440 | tf_op jit(solution)/shard_map/ppermute | solution.py:39
  79.6 30.9 %collective-permute-start.27 = (f32[4,64,768]{2,1,0:T(8,128)S(1)}, f32[4,64,768]{2,1,0:T(8,128)S(1)}, u32[]{:S(2)}, u32[]{:S(2)}) collective-permute-start(f32[4,64,768]{2,1,0:T(8,128)S(1)} %pad_maximum_fusion.7), channel_id=1, source_target_pairs={{4,0},{5,1},{6,2},{7,3},{0,4},{1,5},{2,6},{3,7},{12,8},{13,9},{14,... | collective-permute-start | bytes 2359304 | tf_op jit(solution)/shard_map/ppermute | solution.py:44
  89.7 10.0 %collective-permute-start.22 = (f32[2,40,768]{2,1,0:T(8,128)S(1)}, f32[2,40,768]{2,1,0:T(8,128)S(1)}, u32[]{:S(2)}, u32[]{:S(2)}) collective-permute-start(f32[2,40,768]{2,1,0:T(8,128)S(1)} %get-tuple-element.69), channel_id=1, source_target_pairs={{3,0},{0,1},{1,2},{2,3},{7,4},{4,5},{5,6},{6,7},{11,8},{8,9},{9,10... | collective-permute-start | bytes 737288 | tf_op jit(solution)/shard_map/ppermute | solution.py:44
  91.7 8.0 %collective-permute-start.23 = (f32[2,40,768]{2,1,0:T(8,128)S(1)}, f32[2,40,768]{2,1,0:T(8,128)S(1)}, u32[]{:S(2)}, u32[]{:S(2)}) collective-permute-start(f32[2,40,768]{2,1,0:T(8,128)S(1)} %get-tuple-element.70), channel_id=1, source_target_pairs={{1,0},{2,1},{3,2},{0,3},{5,4},{6,5},{7,6},{4,7},{9,8},{10,9},{11,1... | collective-permute-start | bytes 737288 | tf_op jit(solution)/shard_map/ppermute | solution.py:44
  94.9 11.3 %collective-permute-start.24 = (f32[2,40,768]{2,1,0:T(8,128)S(1)}, f32[2,40,768]{2,1,0:T(8,128)S(1)}, u32[]{:S(2)}, u32[]{:S(2)}) collective-permute-start(f32[2,40,768]{2,1,0:T(8,128)S(1)} %get-tuple-element.71), channel_id=1, source_target_pairs={{2,0},{3,1},{0,2},{1,3},{6,4},{7,5},{4,6},{5,7},{10,8},{11,9},{8,1... | collective-permute-start | bytes 737288 | tf_op jit(solution)/shard_map/ppermute | solution.py:44
  97.7 12.8 %collective-permute-start.26 = (f32[4,24,768]{2,1,0:T(8,128)S(1)}, f32[4,24,768]{2,1,0:T(8,128)S(1)}, u32[]{:S(2)}, u32[]{:S(2)}) collective-permute-start(f32[4,24,768]{2,1,0:T(8,128)S(1)} %get-tuple-element.73), channel_id=1, source_target_pairs={{4,0},{5,1},{6,2},{7,3},{0,4},{1,5},{2,6},{3,7},{12,8},{13,9},{14,... | collective-permute-start | bytes 884744 | tf_op jit(solution)/shard_map/ppermute | solution.py:44
  124.3 25.2 %collective-permute-start.32 = (f32[2,64,768]{2,1,0:T(8,128)S(1)}, f32[2,64,768]{2,1,0:T(8,128)S(1)}, u32[]{:S(2)}, u32[]{:S(2)}) collective-permute-start(f32[2,64,768]{2,1,0:T(8,128)S(1)} %pad_maximum_fusion.8.refs_4_), channel_id=1, source_target_pairs={{1,0},{2,1},{3,2},{0,3},{5,4},{6,5},{7,6},{4,7},{9,8},{10,9},{11,1... | collective-permute-start | bytes 1179656 | tf_op jit(solution)/shard_map/ppermute | solution.py:44
  124.8 24.6 %collective-permute-start.33 = (f32[2,64,768]{2,1,0:T(8,128)S(1)}, f32[2,64,768]{2,1,0:T(8,128)}, u32[]{:S(2)}, u32[]{:S(2)}) collective-permute-start(f32[2,64,768]{2,1,0:T(8,128)S(1)} %pad_maximum_fusion.8.refs_4_), channel_id=1, source_target_pairs={{2,0},{3,1},{0,2},{1,3},{6,4},{7,5},{4,6},{5,7},{10,8},{11,9},{8,1... | collective-permute-start | bytes 1179656 | tf_op jit(solution)/shard_map/ppermute | solution.py:44
  125.8 23.6 %collective-permute-start.34 = (f32[2,64,768]{2,1,0:T(8,128)S(1)}, f32[2,64,768]{2,1,0:T(8,128)}, u32[]{:S(2)}, u32[]{:S(2)}) collective-permute-start(f32[2,64,768]{2,1,0:T(8,128)S(1)} %pad_maximum_fusion.8.refs_4_), channel_id=1, source_target_pairs={{3,0},{0,1},{1,2},{2,3},{7,4},{4,5},{5,6},{6,7},{11,8},{8,9},{9,10... | collective-permute-start | bytes 1179656 | tf_op jit(solution)/shard_map/ppermute | solution.py:44
  126.6 21.8 %all-to-all-start = ((f32[128,1,128]{2,1,0:T(1,128)}), f32[128,1,128]{2,1,0:T(1,128)}, u32[]{:S(2)}, u32[]{:S(2)}) async-start(f32[128,1,128]{2,1,0:T(1,128)} %broadcast_in_dim.72), calls=%async_computation | async-start | bytes 131072 | tf_op jit(solution)/shard_map/all_to_all | solution.py:50
  156.2 8.1 %collective-permute-start.35 = (f32[64,4096]{1,0:T(8,128)S(1)}, f32[64,4096]{1,0:T(8,128)S(1)}, u32[]{:S(2)}, u32[]{:S(2)}) collective-permute-start(f32[64,4096]{1,0:T(8,128)S(1)} %get-tuple-element.80), channel_id=1, source_target_pairs={{8,0},{0,8},{24,16},{16,24},{40,32},{32,40},{56,48},{48,56},{72,64... | collective-permute-start | bytes 3145736 | tf_op jit(solution)/shard_map/ppermute | solution.py:39
  164.9 14.7 %collective-permute-start.38 = (f32[32,4096]{1,0:T(8,128)S(1)}, f32[32,4096]{1,0:T(8,128)S(1)}, u32[]{:S(2)}, u32[]{:S(2)}) collective-permute-start(f32[32,4096]{1,0:T(8,128)S(1)} %slice.213), channel_id=1, source_target_pairs={{16,0},{24,8},{0,16},{8,24},{48,32},{56,40},{32,48},{40,56},{80,64... | collective-permute-start | bytes 1572872 | tf_op jit(solution)/shard_map/ppermute | solution.py:39
  170.0 11.5 %collective-permute-start.37 = (f32[256,4096]{1,0:T(8,128)S(1)}, f32[256,4096]{1,0:T(8,128)S(1)}, u32[]{:S(2)}, u32[]{:S(2)}) collective-permute-start(f32[256,4096]{1,0:T(8,128)S(1)} %get-tuple-element.84), channel_id=1, source_target_pairs={{8,0},{0,8},{24,16},{16,24},{40,32},{32,40},{56,48},{48,56},{72,64... | collective-permute-start | bytes 12582920 | tf_op jit(solution)/shard_map/ppermute | solution.py:39
  170.4 7.8 %collective-permute-start.39 = (f32[16,4096]{1,0:T(8,128)S(1)}, f32[16,4096]{1,0:T(8,128)S(1)}, u32[]{:S(2)}, u32[]{:S(2)}) collective-permute-start(f32[16,4096]{1,0:T(8,128)S(1)} %get-tuple-element.111), channel_id=1, source_target_pairs={{32,0},{40,8},{48,16},{56,24},{64,32},{72,40},{80,48},{88,56},{96,... | collective-permute-start | bytes 786440 | tf_op jit(solution)/shard_map/ppermute | solution.py:39
  170.5 9.0 %collective-permute-start.40 = (f32[16,4096]{1,0:T(8,128)S(1)}, f32[16,4096]{1,0:T(8,128)S(1)}, u32[]{:S(2)}, u32[]{:S(2)}) collective-permute-start(f32[16,4096]{1,0:T(8,128)S(1)} %get-tuple-element.110), channel_id=1, source_target_pairs={{96,0},{104,8},{112,16},{120,24},{0,32},{8,40},{16,48},{24,56},{32... | collective-permute-start | bytes 786440 | tf_op jit(solution)/shard_map/ppermute | solution.py:39
  179.8 23.8 %collective-permute-start.41 = (f32[64,4096]{1,0:T(8,128)S(1)}, f32[64,4096]{1,0:T(8,128)S(1)}, u32[]{:S(2)}, u32[]{:S(2)}) collective-permute-start(f32[64,4096]{1,0:T(8,128)S(1)} %pad_maximum_fusion.3), channel_id=1, source_target_pairs={{32,0},{40,8},{48,16},{56,24},{64,32},{72,40},{80,48},{88,56},{96,... | collective-permute-start | bytes 3145736 | tf_op jit(solution)/shard_map/ppermute | solution.py:39
  180.1 24.9 %collective-permute-start.42 = (f32[64,4096]{1,0:T(8,128)S(1)}, f32[64,4096]{1,0:T(8,128)S(1)}, u32[]{:S(2)}, u32[]{:S(2)}) collective-permute-start(f32[64,4096]{1,0:T(8,128)S(1)} %pad_maximum_fusion.4), channel_id=1, source_target_pairs={{96,0},{104,8},{112,16},{120,24},{0,32},{8,40},{16,48},{24,56},{32... | collective-permute-start | bytes 3145736 | tf_op jit(solution)/shard_map/ppermute | solution.py:39
  181.5 23.6 %collective-permute-start.44 = (f32[64,4096]{1,0:T(8,128)S(1)}, f32[64,4096]{1,0:T(8,128)S(1)}, u32[]{:S(2)}, u32[]{:S(2)}) collective-permute-start(f32[64,4096]{1,0:T(8,128)S(1)} %slice.212), channel_id=1, source_target_pairs={{16,0},{24,8},{0,16},{8,24},{48,32},{56,40},{32,48},{40,56},{80,64... | collective-permute-start | bytes 3145736 | tf_op jit(solution)/shard_map/ppermute | solution.py:39
  205.6 22.7 %collective-permute-start.43 = (f32[64,4096]{1,0:T(8,128)S(1)}, f32[64,4096]{1,0:T(8,128)S(1)}, u32[]{:S(2)}, u32[]{:S(2)}) collective-permute-start(f32[64,4096]{1,0:T(8,128)S(1)} %pad_maximum_fusion.5), channel_id=1, source_target_pairs={{16,0},{24,8},{0,16},{8,24},{48,32},{56,40},{32,48},{40,56},{80,64... | collective-permute-start | bytes 3145736 | tf_op jit(solution)/shard_map/ppermute | solution.py:39
  205.8 22.5 %collective-permute-start.45 = (f32[64,4096]{1,0:T(8,128)S(1)}, f32[64,4096]{1,0:T(8,128)S(1)}, u32[]{:S(2)}, u32[]{:S(2)}) collective-permute-start(f32[64,4096]{1,0:T(8,128)S(1)} %slice_add_fusion), channel_id=1, source_target_pairs={{32,0},{40,8},{48,16},{56,24},{64,32},{72,40},{80,48},{88,56},{96,... | collective-permute-start | bytes 3145736 | tf_op jit(solution)/shard_map/ppermute | solution.py:39
  207.1 23.1 %collective-permute-start.46 = (f32[64,4096]{1,0:T(8,128)S(1)}, f32[64,4096]{1,0:T(8,128)S(1)}, u32[]{:S(2)}, u32[]{:S(2)}) collective-permute-start(f32[64,4096]{1,0:T(8,128)S(1)} %pad_maximum_fusion.6), channel_id=1, source_target_pairs={{96,0},{104,8},{112,16},{120,24},{0,32},{8,40},{16,48},{24,56},{32... | collective-permute-start | bytes 3145736 | tf_op jit(solution)/shard_map/ppermute | solution.py:39
  231.2 18.7 %all-to-all-start.1 = ((f32[128,1,128]{2,1,0:T(1,128)}), f32[128,1,128]{2,1,0:T(1,128)S(1)}, u32[]{:S(2)}, u32[]{:S(2)}) async-start(f32[128,1,128]{2,1,0:T(1,128)} %broadcast_in_dim.73), calls=%async_computation.1 | async-start | bytes 131072 | tf_op jit(solution)/shard_map/all_to_all | solution.py:50
  (26 other events, 285.5 us)

commit v5 on v4

--- a/solution.py
+++ b/solution.py
@@ -312,8 +312,12 @@
     return row_shift(value, -step, 0, 0)
 
 
+def third_rows(kc):
+    return 3 * kc // 8
+
+
 def shard_pieces(kc):
-    h, q = kc // 2, kc // 4
+    h, t = kc // 2, third_rows(kc)
     return (
         ((0, kc, (0, 0), 0),),
         ((0, kc, (0, 1), 0),),
@@ -322,9 +326,9 @@
         ((0, h, (3, 1), h), (h, h, (1, 1), h)),
         ((0, h, (2, 0), 0), (h, h, (3, 1), 0)),
         ((0, h, (2, 0), h), (h, h, (1, 1), 0)),
-        ((0, h, (2, 1), h),),
-        ((0, q, (2, 1), 0),),
-        ((0, q, (2, 1), q),),
+        ((0, kc - 2 * t, (2, 1), 2 * t),),
+        ((0, t, (2, 1), 0),),
+        ((0, t, (2, 1), t),),
     )
 
 
@@ -358,9 +362,9 @@
 
 
 def third_step(z2, up2, down2):
-    h = z2.shape[0] // 2
-    q = h // 2
-    return swap_z(down2[:h]), send_x(up2[h : h + q], 1), send_x(down2[h + q :], -1)
+    h, t = z2.shape[0] // 2, third_rows(z2.shape[0])
+    down3 = jnp.concatenate([down2[h + t :], z2[h : 2 * t]])
+    return swap_z(down2[2 * t - h : h]), send_x(up2[h : h + t], 1), send_x(down3, -1)
 
 
 def with_core(pieces):
@@ -390,12 +394,18 @@
 
 
 def second_back(z2, up2, down2, z3, up3, down3):
-    h = z2.shape[0] // 2
-    q = h // 2
-    z2 = swap_z(z2)
-    up2 = send_x(jnp.concatenate([up2[:h], up2[h : h + q] + up3, up2[h + q :]]), -1)
-    down2 = send_x(jnp.concatenate([down2[:h] + z3, down2[h : h + q], down2[h + q :] + down3]), 1)
-    return z2, up2, down2
+    h, t = z2.shape[0] // 2, third_rows(z2.shape[0])
+    z2 = jnp.concatenate([z2[:h], z2[h : 2 * t] + down3[h - t :], z2[2 * t :]])
+    up2 = jnp.concatenate([up2[:h], up2[h : h + t] + up3, up2[h + t :]])
+    down2 = jnp.concatenate(
+        [
+            down2[: 2 * t - h],
+            down2[2 * t - h : h] + z3,
+            down2[h : h + t],
+            down2[h + t :] + down3[: h - t],
+        ]
+    )
+    return swap_z(z2), send_x(up2, -1), send_x(down2, 1)
 
 
 def first_back(z1, up1, down1, z2, up2, down2):
@@ -443,18 +453,20 @@
 
     own = dirn
     first = first_step(own)
-    first, meta = after(first, meta)
-    own_other, z1_other = swap_core(own), swap_core(first[0])
+    own_other = swap_core(own)
+    ride, own_other = after(res, own_other)
+    ride1, ride3 = col_shift(ride, 0, 1), col_shift(ride, 0, 3)
+    first, meta, ride1, ride3 = after(first, meta, ride1, ride3)
+    z1_other = swap_core(first[0])
     second = second_step(*first)
-    ride, z1_other = after(res, z1_other)
-    ride1, ride3 = col_shift(ride, 0, 1), col_shift(ride, 0, 3)
-    second, ride1, ride3 = after(second, ride1, ride3)
+    ride, z1_other = after(ride, z1_other)
+    ride2 = col_shift(ride, 0, 2)
+    second, ride2 = after(second, ride2)
     third = third_step(*second)
     others = [swap_core(piece) for piece in (*first[1:], *second)]
-    ride, others = after(ride, others)
-    ride2 = col_shift(ride, 0, 2)
     rides = jnp.stack([res, ride1, ride2, ride3])
-    third, rides = after(third, rides)
+    rides, third_x = after(rides, third[1:])
+    third = (third[0], *third_x)
     rides_z = col_shift(rides, 1, 0)
     others += [swap_core(piece) for piece in third]
     pieces = [own, *first, *second, *third, own_other, z1_other, *others]

time: 251 us -> 247 us (0.984)
  waiting for transfers between devices: 139 us -> 126 us
  Pallas kernels: 13.4 us -> 17.7 us
  starting transfers between devices: 79.9 us -> 83 us
    ppermute x31, waiting for transfers between devices: 104 us -> 91.4 us  [row_shift(): return lax.ppermute(value, 'row', pairs)]
    ppermute x31, starting transfers between devices: 31.8 us -> 40 us  [row_shift(): return lax.ppermute(value, 'row', pairs)]
    ppermute x16, starting transfers between devices: 27 us -> 23.3 us  [col_shift(): return lax.ppermute(value, 'col', pairs)]
  transfers between devices with their start and end apart: 49 -> 49, of which waited for: 25 -> 28; matrix products, arithmetic and copies ran while one was open for 6% -> 6% of each run, Pallas kernels for 3% -> 4%
where the time goes in v5:
time: 247 us
  waiting for transfers between devices  126 us (51%)
  starting transfers between devices  83 us (34%)
  Pallas kernels  17.7 us (7%)
  other arithmetic  13.5 us (5%)
  local copies, waits for them, and re-layouts  4.87 us (2%)
    ppermute x31, waiting for transfers between devices, row_shift(): return lax.ppermute(value, 'row', pairs)  91.4 us
    ppermute x31, starting transfers between devices, row_shift(): return lax.ppermute(value, 'row', pairs)  40 us
    ppermute x16, starting transfers between devices, col_shift(): return lax.ppermute(value, 'col', pairs)  23.3 us
    all_to_all x2, starting transfers between devices, sum_over(): return jnp.sum(lax.all_to_all(sent, axes, 0, 0, tiled=True), axis=0)  19.8 us
    all_to_all x2, waiting for transfers between devices, sum_over(): return jnp.sum(lax.all_to_all(sent, axes, 0, 0, tiled=True), axis=0)  17.4 us
    ppermute x16, waiting for transfers between devices, col_shift(): return lax.ppermute(value, 'col', pairs)  17.2 us
    pallas_call x1, Pallas kernels, backward(): pl.pallas_call(functools.partial(backward_kernel, kc, slots, stages, layo...  8.95 us
    pallas_call x1, Pallas kernels, forward(): pl.pallas_call(functools.partial(forward_kernel, kc, slots, stages, place...  8.78 us
  transfers between devices with their start and end apart: 49, of which 28 were waited for; matrix products, arithmetic and copies ran while one was open for 6% of the time, Pallas kernels for 4%

profile of v5, /device:TPU:1, one launch (start us, length us, event | category | flops | bytes accessed | tf_op | source)
XLA Modules:
  0.0 246.9 jit_solution(6926631154580368564)
XLA Ops:
  9.6 2.8 %collective-permute-start.4 = (f32[64,768]{1,0:T(8,128)}, f32[64,768]{1,0:T(8,128)S(1)}, u32[]{:S(2)}, u32[]{:S(2)}) collective-permute-start(f32[64,768]{1,0:T(8,128)} %bitcast.68), channel_id=1, source_target_pairs={{1,0},{2,1},{3,2},{0,3},{5,4},{6,5},{7,6},{4,7},{9,8},{10,9},{11,1... | collective-permute-start | bytes 589832 | tf_op jit(solution)/shard_map/ppermute | solution.py:44
  15.9 11.6 %collective-permute-done.refs_1_ = f32[64,4096]{1,0:T(8,128)S(1)} collective-permute-done((f32[64,4096]{1,0:T(8,128)}, f32[64,4096]{1,0:T(8,128)S(1)}, u32[]{:S(2)}, u32[]{:S(2)}) %collective-permute-start) | collective-permute-done | bytes 1048608 | tf_op jit(solution)/shard_map/ppermute | solution.py:39
  27.5 2.2 collective-permute-done.1.refs_2_
  35.8 2.9 %collective-permute-start.10 = (f32[64,768]{1,0:T(8,128)S(1)}, f32[64,768]{1,0:T(8,128)S(1)}, u32[]{:S(2)}, u32[]{:S(2)}) collective-permute-start(f32[64,768]{1,0:T(8,128)S(1)} %bitcast.70), channel_id=1, source_target_pairs={{2,0},{3,1},{0,2},{1,3},{6,4},{7,5},{4,6},{5,7},{10,8},{11,9},{8,1... | collective-permute-start | bytes 589832 | tf_op jit(solution)/shard_map/ppermute | solution.py:44
  38.7 17.0 %collective-permute-done.6.refs_4_ = f32[64,4096]{1,0:T(8,128)S(1)} collective-permute-done((f32[64,4096]{1,0:T(8,128)S(1)}, f32[64,4096]{1,0:T(8,128)S(1)}, u32[]{:S(2)}, u32[]{:S(2)}) %collective-permute-start.6) | collective-permute-done | bytes 1048608 | tf_op jit(solution)/shard_map/ppermute | solution.py:39
  57.3 2.7 %collective-permute-start.13 = (f32[24,4096]{1,0:T(8,128)S(1)}, f32[24,4096]{1,0:T(8,128)S(1)}, u32[]{:S(2)}, u32[]{:S(2)}) collective-permute-start(f32[24,4096]{1,0:T(8,128)S(1)} %pad_maximum_fusion.9), channel_id=1, source_target_pairs={{32,0},{40,8},{48,16},{56,24},{64,32},{72,40},{80,48},{88,56},{96,... | collective-permute-start | bytes 1179656 | tf_op jit(solution)/shard_map/ppermute | solution.py:39
  60.8 2.8 %collective-permute-start.16 = (f32[64,4096]{1,0:T(8,128)S(1)}, f32[64,4096]{1,0:T(8,128)S(1)}, u32[]{:S(2)}, u32[]{:S(2)}) collective-permute-start(f32[64,4096]{1,0:T(8,128)S(1)} %collective-permute-done.6.refs_4_), channel_id=1, source_target_pairs={{8,0},{0,8},{24,16},{16,24},{40,32},{32,40},{56,48},{48,56},{72,64... | collective-permute-start | bytes 3145736 | tf_op jit(solution)/shard_map/ppermute | solution.py:39
  63.6 2.7 %collective-permute-done.11.refs_7_ = f32[16,4096]{1,0:T(8,128)S(1)} collective-permute-done((f32[16,4096]{1,0:T(8,128)S(1)}, f32[16,4096]{1,0:T(8,128)S(1)}, u32[]{:S(2)}, u32[]{:S(2)}) %collective-permute-start.11) | collective-permute-done | bytes 262176 | tf_op jit(solution)/shard_map/ppermute | solution.py:39
  66.3 2.6 %collective-permute-start.17 = (f32[64,4096]{1,0:T(8,128)S(1)}, f32[64,4096]{1,0:T(8,128)S(1)}, u32[]{:S(2)}, u32[]{:S(2)}) collective-permute-start(f32[64,4096]{1,0:T(8,128)S(1)} %collective-permute-done.7.refs_5_), channel_id=1, source_target_pairs={{8,0},{0,8},{24,16},{16,24},{40,32},{32,40},{56,48},{48,56},{72,64... | collective-permute-start | bytes 3145736 | tf_op jit(solution)/shard_map/ppermute | solution.py:39
  69.9 3.6 %collective-permute-start.19 = (f32[16,4096]{1,0:T(8,128)S(1)}, f32[16,4096]{1,0:T(8,128)S(1)}, u32[]{:S(2)}, u32[]{:S(2)}) collective-permute-start(f32[16,4096]{1,0:T(8,128)S(1)} %collective-permute-done.11.refs_7_), channel_id=1, source_target_pairs={{8,0},{0,8},{24,16},{16,24},{40,32},{32,40},{56,48},{48,56},{72,64... | collective-permute-start | bytes 786440 | tf_op jit(solution)/shard_map/ppermute | solution.py:39
  75.4 3.3 %collective-permute-start.27 = (f32[4,64,768]{2,1,0:T(8,128)S(1)}, f32[4,64,768]{2,1,0:T(8,128)S(1)}, u32[]{:S(2)}, u32[]{:S(2)}) collective-permute-start(f32[4,64,768]{2,1,0:T(8,128)S(1)} %pad_maximum_fusion.8), channel_id=1, source_target_pairs={{4,0},{5,1},{6,2},{7,3},{0,4},{1,5},{2,6},{3,7},{12,8},{13,9},{14,... | collective-permute-start | bytes 2359304 | tf_op jit(solution)/shard_map/ppermute | solution.py:44
  78.7 8.8 %shard_map.112 = (f32[2,40,768]{2,1,0:T(8,128)S(1)}, f32[2,40,768]{2,1,0:T(8,128)S(1)}, f32[2,40,768]{2,1,0:T(8,128)S(1)}, f32[2,40,768]{2,1,0:T(8,128)S(1)}, f3...) custom-call(s32[840]{0:T(1024)S(1)} %concatenate.39.meta_ref, f32[256,128,128]{2,1,0:T(8,128)} %bitcast.66, ...), custom_call_target="tpu_custom_call" | custom-call | flops 1610612736 | bytes 50331648 | tf_op jit(solution)/shard_map/pallas_call | solution.py:241
  89.0 3.1 %collective-permute-start.23 = (f32[2,40,768]{2,1,0:T(8,128)S(1)}, f32[2,40,768]{2,1,0:T(8,128)S(1)}, u32[]{:S(2)}, u32[]{:S(2)}) collective-permute-start(f32[2,40,768]{2,1,0:T(8,128)S(1)} %get-tuple-element.62), channel_id=1, source_target_pairs={{1,0},{2,1},{3,2},{0,3},{5,4},{6,5},{7,6},{4,7},{9,8},{10,9},{11,1... | collective-permute-start | bytes 737288 | tf_op jit(solution)/shard_map/ppermute | solution.py:44
  96.6 5.8 %collective-permute-done.24 = f32[2,40,768]{2,1,0:T(8,128)S(1)} collective-permute-done((f32[2,40,768]{2,1,0:T(8,128)S(1)}, f32[2,40,768]{2,1,0:T(8,128)S(1)}, u32[]{:S(2)}, u32[]{:S(2)}) %collective-permute-start.24) | collective-permute-done | bytes 245792 | tf_op jit(solution)/shard_map/ppermute | solution.py:44
  102.5 3.0 %collective-permute-start.25 = (f32[40,768]{1,0:T(8,128)S(1)}, f32[40,768]{1,0:T(8,128)S(1)}, u32[]{:S(2)}, u32[]{:S(2)}) collective-permute-start(f32[40,768]{1,0:T(8,128)S(1)} %slice_bitcast_fusion), channel_id=1, source_target_pairs={{4,0},{5,1},{6,2},{7,3},{0,4},{1,5},{2,6},{3,7},{12,8},{13,9},{14,... | collective-permute-start | bytes 368648 | tf_op jit(solution)/shard_map/ppermute | solution.py:44
  106.1 2.2 collective-permute-start.29
  108.4 2.0 collective-permute-done.28
  110.5 2.6 %collective-permute-done.30 = f32[24,768]{1,0:T(8,128)S(1)} collective-permute-done((f32[24,768]{1,0:T(8,128)S(1)}, f32[24,768]{1,0:T(8,128)S(1)}, u32[]{:S(2)}, u32[]{:S(2)}) %collective-permute-start.30) | collective-permute-done | bytes 73760 | tf_op jit(solution)/shard_map/ppermute | solution.py:44
  114.2 5.1 %collective-permute-done.31 = f32[64,768]{1,0:T(8,128)S(1)} collective-permute-done((f32[64,768]{1,0:T(8,128)S(1)}, f32[64,768]{1,0:T(8,128)S(1)}, u32[]{:S(2)}, u32[]{:S(2)}) %collective-permute-start.31) | collective-permute-done | bytes 196640 | tf_op jit(solution)/shard_map/ppermute | solution.py:44
  121.7 12.8 %all-to-all-start = ((f32[128,1,128]{2,1,0:T(1,128)}), f32[128,1,128]{2,1,0:T(1,128)}, u32[]{:S(2)}, u32[]{:S(2)}) async-start(f32[128,1,128]{2,1,0:T(1,128)} %broadcast_in_dim.72), calls=%async_computation | async-start | bytes 131072 | tf_op jit(solution)/shard_map/all_to_all | solution.py:50
  135.8 8.4 %all-to-all-done = f32[128,1,128]{2,1,0:T(1,128)} async-done(((f32[128,1,128]{2,1,0:T(1,128)}), f32[128,1,128]{2,1,0:T(1,128)}, u32[]{:S(2)}, u32[]{:S(2)}) %all-to-all-start) | async-done | bytes 65568 | tf_op jit(solution)/shard_map/all_to_all | solution.py:50
  145.2 8.9 %shard_map.113 = (f32[64,4096]{1,0:T(8,128)S(1)}, f32[192,4096]{1,0:T(8,128)S(1)}, f32[256,4096]{1,0:T(8,128)S(1)}, f32[64,4096]{1,0:T(8,128)S(1)}, f32[192,4096]{1,0:T(8,128)S(1)}, /*index=5*/f32[256,4096]{1,0:T(8,128)S(1)}) custom-call(s32[840]{0:T(1024)S(1)} %concatenate.39.meta_ref, f32[256,128,128]{2,1,0:T(8,128)} %bitcast.67, ...), custom_call_target="tpu_custom_call" | custom-call | flops 1610612736 | bytes 50331648 | tf_op jit(solution)/shard_map/pallas_call | solution.py:263
  154.2 2.4 collective-permute-start.35
  156.6 2.3 collective-permute-done.35
  159.4 2.4 collective-permute-start.39
  165.0 4.4 %collective-permute-done.38 = f32[16,4096]{1,0:T(8,128)S(1)} collective-permute-done((f32[16,4096]{1,0:T(8,128)S(1)}, f32[16,4096]{1,0:T(8,128)S(1)}, u32[]{:S(2)}, u32[]{:S(2)}) %collective-permute-start.38) | collective-permute-done | bytes 262176 | tf_op jit(solution)/shard_map/ppermute | solution.py:39
  170.4 2.7 %collective-permute-done.40 = f32[24,4096]{1,0:T(8,128)S(1)} collective-permute-done((f32[24,4096]{1,0:T(8,128)S(1)}, f32[24,4096]{1,0:T(8,128)S(1)}, u32[]{:S(2)}, u32[]{:S(2)}) %collective-permute-start.40) | collective-permute-done | bytes 393248 | tf_op jit(solution)/shard_map/ppermute | solution.py:39
  178.6 2.9 %collective-permute-done.37 = f32[256,4096]{1,0:T(8,128)S(1)} collective-permute-done((f32[256,4096]{1,0:T(8,128)S(1)}, f32[256,4096]{1,0:T(8,128)S(1)}, u32[]{:S(2)}, u32[]{:S(2)}) %collective-permute-start.37) | collective-permute-done | bytes 4194336 | tf_op jit(solution)/shard_map/ppermute | solution.py:39
  182.2 17.8 %collective-permute-done.44 = f32[64,4096]{1,0:T(8,128)S(1)} collective-permute-done((f32[64,4096]{1,0:T(8,128)S(1)}, f32[64,4096]{1,0:T(8,128)S(1)}, u32[]{:S(2)}, u32[]{:S(2)}) %collective-permute-start.44) | collective-permute-done | bytes 1048608 | tf_op jit(solution)/shard_map/ppermute | solution.py:39
  206.3 20.0 %collective-permute-done.43 = f32[64,4096]{1,0:T(8,128)S(1)} collective-permute-done((f32[64,4096]{1,0:T(8,128)S(1)}, f32[64,4096]{1,0:T(8,128)S(1)}, u32[]{:S(2)}, u32[]{:S(2)}) %collective-permute-start.43) | collective-permute-done | bytes 1048608 | tf_op jit(solution)/shard_map/ppermute | solution.py:39
  228.9 7.0 %all-to-all-start.1 = ((f32[128,1,128]{2,1,0:T(1,128)}), f32[128,1,128]{2,1,0:T(1,128)S(1)}, u32[]{:S(2)}, u32[]{:S(2)}) async-start(f32[128,1,128]{2,1,0:T(1,128)} %broadcast_in_dim.73), calls=%async_computation.1 | async-start | bytes 131072 | tf_op jit(solution)/shard_map/all_to_all | solution.py:50
  236.7 8.9 %all-to-all-done.1 = f32[128,1,128]{2,1,0:T(1,128)S(1)} async-done(((f32[128,1,128]{2,1,0:T(1,128)}), f32[128,1,128]{2,1,0:T(1,128)S(1)}, u32[]{:S(2)}, u32[]{:S(2)}) %all-to-all-start.1) | async-done | bytes 65568 | tf_op jit(solution)/shard_map/all_to_all | solution.py:50
  (153 shorter events, 57.3 us)
Async XLA Ops:
  2.1 25.3 %collective-permute-start = (f32[64,4096]{1,0:T(8,128)}, f32[64,4096]{1,0:T(8,128)S(1)}, u32[]{:S(2)}, u32[]{:S(2)}) collective-permute-start(f32[64,4096]{1,0:T(8,128)} %bitcast.62), channel_id=1, source_target_pairs={{16,0},{24,8},{0,16},{8,24},{48,32},{56,40},{32,48},{40,56},{80,64... | collective-permute-start | bytes 3145736 | tf_op jit(solution)/shard_map/ppermute | solution.py:39
  3.9 25.8 %collective-permute-start.1 = (f32[64,4096]{1,0:T(8,128)}, f32[64,4096]{1,0:T(8,128)S(1)}, u32[]{:S(2)}, u32[]{:S(2)}) collective-permute-start(f32[64,4096]{1,0:T(8,128)} %bitcast.63), channel_id=1, source_target_pairs={{96,0},{104,8},{112,16},{120,24},{0,32},{8,40},{16,48},{24,56},{32... | collective-permute-start | bytes 3145736 | tf_op jit(solution)/shard_map/ppermute | solution.py:39
  5.1 24.6 %collective-permute-start.2 = (f32[64,4096]{1,0:T(8,128)}, f32[64,4096]{1,0:T(8,128)S(1)}, u32[]{:S(2)}, u32[]{:S(2)}) collective-permute-start(f32[64,4096]{1,0:T(8,128)} %bitcast.64), channel_id=1, source_target_pairs={{32,0},{40,8},{48,16},{56,24},{64,32},{72,40},{80,48},{88,56},{96,... | collective-permute-start | bytes 3145736 | tf_op jit(solution)/shard_map/ppermute | solution.py:39
  9.6 20.1 %collective-permute-start.4 = (f32[64,768]{1,0:T(8,128)}, f32[64,768]{1,0:T(8,128)S(1)}, u32[]{:S(2)}, u32[]{:S(2)}) collective-permute-start(f32[64,768]{1,0:T(8,128)} %bitcast.68), channel_id=1, source_target_pairs={{1,0},{2,1},{3,2},{0,3},{5,4},{6,5},{7,6},{4,7},{9,8},{10,9},{11,1... | collective-permute-start | bytes 589832 | tf_op jit(solution)/shard_map/ppermute | solution.py:44
  12.4 17.3 %collective-permute-start.5 = (f32[64,768]{1,0:T(8,128)}, f32[64,768]{1,0:T(8,128)S(1)}, u32[]{:S(2)}, u32[]{:S(2)}) collective-permute-start(f32[64,768]{1,0:T(8,128)} %bitcast.69), channel_id=1, source_target_pairs={{3,0},{0,1},{1,2},{2,3},{7,4},{4,5},{5,6},{6,7},{11,8},{8,9},{9,10... | collective-permute-start | bytes 589832 | tf_op jit(solution)/shard_map/ppermute | solution.py:44
  31.5 24.1 %collective-permute-start.6 = (f32[64,4096]{1,0:T(8,128)S(1)}, f32[64,4096]{1,0:T(8,128)S(1)}, u32[]{:S(2)}, u32[]{:S(2)}) collective-permute-start(f32[64,4096]{1,0:T(8,128)S(1)} %get-tuple-element.117), channel_id=1, source_target_pairs={{16,0},{24,8},{0,16},{8,24},{48,32},{56,40},{32,48},{40,56},{80,64... | collective-permute-start | bytes 3145736 | tf_op jit(solution)/shard_map/ppermute | solution.py:39
  31.6 25.6 %collective-permute-start.7 = (f32[64,4096]{1,0:T(8,128)S(1)}, f32[64,4096]{1,0:T(8,128)S(1)}, u32[]{:S(2)}, u32[]{:S(2)}) collective-permute-start(f32[64,4096]{1,0:T(8,128)S(1)} %get-tuple-element.118), channel_id=1, source_target_pairs={{96,0},{104,8},{112,16},{120,24},{0,32},{8,40},{16,48},{24,56},{32... | collective-permute-start | bytes 3145736 | tf_op jit(solution)/shard_map/ppermute | solution.py:39
  32.9 24.3 %collective-permute-start.8 = (f32[64,4096]{1,0:T(8,128)S(1)}, f32[64,4096]{1,0:T(8,128)S(1)}, u32[]{:S(2)}, u32[]{:S(2)}) collective-permute-start(f32[64,4096]{1,0:T(8,128)S(1)} %get-tuple-element.116), channel_id=1, source_target_pairs={{32,0},{40,8},{48,16},{56,24},{64,32},{72,40},{80,48},{88,56},{96,... | collective-permute-start | bytes 3145736 | tf_op jit(solution)/shard_map/ppermute | solution.py:39
  34.4 26.3 %collective-permute-start.14 = (f32[64,4096]{1,0:T(8,128)S(1)}, f32[64,4096]{1,0:T(8,128)S(1)}, u32[]{:S(2)}, u32[]{:S(2)}) collective-permute-start(f32[64,4096]{1,0:T(8,128)S(1)} %collective-permute-done.1.refs_2_), channel_id=1, source_target_pairs={{8,0},{0,8},{24,16},{16,24},{40,32},{32,40},{56,48},{48,56},{72,64... | collective-permute-start | bytes 3145736 | tf_op jit(solution)/shard_map/ppermute | solution.py:39
  35.8 21.4 %collective-permute-start.10 = (f32[64,768]{1,0:T(8,128)S(1)}, f32[64,768]{1,0:T(8,128)S(1)}, u32[]{:S(2)}, u32[]{:S(2)}) collective-permute-start(f32[64,768]{1,0:T(8,128)S(1)} %bitcast.70), channel_id=1, source_target_pairs={{2,0},{3,1},{0,2},{1,3},{6,4},{7,5},{4,6},{5,7},{10,8},{11,9},{8,1... | collective-permute-start | bytes 589832 | tf_op jit(solution)/shard_map/ppermute | solution.py:44
  55.7 17.9 %collective-permute-start.15 = (f32[64,4096]{1,0:T(8,128)S(1)}, f32[64,4096]{1,0:T(8,128)S(1)}, u32[]{:S(2)}, u32[]{:S(2)}) collective-permute-start(f32[64,4096]{1,0:T(8,128)S(1)} %copy-done.2), channel_id=1, source_target_pairs={{8,0},{0,8},{24,16},{16,24},{40,32},{32,40},{56,48},{48,56},{72,64... | collective-permute-start | bytes 3145736 | tf_op jit(solution)/shard_map/ppermute | solution.py:39
  57.3 11.6 %collective-permute-start.13 = (f32[24,4096]{1,0:T(8,128)S(1)}, f32[24,4096]{1,0:T(8,128)S(1)}, u32[]{:S(2)}, u32[]{:S(2)}) collective-permute-start(f32[24,4096]{1,0:T(8,128)S(1)} %pad_maximum_fusion.9), channel_id=1, source_target_pairs={{32,0},{40,8},{48,16},{56,24},{64,32},{72,40},{80,48},{88,56},{96,... | collective-permute-start | bytes 1179656 | tf_op jit(solution)/shard_map/ppermute | solution.py:39
  60.7 9.2 %collective-permute-start.12 = (f32[24,4096]{1,0:T(8,128)S(1)}, f32[24,4096]{1,0:T(8,128)S(1)}, u32[]{:S(2)}, u32[]{:S(2)}) collective-permute-start(f32[24,4096]{1,0:T(8,128)S(1)} %slice.183), channel_id=1, source_target_pairs={{96,0},{104,8},{112,16},{120,24},{0,32},{8,40},{16,48},{24,56},{32... | collective-permute-start | bytes 1179656 | tf_op jit(solution)/shard_map/ppermute | solution.py:39
  60.8 17.9 %collective-permute-start.16 = (f32[64,4096]{1,0:T(8,128)S(1)}, f32[64,4096]{1,0:T(8,128)S(1)}, u32[]{:S(2)}, u32[]{:S(2)}) collective-permute-start(f32[64,4096]{1,0:T(8,128)S(1)} %collective-permute-done.6.refs_4_), channel_id=1, source_target_pairs={{8,0},{0,8},{24,16},{16,24},{40,32},{32,40},{56,48},{48,56},{72,64... | collective-permute-start | bytes 3145736 | tf_op jit(solution)/shard_map/ppermute | solution.py:39
  66.3 12.4 %collective-permute-start.17 = (f32[64,4096]{1,0:T(8,128)S(1)}, f32[64,4096]{1,0:T(8,128)S(1)}, u32[]{:S(2)}, u32[]{:S(2)}) collective-permute-start(f32[64,4096]{1,0:T(8,128)S(1)} %collective-permute-done.7.refs_5_), channel_id=1, source_target_pairs={{8,0},{0,8},{24,16},{16,24},{40,32},{32,40},{56,48},{48,56},{72,64... | collective-permute-start | bytes 3145736 | tf_op jit(solution)/shard_map/ppermute | solution.py:39
  68.8 9.8 %collective-permute-start.18 = (f32[64,4096]{1,0:T(8,128)S(1)}, f32[64,4096]{1,0:T(8,128)S(1)}, u32[]{:S(2)}, u32[]{:S(2)}) collective-permute-start(f32[64,4096]{1,0:T(8,128)S(1)} %collective-permute-done.8.refs_6_), channel_id=1, source_target_pairs={{8,0},{0,8},{24,16},{16,24},{40,32},{32,40},{56,48},{48,56},{72,64... | collective-permute-start | bytes 3145736 | tf_op jit(solution)/shard_map/ppermute | solution.py:39
  75.4 30.2 %collective-permute-start.27 = (f32[4,64,768]{2,1,0:T(8,128)S(1)}, f32[4,64,768]{2,1,0:T(8,128)S(1)}, u32[]{:S(2)}, u32[]{:S(2)}) collective-permute-start(f32[4,64,768]{2,1,0:T(8,128)S(1)} %pad_maximum_fusion.8), channel_id=1, source_target_pairs={{4,0},{5,1},{6,2},{7,3},{0,4},{1,5},{2,6},{3,7},{12,8},{13,9},{14,... | collective-permute-start | bytes 2359304 | tf_op jit(solution)/shard_map/ppermute | solution.py:44
  92.1 10.3 %collective-permute-start.24 = (f32[2,40,768]{2,1,0:T(8,128)S(1)}, f32[2,40,768]{2,1,0:T(8,128)S(1)}, u32[]{:S(2)}, u32[]{:S(2)}) collective-permute-start(f32[2,40,768]{2,1,0:T(8,128)S(1)} %get-tuple-element.63), channel_id=1, source_target_pairs={{2,0},{3,1},{0,2},{1,3},{6,4},{7,5},{4,6},{5,7},{10,8},{11,9},{8,1... | collective-permute-start | bytes 737288 | tf_op jit(solution)/shard_map/ppermute | solution.py:44
  94.0 11.5 %collective-permute-start.26 = (f32[4,24,768]{2,1,0:T(8,128)S(1)}, f32[4,24,768]{2,1,0:T(8,128)S(1)}, u32[]{:S(2)}, u32[]{:S(2)}) collective-permute-start(f32[4,24,768]{2,1,0:T(8,128)S(1)} %get-tuple-element.65), channel_id=1, source_target_pairs={{4,0},{5,1},{6,2},{7,3},{0,4},{1,5},{2,6},{3,7},{12,8},{13,9},{14,... | collective-permute-start | bytes 884744 | tf_op jit(solution)/shard_map/ppermute | solution.py:44
  119.4 25.9 %collective-permute-start.32 = (f32[2,64,768]{2,1,0:T(8,128)S(1)}, f32[2,64,768]{2,1,0:T(8,128)S(1)}, u32[]{:S(2)}, u32[]{:S(2)}) collective-permute-start(f32[2,64,768]{2,1,0:T(8,128)S(1)} %pad_maximum_fusion.10.refs_4_), channel_id=1, source_target_pairs={{1,0},{2,1},{3,2},{0,3},{5,4},{6,5},{7,6},{4,7},{9,8},{10,9},{11,1... | collective-permute-start | bytes 1179656 | tf_op jit(solution)/shard_map/ppermute | solution.py:44
  119.9 25.3 %collective-permute-start.33 = (f32[2,64,768]{2,1,0:T(8,128)S(1)}, f32[2,64,768]{2,1,0:T(8,128)}, u32[]{:S(2)}, u32[]{:S(2)}) collective-permute-start(f32[2,64,768]{2,1,0:T(8,128)S(1)} %pad_maximum_fusion.10.refs_4_), channel_id=1, source_target_pairs={{2,0},{3,1},{0,2},{1,3},{6,4},{7,5},{4,6},{5,7},{10,8},{11,9},{8,1... | collective-permute-start | bytes 1179656 | tf_op jit(solution)/shard_map/ppermute | solution.py:44
  120.6 24.7 %collective-permute-start.34 = (f32[2,64,768]{2,1,0:T(8,128)S(1)}, f32[2,64,768]{2,1,0:T(8,128)}, u32[]{:S(2)}, u32[]{:S(2)}) collective-permute-start(f32[2,64,768]{2,1,0:T(8,128)S(1)} %pad_maximum_fusion.10.refs_4_), channel_id=1, source_target_pairs={{3,0},{0,1},{1,2},{2,3},{7,4},{4,5},{5,6},{6,7},{11,8},{8,9},{9,10... | collective-permute-start | bytes 1179656 | tf_op jit(solution)/shard_map/ppermute | solution.py:44
  121.7 22.5 %all-to-all-start = ((f32[128,1,128]{2,1,0:T(1,128)}), f32[128,1,128]{2,1,0:T(1,128)}, u32[]{:S(2)}, u32[]{:S(2)}) async-start(f32[128,1,128]{2,1,0:T(1,128)} %broadcast_in_dim.72), calls=%async_computation | async-start | bytes 131072 | tf_op jit(solution)/shard_map/all_to_all | solution.py:50
  159.4 10.9 %collective-permute-start.39 = (f32[24,4096]{1,0:T(8,128)S(1)}, f32[24,4096]{1,0:T(8,128)S(1)}, u32[]{:S(2)}, u32[]{:S(2)}) collective-permute-start(f32[24,4096]{1,0:T(8,128)S(1)} %get-tuple-element.105), channel_id=1, source_target_pairs={{32,0},{40,8},{48,16},{56,24},{64,32},{72,40},{80,48},{88,56},{96,... | collective-permute-start | bytes 1179656 | tf_op jit(solution)/shard_map/ppermute | solution.py:39
  161.8 11.2 %collective-permute-start.40 = (f32[24,4096]{1,0:T(8,128)S(1)}, f32[24,4096]{1,0:T(8,128)S(1)}, u32[]{:S(2)}, u32[]{:S(2)}) collective-permute-start(f32[24,4096]{1,0:T(8,128)S(1)} %get-tuple-element.104), channel_id=1, source_target_pairs={{96,0},{104,8},{112,16},{120,24},{0,32},{8,40},{16,48},{24,56},{32... | collective-permute-start | bytes 1179656 | tf_op jit(solution)/shard_map/ppermute | solution.py:39
  174.9 25.1 %collective-permute-start.44 = (f32[64,4096]{1,0:T(8,128)S(1)}, f32[64,4096]{1,0:T(8,128)S(1)}, u32[]{:S(2)}, u32[]{:S(2)}) collective-permute-start(f32[64,4096]{1,0:T(8,128)S(1)} %pad_maximum_fusion.6), channel_id=1, source_target_pairs={{16,0},{24,8},{0,16},{8,24},{48,32},{56,40},{32,48},{40,56},{80,64... | collective-permute-start | bytes 3145736 | tf_op jit(solution)/shard_map/ppermute | solution.py:39
  176.7 24.5 %collective-permute-start.41 = (f32[64,4096]{1,0:T(8,128)S(1)}, f32[64,4096]{1,0:T(8,128)S(1)}, u32[]{:S(2)}, u32[]{:S(2)}) collective-permute-start(f32[64,4096]{1,0:T(8,128)S(1)} %pad_maximum_fusion.3), channel_id=1, source_target_pairs={{32,0},{40,8},{48,16},{56,24},{64,32},{72,40},{80,48},{88,56},{96,... | collective-permute-start | bytes 3145736 | tf_op jit(solution)/shard_map/ppermute | solution.py:39
  176.9 25.6 %collective-permute-start.42 = (f32[64,4096]{1,0:T(8,128)S(1)}, f32[64,4096]{1,0:T(8,128)S(1)}, u32[]{:S(2)}, u32[]{:S(2)}) collective-permute-start(f32[64,4096]{1,0:T(8,128)S(1)} %pad_maximum_fusion.4), channel_id=1, source_target_pairs={{96,0},{104,8},{112,16},{120,24},{0,32},{8,40},{16,48},{24,56},{32... | collective-permute-start | bytes 3145736 | tf_op jit(solution)/shard_map/ppermute | solution.py:39
  203.0 23.3 %collective-permute-start.43 = (f32[64,4096]{1,0:T(8,128)S(1)}, f32[64,4096]{1,0:T(8,128)S(1)}, u32[]{:S(2)}, u32[]{:S(2)}) collective-permute-start(f32[64,4096]{1,0:T(8,128)S(1)} %pad_maximum_fusion.5), channel_id=1, source_target_pairs={{16,0},{24,8},{0,16},{8,24},{48,32},{56,40},{32,48},{40,56},{80,64... | collective-permute-start | bytes 3145736 | tf_op jit(solution)/shard_map/ppermute | solution.py:39
  203.4 23.2 %collective-permute-start.45 = (f32[64,4096]{1,0:T(8,128)S(1)}, f32[64,4096]{1,0:T(8,128)S(1)}, u32[]{:S(2)}, u32[]{:S(2)}) collective-permute-start(f32[64,4096]{1,0:T(8,128)S(1)} %slice_add_fusion), channel_id=1, source_target_pairs={{32,0},{40,8},{48,16},{56,24},{64,32},{72,40},{80,48},{88,56},{96,... | collective-permute-start | bytes 3145736 | tf_op jit(solution)/shard_map/ppermute | solution.py:39
  203.6 24.4 %collective-permute-start.46 = (f32[64,4096]{1,0:T(8,128)S(1)}, f32[64,4096]{1,0:T(8,128)S(1)}, u32[]{:S(2)}, u32[]{:S(2)}) collective-permute-start(f32[64,4096]{1,0:T(8,128)S(1)} %pad_maximum_fusion.7), channel_id=1, source_target_pairs={{96,0},{104,8},{112,16},{120,24},{0,32},{8,40},{16,48},{24,56},{32... | collective-permute-start | bytes 3145736 | tf_op jit(solution)/shard_map/ppermute | solution.py:39
  228.9 16.7 %all-to-all-start.1 = ((f32[128,1,128]{2,1,0:T(1,128)}), f32[128,1,128]{2,1,0:T(1,128)S(1)}, u32[]{:S(2)}, u32[]{:S(2)}) async-start(f32[128,1,128]{2,1,0:T(1,128)} %broadcast_in_dim.73), calls=%async_computation.1 | async-start | bytes 131072 | tf_op jit(solution)/shard_map/all_to_all | solution.py:50
  (26 other events, 298.3 us)

commit v6 on v5

--- a/solution.py
+++ b/solution.py
@@ -101,6 +101,69 @@
     dx, dz, dc = place
     x, z, c = meta_ref[1], meta_ref[2], meta_ref[3]
     return ((x + dx) % NX) * 4 + ((z + dz) % NZ) * 2 + (c + dc) % NCORE
+
+
+def turn_kernel(blocks_ref, out_ref, taken, turned, in_sems, out_sems):
+    depth = taken.shape[0]
+    total = blocks_ref.shape[0] // GROUP
+
+    def take(chunk):
+        span = pl.ds(chunk * GROUP, GROUP)
+        buffer = chunk % depth
+        return pltpu.make_async_copy(blocks_ref.at[span], taken.at[buffer], in_sems.at[buffer])
+
+    def give(chunk):
+        span = pl.ds(chunk * GROUP, GROUP)
+        buffer = chunk % depth
+        return pltpu.make_async_copy(turned.at[buffer], out_ref.at[span], out_sems.at[buffer])
+
+    for chunk in range(depth):
+        take(chunk).start()
+
+    def work(chunk, _):
+        buffer = chunk % depth
+        take(chunk).wait()
+
+        @pl.when(chunk >= depth)
+        def _():
+            give(chunk - depth).wait()
+
+        for inner in range(GROUP):
+            high, low = split(taken[buffer, inner].T)
+            turned[buffer, inner, :BS] = high
+            turned[buffer, inner, BS:] = low
+        give(chunk).start()
+
+        @pl.when(chunk + depth < total)
+        def _():
+            take(chunk + depth).start()
+
+        return 0
+
+    lax.fori_loop(0, total, work, 0)
+    for chunk in range(total - depth, total):
+        give(chunk).wait()
+
+
+def turn_blocks(blocks):
+    depth = 4
+    shape = (blocks.shape[0], 2 * BS, BS)
+    return pl.pallas_call(
+        turn_kernel,
+        in_specs=[pl.BlockSpec(memory_space=pltpu.HBM)],
+        out_specs=pl.BlockSpec(memory_space=pltpu.HBM),
+        scratch_shapes=[
+            pltpu.VMEM((depth, GROUP, BS, BS), jnp.float32),
+            pltpu.VMEM((depth, GROUP, 2 * BS, BS), jnp.bfloat16),
+            pltpu.SemaphoreType.DMA((depth,)),
+            pltpu.SemaphoreType.DMA((depth,)),
+        ],
+        out_shape=jax.ShapeDtypeStruct(shape, jnp.bfloat16),
+        compiler_params=pltpu.CompilerParams(vmem_limit_bytes=16 * 1024 * 1024),
+        cost_estimate=pl.CostEstimate(
+            flops=0, bytes_accessed=8 * blocks.size, transcendentals=0
+        ),
+    )(blocks)
 
 
 def forward_kernel(kc, slots, stages, places, meta_ref, blocks_ref, *refs):
@@ -130,14 +193,13 @@
             slot = group * GROUP + inner
             place = meta_ref[HEAD + 2 * (slots + GROUP) + slot]
             offset = pl.multiple_of((place % 32) * BS, BS)
-            left = doubled(panel[place // 32, :, pl.ds(offset, BS)])
-            high, low = split(held[buffer, inner])
-            right = jnp.concatenate([high, low], axis=1)
-            both = lax.dot_general(
-                right, left, (((1,), (1,)), ((), ())), preferred_element_type=jnp.float32
+            both = jnp.dot(
+                doubled(panel[place // 32, :, pl.ds(offset, BS)]),
+                held[buffer, inner],
+                preferred_element_type=jnp.float32,
             )
             live = jnp.where(slot < last, 1.0, 0.0)
-            acc[meta_ref[HEAD + slots + GROUP + slot]] += both * live
+            acc[meta_ref[HEAD + slots + GROUP + slot]] += (both[:kc] + both[kc:]) * live
 
     done, waited = 0, 0
     for stage in stages:
@@ -155,8 +217,7 @@
         for dz in range(NZH):
             piece = ((zh + dz) % NZH) * 4 + (y + dy) % NY
             for t in range(per):
-                both = acc[piece * per + t].T
-                both = both[:kc] + both[kc:]
+                both = acc[piece * per + t]
                 outs[dy][dz, :, t * BS : (t + 1) * BS] = both[:YROWS]
                 outs[NY + dz][dy, :, t * BS : (t + 1) * BS] = both[YROWS:]
 
@@ -240,12 +301,12 @@
     out_shape += [jax.ShapeDtypeStruct((NY, kc - YROWS, 6 * BS), jnp.float32)] * NZH
     return pl.pallas_call(
         functools.partial(forward_kernel, kc, slots, stages, places),
-        in_specs=[smem] + [any_spec] * (1 + len(pieces)),
+        in_specs=[smem, pl.BlockSpec(memory_space=pltpu.HBM)] + [any_spec] * len(pieces),
         out_specs=[vmem] * len(out_shape),
         scratch_shapes=[
-            pltpu.VMEM((48, BS, 2 * kc), jnp.float32),
+            pltpu.VMEM((48, kc, BS), jnp.float32),
             pltpu.VMEM((16, kc, 4096), jnp.float32),
-            pltpu.VMEM((BUFFERS, GROUP, BS, BS), jnp.float32),
+            pltpu.VMEM((BUFFERS, GROUP, 2 * BS, BS), jnp.bfloat16),
             pltpu.SemaphoreType.DMA((sum(len(entries) for _, entries in places),)),
             pltpu.SemaphoreType.DMA((BUFFERS,)),
         ],
@@ -452,6 +513,7 @@
     meta = jnp.concatenate([head, lists])
 
     own = dirn
+    turned = turn_blocks(tile_blocks)
     first = first_step(own)
     own_other = swap_core(own)
     ride, own_other = after(res, own_other)
@@ -461,7 +523,7 @@
     second = second_step(*first)
     ride, z1_other = after(ride, z1_other)
     ride2 = col_shift(ride, 0, 2)
-    second, ride2 = after(second, ride2)
+    second, ride2, turned = after(second, ride2, turned)
     third = third_step(*second)
     others = [swap_core(piece) for piece in (*first[1:], *second)]
     rides = jnp.stack([res, ride1, ride2, ride3])
@@ -470,7 +532,7 @@
     rides_z = col_shift(rides, 1, 0)
     others += [swap_core(piece) for piece in third]
     pieces = [own, *first, *second, *third, own_other, z1_other, *others]
-    parts = forward(tile_blocks, meta, both_cores(kc), pieces, kc, (7, 14, 16))
+    parts = forward(turned, meta, both_cores(kc), pieces, kc, (7, 14, 16))
 
     far = col_shift(parts[NY + 1], 1, 0)
     far, rides_z = after(far, rides_z)

time: 247 us -> 247 us (level)
  local copies, waits for them, and re-layouts: 4.87 us -> 15.2 us
  waiting for transfers between devices: 126 us -> 117 us
  starting transfers between devices: 83 us -> 74.9 us
  Pallas kernels: 17.7 us -> 25 us
    unnamed x18 -> x26, local copies, waits for them, and re-layouts: 0.05 us -> 11.6 us
    ppermute x31, waiting for transfers between devices: 91.4 us -> 80.8 us  [row_shift(): return lax.ppermute(value, 'row', pairs)]
    pallas_call x0 -> x1, Pallas kernels: none -> 8.3 us  [turn_blocks(): pl.pallas_call(turn_kernel, in_specs=[pl.BlockSpec(memory_space=pltpu.HBM...]
    ppermute x31, starting transfers between devices: 40 us -> 34.4 us  [row_shift(): return lax.ppermute(value, 'row', pairs)]
  transfers between devices with their start and end apart: 49 -> 49, of which waited for: 28 -> 27; matrix products, arithmetic and copies ran while one was open for 6% -> 6% of each run, Pallas kernels for 4% -> 6%
where the time goes in v6:
time: 247 us
  waiting for transfers between devices  117 us (47%)
  starting transfers between devices  74.9 us (30%)
  Pallas kernels  25 us (10%)
  local copies, waits for them, and re-layouts  15.2 us (6%)
  other arithmetic  13.1 us (5%)
    ppermute x31, waiting for transfers between devices, row_shift(): return lax.ppermute(value, 'row', pairs)  80.8 us
    ppermute x31, starting transfers between devices, row_shift(): return lax.ppermute(value, 'row', pairs)  34.4 us
    ppermute x16, starting transfers between devices, col_shift(): return lax.ppermute(value, 'col', pairs)  22.7 us
    all_to_all x2, waiting for transfers between devices, sum_over(): return jnp.sum(lax.all_to_all(sent, axes, 0, 0, tiled=True), axis=0)  18.3 us
    all_to_all x2, starting transfers between devices, sum_over(): return jnp.sum(lax.all_to_all(sent, axes, 0, 0, tiled=True), axis=0)  17.8 us
    ppermute x16, waiting for transfers between devices, col_shift(): return lax.ppermute(value, 'col', pairs)  17.4 us
    unnamed x26, local copies, waits for them, and re-layouts  11.6 us
    pallas_call x1, Pallas kernels, backward(): pl.pallas_call(functools.partial(backward_kernel, kc, slots, stages, layo...  8.95 us
  transfers between devices with their start and end apart: 49, of which 27 were waited for; matrix products, arithmetic and copies ran while one was open for 6% of the time, Pallas kernels for 6%

profile of v6, /device:TPU:1, one launch (start us, length us, event | category | flops | bytes accessed | tf_op | source)
XLA Modules:
  0.0 246.6 jit_solution(393452337786569487)
XLA Ops:
  9.6 2.8 %collective-permute-start.4 = (f32[64,768]{1,0:T(8,128)}, f32[64,768]{1,0:T(8,128)S(1)}, u32[]{:S(2)}, u32[]{:S(2)}) collective-permute-start(f32[64,768]{1,0:T(8,128)} %bitcast.68), channel_id=1, source_target_pairs={{1,0},{2,1},{3,2},{0,3},{5,4},{6,5},{7,6},{4,7},{9,8},{10,9},{11,1... | collective-permute-start | bytes 589832 | tf_op jit(solution)/shard_map/ppermute | solution.py:44
  13.5 14.0 %collective-permute-done.refs_1_ = f32[64,4096]{1,0:T(8,128)S(1)} collective-permute-done((f32[64,4096]{1,0:T(8,128)}, f32[64,4096]{1,0:T(8,128)S(1)}, u32[]{:S(2)}, u32[]{:S(2)}) %collective-permute-start) | collective-permute-done | bytes 1048608 | tf_op jit(solution)/shard_map/ppermute | solution.py:39
  27.5 2.2 collective-permute-done.1.refs_2_
  35.4 2.9 %collective-permute-start.10 = (f32[64,768]{1,0:T(8,128)S(1)}, f32[64,768]{1,0:T(8,128)S(1)}, u32[]{:S(2)}, u32[]{:S(2)}) collective-permute-start(f32[64,768]{1,0:T(8,128)S(1)} %bitcast.70), channel_id=1, source_target_pairs={{2,0},{3,1},{0,2},{1,3},{6,4},{7,5},{4,6},{5,7},{10,8},{11,9},{8,1... | collective-permute-start | bytes 589832 | tf_op jit(solution)/shard_map/ppermute | solution.py:44
  38.3 5.8 %copy-done = f32[1,256,128,128]{3,2,1,0:T(8,128)S(1)} copy-done((f32[1,256,128,128]{3,2,1,0:T(8,128)S(1)}, f32[1,256,128,128]{3,2,1,0:T(8,128)}, u32[]{:S(2)}) %copy-start) | copy-done | bytes 16777240
  44.1 8.3 %shard_map.112.blocks_ref = bf16[256,256,128]{2,1,0:T(8,128)(2,1)S(1)} custom-call(f32[256,128,128]{2,1,0:T(8,128)S(1)} %bitcast.62), custom_call_target="tpu_custom_call" | custom-call | bytes 33554432 | tf_op jit(solution)/shard_map/pallas_call | solution.py:151
  52.4 5.7 %copy-done.1 = bf16[256,256,128]{2,1,0:T(8,128)(2,1)} copy-done((bf16[256,256,128]{2,1,0:T(8,128)(2,1)}, bf16[256,256,128]{2,1,0:T(8,128)(2,1)S(1)}, u32[]{:S(2)}) %copy-start.1) | copy-done | bytes 16777240
  63.5 3.4 %collective-permute-done.11.refs_7_ = f32[16,4096]{1,0:T(8,128)S(1)} collective-permute-done((f32[16,4096]{1,0:T(8,128)S(1)}, f32[16,4096]{1,0:T(8,128)S(1)}, u32[]{:S(2)}, u32[]{:S(2)}) %collective-permute-start.11) | collective-permute-done | bytes 262176 | tf_op jit(solution)/shard_map/ppermute | solution.py:39
  66.8 2.2 collective-permute-start.17
  72.3 2.4 collective-permute-start.19
  77.5 3.3 %collective-permute-start.27 = (f32[4,64,768]{2,1,0:T(8,128)S(1)}, f32[4,64,768]{2,1,0:T(8,128)S(1)}, u32[]{:S(2)}, u32[]{:S(2)}) collective-permute-start(f32[4,64,768]{2,1,0:T(8,128)S(1)} %pad_maximum_fusion.8), channel_id=1, source_target_pairs={{4,0},{5,1},{6,2},{7,3},{0,4},{1,5},{2,6},{3,7},{12,8},{13,9},{14,... | collective-permute-start | bytes 2359304 | tf_op jit(solution)/shard_map/ppermute | solution.py:44
  80.8 7.7 %shard_map.113 = (f32[2,40,768]{2,1,0:T(8,128)S(1)}, f32[2,40,768]{2,1,0:T(8,128)S(1)}, f32[2,40,768]{2,1,0:T(8,128)S(1)}, f32[2,40,768]{2,1,0:T(8,128)S(1)}, f3...) custom-call(s32[840]{0:T(1024)S(1)} %concatenate.39.meta_ref, bf16[256,256,128]{2,1,0:T(8,128)(2,1)} %copy-done.1, ...), custom_call_target="tpu_custom_call" | custom-call | flops 1610612736 | bytes 50331648 | tf_op jit(solution)/shard_map/pallas_call | solution.py:302
  88.6 4.5 %collective-permute-start.23 = (f32[2,40,768]{2,1,0:T(8,128)S(1)}, f32[2,40,768]{2,1,0:T(8,128)S(1)}, u32[]{:S(2)}, u32[]{:S(2)}) collective-permute-start(f32[2,40,768]{2,1,0:T(8,128)S(1)} %get-tuple-element.64), channel_id=1, source_target_pairs={{1,0},{2,1},{3,2},{0,3},{5,4},{6,5},{7,6},{4,7},{9,8},{10,9},{11,1... | collective-permute-start | bytes 737288 | tf_op jit(solution)/shard_map/ppermute | solution.py:44
  94.8 2.6 %collective-permute-done.22 = f32[2,40,768]{2,1,0:T(8,128)S(1)} collective-permute-done((f32[2,40,768]{2,1,0:T(8,128)S(1)}, f32[2,40,768]{2,1,0:T(8,128)S(1)}, u32[]{:S(2)}, u32[]{:S(2)}) %collective-permute-start.22) | collective-permute-done | bytes 245792 | tf_op jit(solution)/shard_map/ppermute | solution.py:44
  98.8 6.9 %collective-permute-done.24 = f32[2,40,768]{2,1,0:T(8,128)S(1)} collective-permute-done((f32[2,40,768]{2,1,0:T(8,128)S(1)}, f32[2,40,768]{2,1,0:T(8,128)S(1)}, u32[]{:S(2)}, u32[]{:S(2)}) %collective-permute-start.24) | collective-permute-done | bytes 245792 | tf_op jit(solution)/shard_map/ppermute | solution.py:44
  106.4 2.3 collective-permute-start.29
  108.9 2.8 %collective-permute-done.25 = f32[40,768]{1,0:T(8,128)S(1)} collective-permute-done((f32[40,768]{1,0:T(8,128)S(1)}, f32[40,768]{1,0:T(8,128)S(1)}, u32[]{:S(2)}, u32[]{:S(2)}) %collective-permute-start.25) | collective-permute-done | bytes 122912 | tf_op jit(solution)/shard_map/ppermute | solution.py:44
  113.5 3.0 %collective-permute-start.31 = (f32[64,768]{1,0:T(8,128)S(1)}, f32[64,768]{1,0:T(8,128)S(1)}, u32[]{:S(2)}, u32[]{:S(2)}) collective-permute-start(f32[64,768]{1,0:T(8,128)S(1)} %get-tuple-element.126), channel_id=1, source_target_pairs={{4,0},{5,1},{6,2},{7,3},{0,4},{1,5},{2,6},{3,7},{12,8},{13,9},{14,... | collective-permute-start | bytes 589832 | tf_op jit(solution)/shard_map/ppermute | solution.py:44
  117.4 2.2 collective-permute-done.31
  122.4 11.8 %all-to-all-start = ((f32[128,1,128]{2,1,0:T(1,128)}), f32[128,1,128]{2,1,0:T(1,128)}, u32[]{:S(2)}, u32[]{:S(2)}) async-start(f32[128,1,128]{2,1,0:T(1,128)} %broadcast_in_dim.72), calls=%async_computation | async-start | bytes 131072 | tf_op jit(solution)/shard_map/all_to_all | solution.py:50
  135.5 9.3 %all-to-all-done = f32[128,1,128]{2,1,0:T(1,128)} async-done(((f32[128,1,128]{2,1,0:T(1,128)}), f32[128,1,128]{2,1,0:T(1,128)}, u32[]{:S(2)}, u32[]{:S(2)}) %all-to-all-start) | async-done | bytes 65568 | tf_op jit(solution)/shard_map/all_to_all | solution.py:50
  145.8 8.9 %shard_map.114 = (f32[64,4096]{1,0:T(8,128)S(1)}, f32[192,4096]{1,0:T(8,128)S(1)}, f32[256,4096]{1,0:T(8,128)S(1)}, f32[64,4096]{1,0:T(8,128)S(1)}, f32[192,4096]{1,0:T(8,128)S(1)}, /*index=5*/f32[256,4096]{1,0:T(8,128)S(1)}) custom-call(s32[840]{0:T(1024)S(1)} %concatenate.39.meta_ref, f32[256,128,128]{2,1,0:T(8,128)} %bitcast.61, ...), custom_call_target="tpu_custom_call" | custom-call | flops 1610612736 | bytes 50331648 | tf_op jit(solution)/shard_map/pallas_call | solution.py:324
  154.8 3.1 %collective-permute-start.35 = (f32[64,4096]{1,0:T(8,128)S(1)}, f32[64,4096]{1,0:T(8,128)S(1)}, u32[]{:S(2)}, u32[]{:S(2)}) collective-permute-start(f32[64,4096]{1,0:T(8,128)S(1)} %get-tuple-element.74), channel_id=1, source_target_pairs={{8,0},{0,8},{24,16},{16,24},{40,32},{32,40},{56,48},{48,56},{72,64... | collective-permute-start | bytes 3145736 | tf_op jit(solution)/shard_map/ppermute | solution.py:39
  157.9 2.3 collective-permute-done.35
  163.1 2.8 %collective-permute-done.36 = f32[192,4096]{1,0:T(8,128)S(1)} collective-permute-done((f32[192,4096]{1,0:T(8,128)S(1)}, f32[192,4096]{1,0:T(8,128)S(1)}, u32[]{:S(2)}, u32[]{:S(2)}) %collective-permute-start.36) | collective-permute-done | bytes 3145760 | tf_op jit(solution)/shard_map/ppermute | solution.py:39
  166.4 3.7 %collective-permute-done.38 = f32[16,4096]{1,0:T(8,128)S(1)} collective-permute-done((f32[16,4096]{1,0:T(8,128)S(1)}, f32[16,4096]{1,0:T(8,128)S(1)}, u32[]{:S(2)}, u32[]{:S(2)}) %collective-permute-start.38) | collective-permute-done | bytes 262176 | tf_op jit(solution)/shard_map/ppermute | solution.py:39
  171.4 2.6 %collective-permute-done.40 = f32[24,4096]{1,0:T(8,128)S(1)} collective-permute-done((f32[24,4096]{1,0:T(8,128)S(1)}, f32[24,4096]{1,0:T(8,128)S(1)}, u32[]{:S(2)}, u32[]{:S(2)}) %collective-permute-start.40) | collective-permute-done | bytes 393248 | tf_op jit(solution)/shard_map/ppermute | solution.py:39
  178.1 4.5 %collective-permute-done.37 = f32[256,4096]{1,0:T(8,128)S(1)} collective-permute-done((f32[256,4096]{1,0:T(8,128)S(1)}, f32[256,4096]{1,0:T(8,128)S(1)}, u32[]{:S(2)}, u32[]{:S(2)}) %collective-permute-start.37) | collective-permute-done | bytes 4194336 | tf_op jit(solution)/shard_map/ppermute | solution.py:39
  183.1 17.7 %collective-permute-done.44 = f32[64,4096]{1,0:T(8,128)S(1)} collective-permute-done((f32[64,4096]{1,0:T(8,128)S(1)}, f32[64,4096]{1,0:T(8,128)S(1)}, u32[]{:S(2)}, u32[]{:S(2)}) %collective-permute-start.44) | collective-permute-done | bytes 1048608 | tf_op jit(solution)/shard_map/ppermute | solution.py:39
  207.0 19.4 %collective-permute-done.43 = f32[64,4096]{1,0:T(8,128)S(1)} collective-permute-done((f32[64,4096]{1,0:T(8,128)S(1)}, f32[64,4096]{1,0:T(8,128)S(1)}, u32[]{:S(2)}, u32[]{:S(2)}) %collective-permute-start.43) | collective-permute-done | bytes 1048608 | tf_op jit(solution)/shard_map/ppermute | solution.py:39
  229.6 6.0 %all-to-all-start.1 = ((f32[128,1,128]{2,1,0:T(1,128)}), f32[128,1,128]{2,1,0:T(1,128)S(1)}, u32[]{:S(2)}, u32[]{:S(2)}) async-start(f32[128,1,128]{2,1,0:T(1,128)} %broadcast_in_dim.73), calls=%async_computation.1 | async-start | bytes 131072 | tf_op jit(solution)/shard_map/all_to_all | solution.py:50
  236.4 9.1 %all-to-all-done.1 = f32[128,1,128]{2,1,0:T(1,128)S(1)} async-done(((f32[128,1,128]{2,1,0:T(1,128)}), f32[128,1,128]{2,1,0:T(1,128)S(1)}, u32[]{:S(2)}, u32[]{:S(2)}) %all-to-all-start.1) | async-done | bytes 65568 | tf_op jit(solution)/shard_map/all_to_all | solution.py:50
  (162 shorter events, 58.7 us)
Async XLA Ops:
  2.1 25.3 %collective-permute-start = (f32[64,4096]{1,0:T(8,128)}, f32[64,4096]{1,0:T(8,128)S(1)}, u32[]{:S(2)}, u32[]{:S(2)}) collective-permute-start(f32[64,4096]{1,0:T(8,128)} %bitcast.64), channel_id=1, source_target_pairs={{16,0},{24,8},{0,16},{8,24},{48,32},{56,40},{32,48},{40,56},{80,64... | collective-permute-start | bytes 3145736 | tf_op jit(solution)/shard_map/ppermute | solution.py:39
  3.9 25.8 %collective-permute-start.1 = (f32[64,4096]{1,0:T(8,128)}, f32[64,4096]{1,0:T(8,128)S(1)}, u32[]{:S(2)}, u32[]{:S(2)}) collective-permute-start(f32[64,4096]{1,0:T(8,128)} %bitcast.65), channel_id=1, source_target_pairs={{96,0},{104,8},{112,16},{120,24},{0,32},{8,40},{16,48},{24,56},{32... | collective-permute-start | bytes 3145736 | tf_op jit(solution)/shard_map/ppermute | solution.py:39
  5.1 24.6 %collective-permute-start.2 = (f32[64,4096]{1,0:T(8,128)}, f32[64,4096]{1,0:T(8,128)S(1)}, u32[]{:S(2)}, u32[]{:S(2)}) collective-permute-start(f32[64,4096]{1,0:T(8,128)} %bitcast.66), channel_id=1, source_target_pairs={{32,0},{40,8},{48,16},{56,24},{64,32},{72,40},{80,48},{88,56},{96,... | collective-permute-start | bytes 3145736 | tf_op jit(solution)/shard_map/ppermute | solution.py:39
  9.6 20.1 %collective-permute-start.4 = (f32[64,768]{1,0:T(8,128)}, f32[64,768]{1,0:T(8,128)S(1)}, u32[]{:S(2)}, u32[]{:S(2)}) collective-permute-start(f32[64,768]{1,0:T(8,128)} %bitcast.68), channel_id=1, source_target_pairs={{1,0},{2,1},{3,2},{0,3},{5,4},{6,5},{7,6},{4,7},{9,8},{10,9},{11,1... | collective-permute-start | bytes 589832 | tf_op jit(solution)/shard_map/ppermute | solution.py:44
  12.4 17.3 %collective-permute-start.5 = (f32[64,768]{1,0:T(8,128)}, f32[64,768]{1,0:T(8,128)}, u32[]{:S(2)}, u32[]{:S(2)}) collective-permute-start(f32[64,768]{1,0:T(8,128)} %bitcast.69), channel_id=1, source_target_pairs={{3,0},{0,1},{1,2},{2,3},{7,4},{4,5},{5,6},{6,7},{11,8},{8,9},{9,10... | collective-permute-start | bytes 589832 | tf_op jit(solution)/shard_map/ppermute | solution.py:44
  31.4 26.7 %collective-permute-start.6 = (f32[64,4096]{1,0:T(8,128)S(1)}, f32[64,4096]{1,0:T(8,128)S(1)}, u32[]{:S(2)}, u32[]{:S(2)}) collective-permute-start(f32[64,4096]{1,0:T(8,128)S(1)} %get-tuple-element.119), channel_id=1, source_target_pairs={{16,0},{24,8},{0,16},{8,24},{48,32},{56,40},{32,48},{40,56},{80,64... | collective-permute-start | bytes 3145736 | tf_op jit(solution)/shard_map/ppermute | solution.py:39
  31.5 27.1 %collective-permute-start.7 = (f32[64,4096]{1,0:T(8,128)S(1)}, f32[64,4096]{1,0:T(8,128)S(1)}, u32[]{:S(2)}, u32[]{:S(2)}) collective-permute-start(f32[64,4096]{1,0:T(8,128)S(1)} %get-tuple-element.120), channel_id=1, source_target_pairs={{96,0},{104,8},{112,16},{120,24},{0,32},{8,40},{16,48},{24,56},{32... | collective-permute-start | bytes 3145736 | tf_op jit(solution)/shard_map/ppermute | solution.py:39
  32.8 25.8 %collective-permute-start.8 = (f32[64,4096]{1,0:T(8,128)S(1)}, f32[64,4096]{1,0:T(8,128)S(1)}, u32[]{:S(2)}, u32[]{:S(2)}) collective-permute-start(f32[64,4096]{1,0:T(8,128)S(1)} %get-tuple-element.118), channel_id=1, source_target_pairs={{32,0},{40,8},{48,16},{56,24},{64,32},{72,40},{80,48},{88,56},{96,... | collective-permute-start | bytes 3145736 | tf_op jit(solution)/shard_map/ppermute | solution.py:39
  34.3 27.6 %collective-permute-start.14 = (f32[64,4096]{1,0:T(8,128)S(1)}, f32[64,4096]{1,0:T(8,128)S(1)}, u32[]{:S(2)}, u32[]{:S(2)}) collective-permute-start(f32[64,4096]{1,0:T(8,128)S(1)} %collective-permute-done.1.refs_2_), channel_id=1, source_target_pairs={{8,0},{0,8},{24,16},{16,24},{40,32},{32,40},{56,48},{48,56},{72,64... | collective-permute-start | bytes 3145736 | tf_op jit(solution)/shard_map/ppermute | solution.py:39
  35.4 23.2 %collective-permute-start.10 = (f32[64,768]{1,0:T(8,128)S(1)}, f32[64,768]{1,0:T(8,128)S(1)}, u32[]{:S(2)}, u32[]{:S(2)}) collective-permute-start(f32[64,768]{1,0:T(8,128)S(1)} %bitcast.70), channel_id=1, source_target_pairs={{2,0},{3,1},{0,2},{1,3},{6,4},{7,5},{4,6},{5,7},{10,8},{11,9},{8,1... | collective-permute-start | bytes 589832 | tf_op jit(solution)/shard_map/ppermute | solution.py:44
  58.2 17.5 %collective-permute-start.15 = (f32[64,4096]{1,0:T(8,128)S(1)}, f32[64,4096]{1,0:T(8,128)S(1)}, u32[]{:S(2)}, u32[]{:S(2)}) collective-permute-start(f32[64,4096]{1,0:T(8,128)S(1)} %copy-done.4), channel_id=1, source_target_pairs={{8,0},{0,8},{24,16},{16,24},{40,32},{32,40},{56,48},{48,56},{72,64... | collective-permute-start | bytes 3145736 | tf_op jit(solution)/shard_map/ppermute | solution.py:39
  58.7 10.6 %collective-permute-start.13 = (f32[24,4096]{1,0:T(8,128)S(1)}, f32[24,4096]{1,0:T(8,128)S(1)}, u32[]{:S(2)}, u32[]{:S(2)}) collective-permute-start(f32[24,4096]{1,0:T(8,128)S(1)} %pad_maximum_fusion.9), channel_id=1, source_target_pairs={{32,0},{40,8},{48,16},{56,24},{64,32},{72,40},{80,48},{88,56},{96,... | collective-permute-start | bytes 1179656 | tf_op jit(solution)/shard_map/ppermute | solution.py:39
  61.8 10.4 %collective-permute-start.12 = (f32[24,4096]{1,0:T(8,128)S(1)}, f32[24,4096]{1,0:T(8,128)S(1)}, u32[]{:S(2)}, u32[]{:S(2)}) collective-permute-start(f32[24,4096]{1,0:T(8,128)S(1)} %slice.183), channel_id=1, source_target_pairs={{96,0},{104,8},{112,16},{120,24},{0,32},{8,40},{16,48},{24,56},{32... | collective-permute-start | bytes 1179656 | tf_op jit(solution)/shard_map/ppermute | solution.py:39
  61.9 18.8 %collective-permute-start.16 = (f32[64,4096]{1,0:T(8,128)S(1)}, f32[64,4096]{1,0:T(8,128)S(1)}, u32[]{:S(2)}, u32[]{:S(2)}) collective-permute-start(f32[64,4096]{1,0:T(8,128)S(1)} %collective-permute-done.6.refs_4_), channel_id=1, source_target_pairs={{8,0},{0,8},{24,16},{16,24},{40,32},{32,40},{56,48},{48,56},{72,64... | collective-permute-start | bytes 3145736 | tf_op jit(solution)/shard_map/ppermute | solution.py:39
  66.8 13.9 %collective-permute-start.17 = (f32[64,4096]{1,0:T(8,128)S(1)}, f32[64,4096]{1,0:T(8,128)S(1)}, u32[]{:S(2)}, u32[]{:S(2)}) collective-permute-start(f32[64,4096]{1,0:T(8,128)S(1)} %collective-permute-done.7.refs_5_), channel_id=1, source_target_pairs={{8,0},{0,8},{24,16},{16,24},{40,32},{32,40},{56,48},{48,56},{72,64... | collective-permute-start | bytes 3145736 | tf_op jit(solution)/shard_map/ppermute | solution.py:39
  69.3 11.4 %collective-permute-start.18 = (f32[64,4096]{1,0:T(8,128)S(1)}, f32[64,4096]{1,0:T(8,128)S(1)}, u32[]{:S(2)}, u32[]{:S(2)}) collective-permute-start(f32[64,4096]{1,0:T(8,128)S(1)} %collective-permute-done.8.refs_6_), channel_id=1, source_target_pairs={{8,0},{0,8},{24,16},{16,24},{40,32},{32,40},{56,48},{48,56},{72,64... | collective-permute-start | bytes 3145736 | tf_op jit(solution)/shard_map/ppermute | solution.py:39
  77.5 28.4 %collective-permute-start.27 = (f32[4,64,768]{2,1,0:T(8,128)S(1)}, f32[4,64,768]{2,1,0:T(8,128)S(1)}, u32[]{:S(2)}, u32[]{:S(2)}) collective-permute-start(f32[4,64,768]{2,1,0:T(8,128)S(1)} %pad_maximum_fusion.8), channel_id=1, source_target_pairs={{4,0},{5,1},{6,2},{7,3},{0,4},{1,5},{2,6},{3,7},{12,8},{13,9},{14,... | collective-permute-start | bytes 2359304 | tf_op jit(solution)/shard_map/ppermute | solution.py:44
  93.1 12.6 %collective-permute-start.24 = (f32[2,40,768]{2,1,0:T(8,128)S(1)}, f32[2,40,768]{2,1,0:T(8,128)S(1)}, u32[]{:S(2)}, u32[]{:S(2)}) collective-permute-start(f32[2,40,768]{2,1,0:T(8,128)S(1)} %get-tuple-element.65), channel_id=1, source_target_pairs={{2,0},{3,1},{0,2},{1,3},{6,4},{7,5},{4,6},{5,7},{10,8},{11,9},{8,1... | collective-permute-start | bytes 737288 | tf_op jit(solution)/shard_map/ppermute | solution.py:44
  94.8 11.0 %collective-permute-start.26 = (f32[4,24,768]{2,1,0:T(8,128)S(1)}, f32[4,24,768]{2,1,0:T(8,128)S(1)}, u32[]{:S(2)}, u32[]{:S(2)}) collective-permute-start(f32[4,24,768]{2,1,0:T(8,128)S(1)} %get-tuple-element.67), channel_id=1, source_target_pairs={{4,0},{5,1},{6,2},{7,3},{0,4},{1,5},{2,6},{3,7},{12,8},{13,9},{14,... | collective-permute-start | bytes 884744 | tf_op jit(solution)/shard_map/ppermute | solution.py:44
  119.6 26.2 %collective-permute-start.32 = (f32[2,64,768]{2,1,0:T(8,128)S(1)}, f32[2,64,768]{2,1,0:T(8,128)S(1)}, u32[]{:S(2)}, u32[]{:S(2)}) collective-permute-start(f32[2,64,768]{2,1,0:T(8,128)S(1)} %pad_maximum_fusion.10.refs_4_), channel_id=1, source_target_pairs={{1,0},{2,1},{3,2},{0,3},{5,4},{6,5},{7,6},{4,7},{9,8},{10,9},{11,1... | collective-permute-start | bytes 1179656 | tf_op jit(solution)/shard_map/ppermute | solution.py:44
  121.0 24.8 %collective-permute-start.33 = (f32[2,64,768]{2,1,0:T(8,128)S(1)}, f32[2,64,768]{2,1,0:T(8,128)}, u32[]{:S(2)}, u32[]{:S(2)}) collective-permute-start(f32[2,64,768]{2,1,0:T(8,128)S(1)} %pad_maximum_fusion.10.refs_4_), channel_id=1, source_target_pairs={{2,0},{3,1},{0,2},{1,3},{6,4},{7,5},{4,6},{5,7},{10,8},{11,9},{8,1... | collective-permute-start | bytes 1179656 | tf_op jit(solution)/shard_map/ppermute | solution.py:44
  121.3 24.6 %collective-permute-start.34 = (f32[2,64,768]{2,1,0:T(8,128)S(1)}, f32[2,64,768]{2,1,0:T(8,128)}, u32[]{:S(2)}, u32[]{:S(2)}) collective-permute-start(f32[2,64,768]{2,1,0:T(8,128)S(1)} %pad_maximum_fusion.10.refs_4_), channel_id=1, source_target_pairs={{3,0},{0,1},{1,2},{2,3},{7,4},{4,5},{5,6},{6,7},{11,8},{8,9},{9,10... | collective-permute-start | bytes 1179656 | tf_op jit(solution)/shard_map/ppermute | solution.py:44
  122.4 22.3 %all-to-all-start = ((f32[128,1,128]{2,1,0:T(1,128)}), f32[128,1,128]{2,1,0:T(1,128)}, u32[]{:S(2)}, u32[]{:S(2)}) async-start(f32[128,1,128]{2,1,0:T(1,128)} %broadcast_in_dim.72), calls=%async_computation | async-start | bytes 131072 | tf_op jit(solution)/shard_map/all_to_all | solution.py:50
  160.8 10.6 %collective-permute-start.39 = (f32[24,4096]{1,0:T(8,128)S(1)}, f32[24,4096]{1,0:T(8,128)S(1)}, u32[]{:S(2)}, u32[]{:S(2)}) collective-permute-start(f32[24,4096]{1,0:T(8,128)S(1)} %get-tuple-element.107), channel_id=1, source_target_pairs={{32,0},{40,8},{48,16},{56,24},{64,32},{72,40},{80,48},{88,56},{96,... | collective-permute-start | bytes 1179656 | tf_op jit(solution)/shard_map/ppermute | solution.py:39
  162.8 11.2 %collective-permute-start.40 = (f32[24,4096]{1,0:T(8,128)S(1)}, f32[24,4096]{1,0:T(8,128)S(1)}, u32[]{:S(2)}, u32[]{:S(2)}) collective-permute-start(f32[24,4096]{1,0:T(8,128)S(1)} %get-tuple-element.106), channel_id=1, source_target_pairs={{96,0},{104,8},{112,16},{120,24},{0,32},{8,40},{16,48},{24,56},{32... | collective-permute-start | bytes 1179656 | tf_op jit(solution)/shard_map/ppermute | solution.py:39
  175.9 24.9 %collective-permute-start.44 = (f32[64,4096]{1,0:T(8,128)S(1)}, f32[64,4096]{1,0:T(8,128)S(1)}, u32[]{:S(2)}, u32[]{:S(2)}) collective-permute-start(f32[64,4096]{1,0:T(8,128)S(1)} %pad_maximum_fusion.6), channel_id=1, source_target_pairs={{16,0},{24,8},{0,16},{8,24},{48,32},{56,40},{32,48},{40,56},{80,64... | collective-permute-start | bytes 3145736 | tf_op jit(solution)/shard_map/ppermute | solution.py:39
  176.1 24.8 %collective-permute-start.41 = (f32[64,4096]{1,0:T(8,128)S(1)}, f32[64,4096]{1,0:T(8,128)S(1)}, u32[]{:S(2)}, u32[]{:S(2)}) collective-permute-start(f32[64,4096]{1,0:T(8,128)S(1)} %pad_maximum_fusion.3), channel_id=1, source_target_pairs={{32,0},{40,8},{48,16},{56,24},{64,32},{72,40},{80,48},{88,56},{96,... | collective-permute-start | bytes 3145736 | tf_op jit(solution)/shard_map/ppermute | solution.py:39
  176.3 26.0 %collective-permute-start.42 = (f32[64,4096]{1,0:T(8,128)S(1)}, f32[64,4096]{1,0:T(8,128)S(1)}, u32[]{:S(2)}, u32[]{:S(2)}) collective-permute-start(f32[64,4096]{1,0:T(8,128)S(1)} %pad_maximum_fusion.4), channel_id=1, source_target_pairs={{96,0},{104,8},{112,16},{120,24},{0,32},{8,40},{16,48},{24,56},{32... | collective-permute-start | bytes 3145736 | tf_op jit(solution)/shard_map/ppermute | solution.py:39
  202.8 23.6 %collective-permute-start.43 = (f32[64,4096]{1,0:T(8,128)S(1)}, f32[64,4096]{1,0:T(8,128)S(1)}, u32[]{:S(2)}, u32[]{:S(2)}) collective-permute-start(f32[64,4096]{1,0:T(8,128)S(1)} %pad_maximum_fusion.5), channel_id=1, source_target_pairs={{16,0},{24,8},{0,16},{8,24},{48,32},{56,40},{32,48},{40,56},{80,64... | collective-permute-start | bytes 3145736 | tf_op jit(solution)/shard_map/ppermute | solution.py:39
  204.1 23.0 %collective-permute-start.45 = (f32[64,4096]{1,0:T(8,128)S(1)}, f32[64,4096]{1,0:T(8,128)S(1)}, u32[]{:S(2)}, u32[]{:S(2)}) collective-permute-start(f32[64,4096]{1,0:T(8,128)S(1)} %slice_add_fusion), channel_id=1, source_target_pairs={{32,0},{40,8},{48,16},{56,24},{64,32},{72,40},{80,48},{88,56},{96,... | collective-permute-start | bytes 3145736 | tf_op jit(solution)/shard_map/ppermute | solution.py:39
  204.3 24.2 %collective-permute-start.46 = (f32[64,4096]{1,0:T(8,128)S(1)}, f32[64,4096]{1,0:T(8,128)S(1)}, u32[]{:S(2)}, u32[]{:S(2)}) collective-permute-start(f32[64,4096]{1,0:T(8,128)S(1)} %pad_maximum_fusion.7), channel_id=1, source_target_pairs={{96,0},{104,8},{112,16},{120,24},{0,32},{8,40},{16,48},{24,56},{32... | collective-permute-start | bytes 3145736 | tf_op jit(solution)/shard_map/ppermute | solution.py:39
  229.6 15.9 %all-to-all-start.1 = ((f32[128,1,128]{2,1,0:T(1,128)}), f32[128,1,128]{2,1,0:T(1,128)S(1)}, u32[]{:S(2)}, u32[]{:S(2)}) async-start(f32[128,1,128]{2,1,0:T(1,128)} %broadcast_in_dim.73), calls=%async_computation.1 | async-start | bytes 131072 | tf_op jit(solution)/shard_map/all_to_all | solution.py:50
  (30 other events, 281.8 us)

commit v7 on v6

--- a/solution.py
+++ b/solution.py
@@ -183,9 +183,13 @@
                 sems.at[len(copies)],
             )
             copies.append((position, copy))
-    for _, copy in copies:
-        copy.start()
+    for position, copy in copies:
+        if position < stages[0]:
+            copy.start()
     fetch_first(blocks_ref, held, block_sems, meta_ref, total)
+    for position, copy in copies:
+        if position >= stages[0]:
+            copy.start()
     acc[...] = jnp.zeros_like(acc)
 
     def work(group, buffer):

time: 247 us -> 246 us (level)
  starting transfers between devices: 74.9 us -> 77.6 us
    ppermute x16, starting transfers between devices: 22.7 us -> 26.2 us  [col_shift(): return lax.ppermute(value, 'col', pairs)]
  transfers between devices with their start and end apart: 49 -> 49, of which waited for: 27 -> 26; matrix products, arithmetic and copies ran while one was open for 6% -> 6% of each run, Pallas kernels for 6% -> 6%
where the time goes in v7:
time: 246 us
  waiting for transfers between devices  115 us (47%)
  starting transfers between devices  77.6 us (32%)
  Pallas kernels  23 us (9%)
  local copies, waits for them, and re-layouts  15.2 us (6%)
  other arithmetic  13.1 us (5%)
    ppermute x31, waiting for transfers between devices, row_shift(): return lax.ppermute(value, 'row', pairs)  80.5 us
    ppermute x31, starting transfers between devices, row_shift(): return lax.ppermute(value, 'row', pairs)  35.6 us
    ppermute x16, starting transfers between devices, col_shift(): return lax.ppermute(value, 'col', pairs)  26.2 us
    all_to_all x2, waiting for transfers between devices, sum_over(): return jnp.sum(lax.all_to_all(sent, axes, 0, 0, tiled=True), axis=0)  18.8 us
    ppermute x16, waiting for transfers between devices, col_shift(): return lax.ppermute(value, 'col', pairs)  16 us
    all_to_all x2, starting transfers between devices, sum_over(): return jnp.sum(lax.all_to_all(sent, axes, 0, 0, tiled=True), axis=0)  15.8 us
    unnamed x26, local copies, waits for them, and re-layouts  11.6 us
    pallas_call x1, Pallas kernels, turn_blocks(): pl.pallas_call(turn_kernel, in_specs=[pl.BlockSpec(memory_space=pltpu.HBM...  8.3 us
  transfers between devices with their start and end apart: 49, of which 26 were waited for; matrix products, arithmetic and copies ran while one was open for 6% of the time, Pallas kernels for 6%

profile of v7, /device:TPU:1, one launch (start us, length us, event | category | flops | bytes accessed | tf_op | source)
XLA Modules:
  0.0 246.0 jit_solution(3627187422406488836)
XLA Ops:
  9.6 2.8 %collective-permute-start.4 = (f32[64,768]{1,0:T(8,128)}, f32[64,768]{1,0:T(8,128)S(1)}, u32[]{:S(2)}, u32[]{:S(2)}) collective-permute-start(f32[64,768]{1,0:T(8,128)} %bitcast.68), channel_id=1, source_target_pairs={{1,0},{2,1},{3,2},{0,3},{5,4},{6,5},{7,6},{4,7},{9,8},{10,9},{11,1... | collective-permute-start | bytes 589832 | tf_op jit(solution)/shard_map/ppermute | solution.py:44
  13.5 14.0 %collective-permute-done.refs_1_ = f32[64,4096]{1,0:T(8,128)S(1)} collective-permute-done((f32[64,4096]{1,0:T(8,128)}, f32[64,4096]{1,0:T(8,128)S(1)}, u32[]{:S(2)}, u32[]{:S(2)}) %collective-permute-start) | collective-permute-done | bytes 1048608 | tf_op jit(solution)/shard_map/ppermute | solution.py:39
  27.5 2.2 collective-permute-done.1.refs_2_
  35.4 2.9 %collective-permute-start.10 = (f32[64,768]{1,0:T(8,128)S(1)}, f32[64,768]{1,0:T(8,128)S(1)}, u32[]{:S(2)}, u32[]{:S(2)}) collective-permute-start(f32[64,768]{1,0:T(8,128)S(1)} %bitcast.70), channel_id=1, source_target_pairs={{2,0},{3,1},{0,2},{1,3},{6,4},{7,5},{4,6},{5,7},{10,8},{11,9},{8,1... | collective-permute-start | bytes 589832 | tf_op jit(solution)/shard_map/ppermute | solution.py:44
  38.3 5.8 %copy-done = f32[1,256,128,128]{3,2,1,0:T(8,128)S(1)} copy-done((f32[1,256,128,128]{3,2,1,0:T(8,128)S(1)}, f32[1,256,128,128]{3,2,1,0:T(8,128)}, u32[]{:S(2)}) %copy-start) | copy-done | bytes 16777240
  44.1 8.3 %shard_map.112.blocks_ref = bf16[256,256,128]{2,1,0:T(8,128)(2,1)S(1)} custom-call(f32[256,128,128]{2,1,0:T(8,128)S(1)} %bitcast.62), custom_call_target="tpu_custom_call" | custom-call | bytes 33554432 | tf_op jit(solution)/shard_map/pallas_call | solution.py:151
  52.4 5.7 %copy-done.1 = bf16[256,256,128]{2,1,0:T(8,128)(2,1)} copy-done((bf16[256,256,128]{2,1,0:T(8,128)(2,1)}, bf16[256,256,128]{2,1,0:T(8,128)(2,1)S(1)}, u32[]{:S(2)}) %copy-start.1) | copy-done | bytes 16777240
  63.5 3.4 %collective-permute-done.11.refs_7_ = f32[16,4096]{1,0:T(8,128)S(1)} collective-permute-done((f32[16,4096]{1,0:T(8,128)S(1)}, f32[16,4096]{1,0:T(8,128)S(1)}, u32[]{:S(2)}, u32[]{:S(2)}) %collective-permute-start.11) | collective-permute-done | bytes 262176 | tf_op jit(solution)/shard_map/ppermute | solution.py:39
  66.8 2.2 collective-permute-start.17
  70.3 2.0 collective-permute-done.12.refs_8_
  72.3 2.4 collective-permute-start.19
  77.5 3.3 %collective-permute-start.27 = (f32[4,64,768]{2,1,0:T(8,128)S(1)}, f32[4,64,768]{2,1,0:T(8,128)S(1)}, u32[]{:S(2)}, u32[]{:S(2)}) collective-permute-start(f32[4,64,768]{2,1,0:T(8,128)S(1)} %pad_maximum_fusion.8), channel_id=1, source_target_pairs={{4,0},{5,1},{6,2},{7,3},{0,4},{1,5},{2,6},{3,7},{12,8},{13,9},{14,... | collective-permute-start | bytes 2359304 | tf_op jit(solution)/shard_map/ppermute | solution.py:44
  80.8 6.7 %shard_map.113 = (f32[2,40,768]{2,1,0:T(8,128)S(1)}, f32[2,40,768]{2,1,0:T(8,128)S(1)}, f32[2,40,768]{2,1,0:T(8,128)S(1)}, f32[2,40,768]{2,1,0:T(8,128)S(1)}, f3...) custom-call(s32[840]{0:T(1024)S(1)} %concatenate.39.meta_ref, bf16[256,256,128]{2,1,0:T(8,128)(2,1)} %copy-done.1, ...), custom_call_target="tpu_custom_call" | custom-call | flops 1610612736 | bytes 50331648 | tf_op jit(solution)/shard_map/pallas_call | solution.py:306
  87.5 4.1 %collective-permute-start.22 = (f32[2,40,768]{2,1,0:T(8,128)S(1)}, f32[2,40,768]{2,1,0:T(8,128)S(1)}, u32[]{:S(2)}, u32[]{:S(2)}) collective-permute-start(f32[2,40,768]{2,1,0:T(8,128)S(1)} %get-tuple-element.63), channel_id=1, source_target_pairs={{3,0},{0,1},{1,2},{2,3},{7,4},{4,5},{5,6},{6,7},{11,8},{8,9},{9,10... | collective-permute-start | bytes 737288 | tf_op jit(solution)/shard_map/ppermute | solution.py:44
  98.4 5.1 %collective-permute-done.24 = f32[2,40,768]{2,1,0:T(8,128)S(1)} collective-permute-done((f32[2,40,768]{2,1,0:T(8,128)S(1)}, f32[2,40,768]{2,1,0:T(8,128)S(1)}, u32[]{:S(2)}, u32[]{:S(2)}) %collective-permute-start.24) | collective-permute-done | bytes 245792 | tf_op jit(solution)/shard_map/ppermute | solution.py:44
  103.5 3.2 %collective-permute-start.25 = (f32[40,768]{1,0:T(8,128)S(1)}, f32[40,768]{1,0:T(8,128)S(1)}, u32[]{:S(2)}, u32[]{:S(2)}) collective-permute-start(f32[40,768]{1,0:T(8,128)S(1)} %slice_bitcast_fusion), channel_id=1, source_target_pairs={{4,0},{5,1},{6,2},{7,3},{0,4},{1,5},{2,6},{3,7},{12,8},{13,9},{14,... | collective-permute-start | bytes 368648 | tf_op jit(solution)/shard_map/ppermute | solution.py:44
  107.2 2.4 collective-permute-start.29
  111.3 3.2 %collective-permute-done.30 = f32[24,768]{1,0:T(8,128)S(1)} collective-permute-done((f32[24,768]{1,0:T(8,128)S(1)}, f32[24,768]{1,0:T(8,128)S(1)}, u32[]{:S(2)}, u32[]{:S(2)}) %collective-permute-start.30) | collective-permute-done | bytes 73760 | tf_op jit(solution)/shard_map/ppermute | solution.py:44
  116.5 4.3 %collective-permute-done.31 = f32[64,768]{1,0:T(8,128)S(1)} collective-permute-done((f32[64,768]{1,0:T(8,128)S(1)}, f32[64,768]{1,0:T(8,128)S(1)}, u32[]{:S(2)}, u32[]{:S(2)}) %collective-permute-start.31) | collective-permute-done | bytes 196640 | tf_op jit(solution)/shard_map/ppermute | solution.py:44
  123.4 9.8 %all-to-all-start = ((f32[128,1,128]{2,1,0:T(1,128)}), f32[128,1,128]{2,1,0:T(1,128)}, u32[]{:S(2)}, u32[]{:S(2)}) async-start(f32[128,1,128]{2,1,0:T(1,128)} %broadcast_in_dim.72), calls=%async_computation | async-start | bytes 131072 | tf_op jit(solution)/shard_map/all_to_all | solution.py:50
  134.5 9.7 %all-to-all-done = f32[128,1,128]{2,1,0:T(1,128)} async-done(((f32[128,1,128]{2,1,0:T(1,128)}), f32[128,1,128]{2,1,0:T(1,128)}, u32[]{:S(2)}, u32[]{:S(2)}) %all-to-all-start) | async-done | bytes 65568 | tf_op jit(solution)/shard_map/all_to_all | solution.py:50
  145.3 8.0 %shard_map.114 = (f32[64,4096]{1,0:T(8,128)S(1)}, f32[192,4096]{1,0:T(8,128)S(1)}, f32[256,4096]{1,0:T(8,128)S(1)}, f32[64,4096]{1,0:T(8,128)S(1)}, f32[192,4096]{1,0:T(8,128)S(1)}, /*index=5*/f32[256,4096]{1,0:T(8,128)S(1)}) custom-call(s32[840]{0:T(1024)S(1)} %concatenate.39.meta_ref, f32[256,128,128]{2,1,0:T(8,128)} %bitcast.61, ...), custom_call_target="tpu_custom_call" | custom-call | flops 1610612736 | bytes 50331648 | tf_op jit(solution)/shard_map/pallas_call | solution.py:328
  153.2 5.0 %collective-permute-start.35 = (f32[64,4096]{1,0:T(8,128)S(1)}, f32[64,4096]{1,0:T(8,128)S(1)}, u32[]{:S(2)}, u32[]{:S(2)}) collective-permute-start(f32[64,4096]{1,0:T(8,128)S(1)} %get-tuple-element.74), channel_id=1, source_target_pairs={{8,0},{0,8},{24,16},{16,24},{40,32},{32,40},{56,48},{48,56},{72,64... | collective-permute-start | bytes 3145736 | tf_op jit(solution)/shard_map/ppermute | solution.py:39
  158.2 2.3 collective-permute-done.35
  162.7 3.4 %collective-permute-done.36 = f32[192,4096]{1,0:T(8,128)S(1)} collective-permute-done((f32[192,4096]{1,0:T(8,128)S(1)}, f32[192,4096]{1,0:T(8,128)S(1)}, u32[]{:S(2)}, u32[]{:S(2)}) %collective-permute-start.36) | collective-permute-done | bytes 3145760 | tf_op jit(solution)/shard_map/ppermute | solution.py:39
  166.7 3.2 %collective-permute-done.38 = f32[16,4096]{1,0:T(8,128)S(1)} collective-permute-done((f32[16,4096]{1,0:T(8,128)S(1)}, f32[16,4096]{1,0:T(8,128)S(1)}, u32[]{:S(2)}, u32[]{:S(2)}) %collective-permute-start.38) | collective-permute-done | bytes 262176 | tf_op jit(solution)/shard_map/ppermute | solution.py:39
  171.7 1.9 collective-permute-done.40
  177.4 4.5 %collective-permute-done.37 = f32[256,4096]{1,0:T(8,128)S(1)} collective-permute-done((f32[256,4096]{1,0:T(8,128)S(1)}, f32[256,4096]{1,0:T(8,128)S(1)}, u32[]{:S(2)}, u32[]{:S(2)}) %collective-permute-start.37) | collective-permute-done | bytes 4194336 | tf_op jit(solution)/shard_map/ppermute | solution.py:39
  182.4 17.7 %collective-permute-done.44 = f32[64,4096]{1,0:T(8,128)S(1)} collective-permute-done((f32[64,4096]{1,0:T(8,128)S(1)}, f32[64,4096]{1,0:T(8,128)S(1)}, u32[]{:S(2)}, u32[]{:S(2)}) %collective-permute-start.44) | collective-permute-done | bytes 1048608 | tf_op jit(solution)/shard_map/ppermute | solution.py:39
  206.4 18.9 %collective-permute-done.43 = f32[64,4096]{1,0:T(8,128)S(1)} collective-permute-done((f32[64,4096]{1,0:T(8,128)S(1)}, f32[64,4096]{1,0:T(8,128)S(1)}, u32[]{:S(2)}, u32[]{:S(2)}) %collective-permute-start.43) | collective-permute-done | bytes 1048608 | tf_op jit(solution)/shard_map/ppermute | solution.py:39
  228.9 6.0 %all-to-all-start.1 = ((f32[128,1,128]{2,1,0:T(1,128)}), f32[128,1,128]{2,1,0:T(1,128)S(1)}, u32[]{:S(2)}, u32[]{:S(2)}) async-start(f32[128,1,128]{2,1,0:T(1,128)} %broadcast_in_dim.73), calls=%async_computation.1 | async-start | bytes 131072 | tf_op jit(solution)/shard_map/all_to_all | solution.py:50
  235.7 9.1 %all-to-all-done.1 = f32[128,1,128]{2,1,0:T(1,128)S(1)} async-done(((f32[128,1,128]{2,1,0:T(1,128)}), f32[128,1,128]{2,1,0:T(1,128)S(1)}, u32[]{:S(2)}, u32[]{:S(2)}) %all-to-all-start.1) | async-done | bytes 65568 | tf_op jit(solution)/shard_map/all_to_all | solution.py:50
  (162 shorter events, 60.8 us)
Async XLA Ops:
  2.1 25.3 %collective-permute-start = (f32[64,4096]{1,0:T(8,128)}, f32[64,4096]{1,0:T(8,128)S(1)}, u32[]{:S(2)}, u32[]{:S(2)}) collective-permute-start(f32[64,4096]{1,0:T(8,128)} %bitcast.64), channel_id=1, source_target_pairs={{16,0},{24,8},{0,16},{8,24},{48,32},{56,40},{32,48},{40,56},{80,64... | collective-permute-start | bytes 3145736 | tf_op jit(solution)/shard_map/ppermute | solution.py:39
  3.9 25.8 %collective-permute-start.1 = (f32[64,4096]{1,0:T(8,128)}, f32[64,4096]{1,0:T(8,128)S(1)}, u32[]{:S(2)}, u32[]{:S(2)}) collective-permute-start(f32[64,4096]{1,0:T(8,128)} %bitcast.65), channel_id=1, source_target_pairs={{96,0},{104,8},{112,16},{120,24},{0,32},{8,40},{16,48},{24,56},{32... | collective-permute-start | bytes 3145736 | tf_op jit(solution)/shard_map/ppermute | solution.py:39
  5.1 24.6 %collective-permute-start.2 = (f32[64,4096]{1,0:T(8,128)}, f32[64,4096]{1,0:T(8,128)S(1)}, u32[]{:S(2)}, u32[]{:S(2)}) collective-permute-start(f32[64,4096]{1,0:T(8,128)} %bitcast.66), channel_id=1, source_target_pairs={{32,0},{40,8},{48,16},{56,24},{64,32},{72,40},{80,48},{88,56},{96,... | collective-permute-start | bytes 3145736 | tf_op jit(solution)/shard_map/ppermute | solution.py:39
  9.6 20.1 %collective-permute-start.4 = (f32[64,768]{1,0:T(8,128)}, f32[64,768]{1,0:T(8,128)S(1)}, u32[]{:S(2)}, u32[]{:S(2)}) collective-permute-start(f32[64,768]{1,0:T(8,128)} %bitcast.68), channel_id=1, source_target_pairs={{1,0},{2,1},{3,2},{0,3},{5,4},{6,5},{7,6},{4,7},{9,8},{10,9},{11,1... | collective-permute-start | bytes 589832 | tf_op jit(solution)/shard_map/ppermute | solution.py:44
  12.4 17.3 %collective-permute-start.5 = (f32[64,768]{1,0:T(8,128)}, f32[64,768]{1,0:T(8,128)}, u32[]{:S(2)}, u32[]{:S(2)}) collective-permute-start(f32[64,768]{1,0:T(8,128)} %bitcast.69), channel_id=1, source_target_pairs={{3,0},{0,1},{1,2},{2,3},{7,4},{4,5},{5,6},{6,7},{11,8},{8,9},{9,10... | collective-permute-start | bytes 589832 | tf_op jit(solution)/shard_map/ppermute | solution.py:44
  31.4 26.7 %collective-permute-start.6 = (f32[64,4096]{1,0:T(8,128)S(1)}, f32[64,4096]{1,0:T(8,128)S(1)}, u32[]{:S(2)}, u32[]{:S(2)}) collective-permute-start(f32[64,4096]{1,0:T(8,128)S(1)} %get-tuple-element.119), channel_id=1, source_target_pairs={{16,0},{24,8},{0,16},{8,24},{48,32},{56,40},{32,48},{40,56},{80,64... | collective-permute-start | bytes 3145736 | tf_op jit(solution)/shard_map/ppermute | solution.py:39
  31.5 27.1 %collective-permute-start.7 = (f32[64,4096]{1,0:T(8,128)S(1)}, f32[64,4096]{1,0:T(8,128)S(1)}, u32[]{:S(2)}, u32[]{:S(2)}) collective-permute-start(f32[64,4096]{1,0:T(8,128)S(1)} %get-tuple-element.120), channel_id=1, source_target_pairs={{96,0},{104,8},{112,16},{120,24},{0,32},{8,40},{16,48},{24,56},{32... | collective-permute-start | bytes 3145736 | tf_op jit(solution)/shard_map/ppermute | solution.py:39
  32.8 25.8 %collective-permute-start.8 = (f32[64,4096]{1,0:T(8,128)S(1)}, f32[64,4096]{1,0:T(8,128)S(1)}, u32[]{:S(2)}, u32[]{:S(2)}) collective-permute-start(f32[64,4096]{1,0:T(8,128)S(1)} %get-tuple-element.118), channel_id=1, source_target_pairs={{32,0},{40,8},{48,16},{56,24},{64,32},{72,40},{80,48},{88,56},{96,... | collective-permute-start | bytes 3145736 | tf_op jit(solution)/shard_map/ppermute | solution.py:39
  34.3 27.6 %collective-permute-start.14 = (f32[64,4096]{1,0:T(8,128)S(1)}, f32[64,4096]{1,0:T(8,128)S(1)}, u32[]{:S(2)}, u32[]{:S(2)}) collective-permute-start(f32[64,4096]{1,0:T(8,128)S(1)} %collective-permute-done.1.refs_2_), channel_id=1, source_target_pairs={{8,0},{0,8},{24,16},{16,24},{40,32},{32,40},{56,48},{48,56},{72,64... | collective-permute-start | bytes 3145736 | tf_op jit(solution)/shard_map/ppermute | solution.py:39
  35.4 23.2 %collective-permute-start.10 = (f32[64,768]{1,0:T(8,128)S(1)}, f32[64,768]{1,0:T(8,128)S(1)}, u32[]{:S(2)}, u32[]{:S(2)}) collective-permute-start(f32[64,768]{1,0:T(8,128)S(1)} %bitcast.70), channel_id=1, source_target_pairs={{2,0},{3,1},{0,2},{1,3},{6,4},{7,5},{4,6},{5,7},{10,8},{11,9},{8,1... | collective-permute-start | bytes 589832 | tf_op jit(solution)/shard_map/ppermute | solution.py:44
  58.2 17.5 %collective-permute-start.15 = (f32[64,4096]{1,0:T(8,128)S(1)}, f32[64,4096]{1,0:T(8,128)S(1)}, u32[]{:S(2)}, u32[]{:S(2)}) collective-permute-start(f32[64,4096]{1,0:T(8,128)S(1)} %copy-done.4), channel_id=1, source_target_pairs={{8,0},{0,8},{24,16},{16,24},{40,32},{32,40},{56,48},{48,56},{72,64... | collective-permute-start | bytes 3145736 | tf_op jit(solution)/shard_map/ppermute | solution.py:39
  58.7 10.6 %collective-permute-start.13 = (f32[24,4096]{1,0:T(8,128)S(1)}, f32[24,4096]{1,0:T(8,128)S(1)}, u32[]{:S(2)}, u32[]{:S(2)}) collective-permute-start(f32[24,4096]{1,0:T(8,128)S(1)} %pad_maximum_fusion.9), channel_id=1, source_target_pairs={{32,0},{40,8},{48,16},{56,24},{64,32},{72,40},{80,48},{88,56},{96,... | collective-permute-start | bytes 1179656 | tf_op jit(solution)/shard_map/ppermute | solution.py:39
  61.8 10.4 %collective-permute-start.12 = (f32[24,4096]{1,0:T(8,128)S(1)}, f32[24,4096]{1,0:T(8,128)S(1)}, u32[]{:S(2)}, u32[]{:S(2)}) collective-permute-start(f32[24,4096]{1,0:T(8,128)S(1)} %slice.183), channel_id=1, source_target_pairs={{96,0},{104,8},{112,16},{120,24},{0,32},{8,40},{16,48},{24,56},{32... | collective-permute-start | bytes 1179656 | tf_op jit(solution)/shard_map/ppermute | solution.py:39
  61.9 18.8 %collective-permute-start.16 = (f32[64,4096]{1,0:T(8,128)S(1)}, f32[64,4096]{1,0:T(8,128)S(1)}, u32[]{:S(2)}, u32[]{:S(2)}) collective-permute-start(f32[64,4096]{1,0:T(8,128)S(1)} %collective-permute-done.6.refs_4_), channel_id=1, source_target_pairs={{8,0},{0,8},{24,16},{16,24},{40,32},{32,40},{56,48},{48,56},{72,64... | collective-permute-start | bytes 3145736 | tf_op jit(solution)/shard_map/ppermute | solution.py:39
  66.8 13.9 %collective-permute-start.17 = (f32[64,4096]{1,0:T(8,128)S(1)}, f32[64,4096]{1,0:T(8,128)S(1)}, u32[]{:S(2)}, u32[]{:S(2)}) collective-permute-start(f32[64,4096]{1,0:T(8,128)S(1)} %collective-permute-done.7.refs_5_), channel_id=1, source_target_pairs={{8,0},{0,8},{24,16},{16,24},{40,32},{32,40},{56,48},{48,56},{72,64... | collective-permute-start | bytes 3145736 | tf_op jit(solution)/shard_map/ppermute | solution.py:39
  69.3 11.4 %collective-permute-start.18 = (f32[64,4096]{1,0:T(8,128)S(1)}, f32[64,4096]{1,0:T(8,128)S(1)}, u32[]{:S(2)}, u32[]{:S(2)}) collective-permute-start(f32[64,4096]{1,0:T(8,128)S(1)} %collective-permute-done.8.refs_6_), channel_id=1, source_target_pairs={{8,0},{0,8},{24,16},{16,24},{40,32},{32,40},{56,48},{48,56},{72,64... | collective-permute-start | bytes 3145736 | tf_op jit(solution)/shard_map/ppermute | solution.py:39
  77.5 29.3 %collective-permute-start.27 = (f32[4,64,768]{2,1,0:T(8,128)S(1)}, f32[4,64,768]{2,1,0:T(8,128)S(1)}, u32[]{:S(2)}, u32[]{:S(2)}) collective-permute-start(f32[4,64,768]{2,1,0:T(8,128)S(1)} %pad_maximum_fusion.8), channel_id=1, source_target_pairs={{4,0},{5,1},{6,2},{7,3},{0,4},{1,5},{2,6},{3,7},{12,8},{13,9},{14,... | collective-permute-start | bytes 2359304 | tf_op jit(solution)/shard_map/ppermute | solution.py:44
  91.8 11.6 %collective-permute-start.24 = (f32[2,40,768]{2,1,0:T(8,128)S(1)}, f32[2,40,768]{2,1,0:T(8,128)S(1)}, u32[]{:S(2)}, u32[]{:S(2)}) collective-permute-start(f32[2,40,768]{2,1,0:T(8,128)S(1)} %get-tuple-element.65), channel_id=1, source_target_pairs={{2,0},{3,1},{0,2},{1,3},{6,4},{7,5},{4,6},{5,7},{10,8},{11,9},{8,1... | collective-permute-start | bytes 737288 | tf_op jit(solution)/shard_map/ppermute | solution.py:44
  94.5 12.3 %collective-permute-start.26 = (f32[4,24,768]{2,1,0:T(8,128)S(1)}, f32[4,24,768]{2,1,0:T(8,128)S(1)}, u32[]{:S(2)}, u32[]{:S(2)}) collective-permute-start(f32[4,24,768]{2,1,0:T(8,128)S(1)} %get-tuple-element.67), channel_id=1, source_target_pairs={{4,0},{5,1},{6,2},{7,3},{0,4},{1,5},{2,6},{3,7},{12,8},{13,9},{14,... | collective-permute-start | bytes 884744 | tf_op jit(solution)/shard_map/ppermute | solution.py:44
  120.8 24.4 %collective-permute-start.32 = (f32[2,64,768]{2,1,0:T(8,128)S(1)}, f32[2,64,768]{2,1,0:T(8,128)S(1)}, u32[]{:S(2)}, u32[]{:S(2)}) collective-permute-start(f32[2,64,768]{2,1,0:T(8,128)S(1)} %pad_maximum_fusion.10.refs_4_), channel_id=1, source_target_pairs={{1,0},{2,1},{3,2},{0,3},{5,4},{6,5},{7,6},{4,7},{9,8},{10,9},{11,1... | collective-permute-start | bytes 1179656 | tf_op jit(solution)/shard_map/ppermute | solution.py:44
  122.0 23.2 %collective-permute-start.33 = (f32[2,64,768]{2,1,0:T(8,128)S(1)}, f32[2,64,768]{2,1,0:T(8,128)}, u32[]{:S(2)}, u32[]{:S(2)}) collective-permute-start(f32[2,64,768]{2,1,0:T(8,128)S(1)} %pad_maximum_fusion.10.refs_4_), channel_id=1, source_target_pairs={{2,0},{3,1},{0,2},{1,3},{6,4},{7,5},{4,6},{5,7},{10,8},{11,9},{8,1... | collective-permute-start | bytes 1179656 | tf_op jit(solution)/shard_map/ppermute | solution.py:44
  122.2 23.1 %collective-permute-start.34 = (f32[2,64,768]{2,1,0:T(8,128)S(1)}, f32[2,64,768]{2,1,0:T(8,128)}, u32[]{:S(2)}, u32[]{:S(2)}) collective-permute-start(f32[2,64,768]{2,1,0:T(8,128)S(1)} %pad_maximum_fusion.10.refs_4_), channel_id=1, source_target_pairs={{3,0},{0,1},{1,2},{2,3},{7,4},{4,5},{5,6},{6,7},{11,8},{8,9},{9,10... | collective-permute-start | bytes 1179656 | tf_op jit(solution)/shard_map/ppermute | solution.py:44
  123.4 20.8 %all-to-all-start = ((f32[128,1,128]{2,1,0:T(1,128)}), f32[128,1,128]{2,1,0:T(1,128)}, u32[]{:S(2)}, u32[]{:S(2)}) async-start(f32[128,1,128]{2,1,0:T(1,128)} %broadcast_in_dim.72), calls=%async_computation | async-start | bytes 131072 | tf_op jit(solution)/shard_map/all_to_all | solution.py:50
  161.1 10.6 %collective-permute-start.39 = (f32[24,4096]{1,0:T(8,128)S(1)}, f32[24,4096]{1,0:T(8,128)S(1)}, u32[]{:S(2)}, u32[]{:S(2)}) collective-permute-start(f32[24,4096]{1,0:T(8,128)S(1)} %get-tuple-element.107), channel_id=1, source_target_pairs={{32,0},{40,8},{48,16},{56,24},{64,32},{72,40},{80,48},{88,56},{96,... | collective-permute-start | bytes 1179656 | tf_op jit(solution)/shard_map/ppermute | solution.py:39
  162.1 11.5 %collective-permute-start.40 = (f32[24,4096]{1,0:T(8,128)S(1)}, f32[24,4096]{1,0:T(8,128)S(1)}, u32[]{:S(2)}, u32[]{:S(2)}) collective-permute-start(f32[24,4096]{1,0:T(8,128)S(1)} %get-tuple-element.106), channel_id=1, source_target_pairs={{96,0},{104,8},{112,16},{120,24},{0,32},{8,40},{16,48},{24,56},{32... | collective-permute-start | bytes 1179656 | tf_op jit(solution)/shard_map/ppermute | solution.py:39
  175.2 24.9 %collective-permute-start.44 = (f32[64,4096]{1,0:T(8,128)S(1)}, f32[64,4096]{1,0:T(8,128)S(1)}, u32[]{:S(2)}, u32[]{:S(2)}) collective-permute-start(f32[64,4096]{1,0:T(8,128)S(1)} %pad_maximum_fusion.6), channel_id=1, source_target_pairs={{16,0},{24,8},{0,16},{8,24},{48,32},{56,40},{32,48},{40,56},{80,64... | collective-permute-start | bytes 3145736 | tf_op jit(solution)/shard_map/ppermute | solution.py:39
  175.5 24.6 %collective-permute-start.41 = (f32[64,4096]{1,0:T(8,128)S(1)}, f32[64,4096]{1,0:T(8,128)S(1)}, u32[]{:S(2)}, u32[]{:S(2)}) collective-permute-start(f32[64,4096]{1,0:T(8,128)S(1)} %pad_maximum_fusion.3), channel_id=1, source_target_pairs={{32,0},{40,8},{48,16},{56,24},{64,32},{72,40},{80,48},{88,56},{96,... | collective-permute-start | bytes 3145736 | tf_op jit(solution)/shard_map/ppermute | solution.py:39
  175.7 25.7 %collective-permute-start.42 = (f32[64,4096]{1,0:T(8,128)S(1)}, f32[64,4096]{1,0:T(8,128)S(1)}, u32[]{:S(2)}, u32[]{:S(2)}) collective-permute-start(f32[64,4096]{1,0:T(8,128)S(1)} %pad_maximum_fusion.4), channel_id=1, source_target_pairs={{96,0},{104,8},{112,16},{120,24},{0,32},{8,40},{16,48},{24,56},{32... | collective-permute-start | bytes 3145736 | tf_op jit(solution)/shard_map/ppermute | solution.py:39
  201.9 23.4 %collective-permute-start.43 = (f32[64,4096]{1,0:T(8,128)S(1)}, f32[64,4096]{1,0:T(8,128)S(1)}, u32[]{:S(2)}, u32[]{:S(2)}) collective-permute-start(f32[64,4096]{1,0:T(8,128)S(1)} %pad_maximum_fusion.5), channel_id=1, source_target_pairs={{16,0},{24,8},{0,16},{8,24},{48,32},{56,40},{32,48},{40,56},{80,64... | collective-permute-start | bytes 3145736 | tf_op jit(solution)/shard_map/ppermute | solution.py:39
  203.5 23.0 %collective-permute-start.45 = (f32[64,4096]{1,0:T(8,128)S(1)}, f32[64,4096]{1,0:T(8,128)S(1)}, u32[]{:S(2)}, u32[]{:S(2)}) collective-permute-start(f32[64,4096]{1,0:T(8,128)S(1)} %slice_add_fusion), channel_id=1, source_target_pairs={{32,0},{40,8},{48,16},{56,24},{64,32},{72,40},{80,48},{88,56},{96,... | collective-permute-start | bytes 3145736 | tf_op jit(solution)/shard_map/ppermute | solution.py:39
  203.6 24.2 %collective-permute-start.46 = (f32[64,4096]{1,0:T(8,128)S(1)}, f32[64,4096]{1,0:T(8,128)S(1)}, u32[]{:S(2)}, u32[]{:S(2)}) collective-permute-start(f32[64,4096]{1,0:T(8,128)S(1)} %pad_maximum_fusion.7), channel_id=1, source_target_pairs={{96,0},{104,8},{112,16},{120,24},{0,32},{8,40},{16,48},{24,56},{32... | collective-permute-start | bytes 3145736 | tf_op jit(solution)/shard_map/ppermute | solution.py:39
  228.9 15.9 %all-to-all-start.1 = ((f32[128,1,128]{2,1,0:T(1,128)}), f32[128,1,128]{2,1,0:T(1,128)S(1)}, u32[]{:S(2)}, u32[]{:S(2)}) async-start(f32[128,1,128]{2,1,0:T(1,128)} %broadcast_in_dim.73), calls=%async_computation.1 | async-start | bytes 131072 | tf_op jit(solution)/shard_map/all_to_all | solution.py:50
  (30 other events, 281.2 us)
